TPU v7x, 128 devices: a whole 4x4x4 slice. The times are simulated.
128 devices in a mesh: section: 2 (over x_lo), ctx: 16 (over x_hi, y, core), fsdp: 4 (over z).
Axes of the slice: x: 4 (x_hi: 2, x_lo: 2; x = x_hi * 2 + x_lo), y: 4, z: 4, core: 2. Of those that a mesh axis runs over, the one named last changes fastest.
Arguments:
- ends: bfloat16 [2, 2, 4, 1024, 768], P('section', None, 'fsdp', 'ctx'), may hold values from -6 to 6
- blocks: int32 [2, 32], replicated, may hold values from 0 to 31, as said below
- ln1_gain: bfloat16 [4, 768], P('section', 'fsdp'), may hold values from 0.5 to 1.5
- ln1_bias: bfloat16 [4, 768], P('section', 'fsdp'), may hold values from -3 to 3
- ln2_gain: bfloat16 [4, 768], P('section', 'fsdp'), may hold values from 0.5 to 1.5
- ln2_bias: bfloat16 [4, 768], P('section', 'fsdp'), may hold values from -3 to 3
- qkv_weight: bfloat16 [4, 768, 2304], P('section', 'fsdp'), may hold values from -0.3125 to 0.3125
- qkv_bias: bfloat16 [4, 2304], P('section', 'fsdp'), may hold values from -3 to 3
- out_weight: bfloat16 [4, 768, 768], P('section', 'fsdp'), may hold values from -0.875 to 0.875
- out_bias: bfloat16 [4, 768], P('section', 'fsdp'), may hold values from -3 to 3
- up_weight: bfloat16 [4, 768, 3072], P('section', 'fsdp'), may hold values from -0.21875 to 0.21875
- up_bias: bfloat16 [4, 3072], P('section', 'fsdp'), may hold values from -3 to 3
- down_weight: bfloat16 [4, 3072, 768], P('section', 'fsdp'), may hold values from -0.109375 to 0.109375
- down_bias: bfloat16 [4, 768], P('section', 'fsdp'), may hold values from -3 to 3
Outputs:
- boundary: float32 [2, 2, 4, 1024, 768], P('section', None, 'fsdp', 'ctx')
- grad_ln1_gain: float32 [4, 768], P('section', 'fsdp')
- grad_ln1_bias: float32 [4, 768], P('section', 'fsdp')
- grad_ln2_gain: float32 [4, 768], P('section', 'fsdp')
- grad_ln2_bias: float32 [4, 768], P('section', 'fsdp')
- grad_qkv_weight: float32 [4, 768, 2304], P('section', 'fsdp')
- grad_qkv_bias: float32 [4, 2304], P('section', 'fsdp')
- grad_out_weight: float32 [4, 768, 768], P('section', 'fsdp')
- grad_out_bias: float32 [4, 768], P('section', 'fsdp')
- grad_up_weight: float32 [4, 768, 3072], P('section', 'fsdp')
- grad_up_bias: float32 [4, 3072], P('section', 'fsdp')
- grad_down_weight: float32 [4, 3072, 768], P('section', 'fsdp')
- grad_down_bias: float32 [4, 768], P('section', 'fsdp')
Inputs may be any that keep to these rules, and one draw needn't show every extreme that they name: `blocks`: each row holds every number below 32 once; entries 2 c and 2 c + 1 are j and 31 - j for some j, in either order.
All inputs are finite; a program needn't handle non-finite values.
Results may differ from a plain program's by a relative error of at most 0.024.
Values may be sent and summed in bfloat16 or wider, within the bound.
No kernel may reach another device: no remote copies, remote signals or barrier semaphores. Data moves between devices by JAX's collectives and lax.ppermute only.
A program may use at most 320 MiB of HBM per device.

v0:
```python
import jax
import jax.numpy as jnp
from jax import lax
from jax.sharding import PartitionSpec as P

D = 768
H = 12
HD = 64
ROT = 16


EPSILON = 1e-05
SCORE_SCALE = 0.125


def in_one_piece(arrays, axis, dim, along):
    both = jnp.concatenate(arrays, axis=along)
    whole, at, gathered = (lax.all_gather(both, axis, axis=dim, tiled=True), 0, [])
    for a in arrays:
        gathered.append(lax.slice_in_dim(whole, at, at + a.shape[along], axis=along))
        at += a.shape[along]
    return tuple(gathered)


def in_one_piece_2(arrays, axis, dim, along):
    both = jnp.concatenate(arrays, axis=along)
    whole, at, gathered = (lax.psum_scatter(both, axis, scatter_dimension=dim, tiled=True), 0, [])
    for a in arrays:
        gathered.append(lax.slice_in_dim(whole, at, at + a.shape[along], axis=along))
        at += a.shape[along]
    return tuple(gathered)


def side_by_side(arrays, axis, dim, along):
    columns = [a.reshape(*a.shape[:along], -1) for a in arrays]
    both = jnp.concatenate(columns, axis=along)
    whole, at, gathered = (lax.all_gather(both, axis, axis=dim, tiled=True), 0, [])
    for a, column in zip(arrays, columns):
        share = whole[..., at : at + column.shape[along]]
        gathered.append(share.reshape(*share.shape[:along], *a.shape[along:]))
        at += column.shape[along]
    return tuple(gathered)


def passed_along(block, axis, distance):
    devices = range(lax.axis_size(axis))
    route = [(i - distance, i) for i in devices if i - distance in devices]
    return lax.ppermute(block, axis, route)


def cut_along(x, dim, size):
    dims = x.shape
    blocks = x.reshape(*dims[:dim], size, dims[dim] // size, *dims[dim + 1 :])
    return jnp.moveaxis(blocks, dim, 0)


def summed_on_arrival(x, axis, dim):
    blocks = cut_along(x, dim, lax.axis_size(axis))
    arrived = lax.all_to_all(blocks, axis, split_axis=0, concat_axis=0, tiled=True)
    return arrived.sum(axis=0)


def layer_norm(values, gain_vec, shift_vec):
    center = jnp.mean(values, -1, keepdims=True)
    offset = values - center
    spread = jnp.mean(offset * offset, -1, keepdims=True)
    return offset * lax.rsqrt(spread + EPSILON) * gain_vec + shift_vec


def rotate(head_values, places):
    half_rot = ROT // 2
    frequencies = 10000.0 ** (-jnp.arange(half_rot, dtype=jnp.float32) * 2.0 / ROT)
    angles = places.astype(jnp.float32)[:, None] * frequencies[None, :]
    cosine = jnp.concatenate([jnp.cos(angles), jnp.cos(angles)], -1)[:, None, :]
    sine_table = jnp.concatenate([jnp.sin(angles), jnp.sin(angles)], -1)[:, None, :]
    turned = head_values[..., :ROT]
    swapped = jnp.concatenate([-turned[..., half_rot:], turned[..., :half_rot]], -1)
    return jnp.concatenate([turned * cosine + swapped * sine_table, head_values[..., ROT:]], -1)


def gelu_exact(pre_values):
    return jax.nn.gelu(pre_values, approximate=False)


def matmul(left_side, right_side):
    return jnp.dot(left_side, right_side, preferred_element_type=jnp.float32)


def by_rows(left_side, right_side):
    return lax.dot_general(
        left_side, right_side, (((0,), (0,)), ((), ())), preferred_element_type=jnp.float32
    )


def by_cols(left_side, right_side):
    return lax.dot_general(
        left_side, right_side, (((1,), (1,)), ((), ())), preferred_element_type=jnp.float32
    )


def own_columns(vector, owner_index, owner_count):
    width = vector.shape[0] // owner_count
    return lax.dynamic_slice_in_dim(vector, owner_index * width, width, 0)


def masked_scores(queries, key_heads, query_places, key_places):
    raw_scores = (
        jnp.einsum("qhd,khd->hqk", queries, key_heads, preferred_element_type=jnp.float32)
        * SCORE_SCALE
    )
    return jnp.where(query_places[None, :, None] >= key_places[None, None, :], raw_scores, -1e30)


def forward_layer(hidden, weights, query_places, key_places):
    (
        gain_one,
        shift_one,
        gain_two,
        shift_two,
        w_qkv,
        b_qkv,
        w_out,
        b_out,
        w_up,
        b_up,
        w_down,
        b_down,
    ) = weights
    row_count = hidden.shape[0]
    normed_one = layer_norm(
        hidden, gain_one.astype(jnp.float32), shift_one.astype(jnp.float32)
    ).astype(jnp.bfloat16)
    normed_two = layer_norm(
        hidden, gain_two.astype(jnp.float32), shift_two.astype(jnp.float32)
    ).astype(jnp.bfloat16)
    merged_proj = matmul(normed_one, w_qkv) + b_qkv.astype(jnp.float32)
    queries = rotate(merged_proj[:, :D].reshape(row_count, H, HD), query_places).astype(
        jnp.bfloat16
    )
    key_local = (
        rotate(merged_proj[:, D : 2 * D].reshape(row_count, H, HD), query_places)
        .astype(jnp.bfloat16)
        .reshape(row_count, D)
    )
    value_local = merged_proj[:, 2 * D :].astype(jnp.bfloat16)
    key_all, value_all = in_one_piece((key_local, value_local), "ctx", 0, 1)
    key_heads = key_all.reshape(-1, H, HD)
    value_heads = value_all.reshape(-1, H, HD)
    scores = masked_scores(queries, key_heads, query_places, key_places)
    row_max = jnp.max(scores, -1, keepdims=True)
    raised = jnp.exp(scores - row_max)
    row_total = jnp.sum(raised, -1, keepdims=True)
    softmax_probs = (raised / row_total).astype(jnp.bfloat16)
    log_total = row_max + jnp.log(row_total)
    attended = (
        jnp.einsum("hqk,khd->qhd", softmax_probs, value_heads, preferred_element_type=jnp.float32)
        .reshape(row_count, D)
        .astype(jnp.bfloat16)
    )
    pre_gelu = matmul(normed_two, w_up) + b_up.astype(jnp.float32)
    activated = gelu_exact(pre_gelu).astype(jnp.bfloat16)
    output = hidden + (
        matmul(attended, w_out)
        + b_out.astype(jnp.float32)
        + matmul(activated, w_down)
        + b_down.astype(jnp.float32)
    )
    kept_state = (
        hidden,
        normed_one,
        normed_two,
        queries,
        key_heads,
        value_heads,
        log_total,
        attended,
        pre_gelu,
        activated,
    )
    return (output, kept_state)


def backward_layer(grad_out, weights, kept_state, query_places, key_places):
    (
        gain_one,
        shift_one,
        gain_two,
        shift_two,
        w_qkv,
        b_qkv,
        w_out,
        b_out,
        w_up,
        b_up,
        w_down,
        b_down,
    ) = weights
    (
        hidden,
        normed_one,
        normed_two,
        queries,
        key_heads,
        value_heads,
        log_total,
        attended,
        pre_gelu,
        activated,
    ) = kept_state
    row_count = hidden.shape[0]
    branch_grad = grad_out.astype(jnp.bfloat16)
    hidden_grad = by_cols(branch_grad, w_down)
    gelu_pull = jax.vjp(gelu_exact, pre_gelu)[1]
    up_grad = gelu_pull(hidden_grad)[0].astype(jnp.bfloat16)
    two_grad = by_cols(up_grad, w_up)
    attended_grad = by_cols(branch_grad, w_out).astype(jnp.bfloat16).reshape(row_count, H, HD)
    scores = masked_scores(queries, key_heads, query_places, key_places)
    softmax_probs = jnp.exp(scores - log_total)
    prob_grad = jnp.einsum(
        "qhd,khd->hqk", attended_grad, value_heads, preferred_element_type=jnp.float32
    )
    row_inner = jnp.sum(softmax_probs * prob_grad, -1, keepdims=True)
    score_grad = (softmax_probs * (prob_grad - row_inner)).astype(jnp.bfloat16)
    query_grad = (
        jnp.einsum("hqk,khd->qhd", score_grad, key_heads, preferred_element_type=jnp.float32)
        * SCORE_SCALE
    )
    key_part = (
        jnp.einsum("hqk,qhd->khd", score_grad, queries, preferred_element_type=jnp.float32).reshape(
            -1, D
        )
        * SCORE_SCALE
    )
    value_part = jnp.einsum(
        "hqk,qhd->khd",
        softmax_probs.astype(jnp.bfloat16),
        attended_grad,
        preferred_element_type=jnp.float32,
    ).reshape(-1, D)
    key_grad, value_grad = tuple(
        (
            part.astype(jnp.float32)
            for part in in_one_piece_2(
                (key_part.astype(jnp.bfloat16), value_part.astype(jnp.bfloat16)), "ctx", 0, 1
            )
        )
    )
    rotate_pull = jax.vjp(
        lambda head_values: rotate(head_values, query_places),
        jnp.zeros((row_count, H, HD), jnp.float32),
    )[1]
    query_back = rotate_pull(query_grad)[0].reshape(row_count, D)
    key_back = rotate_pull(key_grad.reshape(row_count, H, HD))[0].reshape(row_count, D)
    qkv_grad = jnp.concatenate([query_back, key_back, value_grad], 1).astype(jnp.bfloat16)
    one_grad = by_cols(qkv_grad, w_qkv)
    pull_one = jax.vjp(
        layer_norm, hidden, gain_one.astype(jnp.float32), shift_one.astype(jnp.float32)
    )[1]
    input_one, gain_one_grad, shift_one_grad = pull_one(one_grad)
    pull_two = jax.vjp(
        layer_norm, hidden, gain_two.astype(jnp.float32), shift_two.astype(jnp.float32)
    )[1]
    input_two, gain_two_grad, shift_two_grad = pull_two(two_grad)
    input_grad = grad_out + input_one + input_two
    norm_grads = (gain_one_grad, shift_one_grad, gain_two_grad, shift_two_grad)
    grad_pieces = (normed_one, qkv_grad, attended, branch_grad, normed_two, up_grad, activated)
    return (input_grad, norm_grads, grad_pieces)


def body(
    ends,
    blocks,
    ln1_gain,
    ln1_bias,
    ln2_gain,
    ln2_bias,
    qkv_weight,
    qkv_bias,
    out_weight,
    out_bias,
    up_weight,
    up_bias,
    down_weight,
    down_bias,
):
    shards = (
        ln1_gain,
        ln1_bias,
        ln2_gain,
        ln2_bias,
        qkv_weight,
        qkv_bias,
        out_weight,
        out_bias,
        up_weight,
        up_bias,
        down_weight,
        down_bias,
    )
    section_index = lax.axis_index("section")
    ctx_index = lax.axis_index("ctx")
    micro_count = ends.shape[1]
    row_count = ends.shape[3]
    half_block = row_count // 2
    layers_here = qkv_weight.shape[0]
    offsets = jnp.arange(row_count * lax.axis_size("ctx"), dtype=jnp.int32)
    key_table = blocks[:, offsets // half_block] * half_block + offsets % half_block
    own_table = lax.dynamic_slice_in_dim(key_table, ctx_index * row_count, row_count, 1)
    is_first = section_index == 0
    is_last = section_index == 1
    local_in = ends[0, :, 0].astype(jnp.float32)
    gathered_all = []
    for layer_index in range(layers_here):
        own_piece = tuple((member[layer_index] for member in shards))
        gathered_all.append(
            (
                lax.all_gather(own_piece[0], "fsdp", axis=0, tiled=True),
                lax.all_gather(own_piece[1], "fsdp", axis=0, tiled=True),
                lax.all_gather(own_piece[2], "fsdp", axis=0, tiled=True),
                *side_by_side((own_piece[3], own_piece[4]), "fsdp", 0, 1),
                lax.all_gather(own_piece[5], "fsdp", axis=0, tiled=True),
                *side_by_side((own_piece[6], own_piece[7], own_piece[8]), "fsdp", 0, 1),
                *side_by_side((own_piece[9], own_piece[10]), "fsdp", 0, 1),
                lax.all_gather(own_piece[11], "fsdp", axis=0, tiled=True),
            )
        )
    received = jnp.zeros((row_count, D), jnp.float32)
    kept_ticks = []
    final_ticks = []
    for tick_index in range(micro_count + 1):
        current = jnp.where(is_first, local_in[min(tick_index, micro_count - 1)], received)
        query_places = jnp.where(
            is_first, own_table[min(tick_index, micro_count - 1)], own_table[max(tick_index - 1, 0)]
        )
        key_places = jnp.where(
            is_first, key_table[min(tick_index, micro_count - 1)], key_table[max(tick_index - 1, 0)]
        )
        kept_layers = []
        for layer_index in range(layers_here):
            weights = gathered_all[layer_index]
            current, kept_state = forward_layer(current, weights, query_places, key_places)
            kept_layers.append(kept_state)
        kept_ticks.append((tuple(kept_layers), query_places, key_places))
        final_ticks.append(current)
        if tick_index < micro_count:
            received = passed_along(current.astype(jnp.bfloat16), "section", 1).astype(jnp.float32)
    incoming = jnp.zeros((row_count, D), jnp.float32)
    input_ticks = []
    shard_totals = [None] * layers_here
    norm_totals = [None] * layers_here
    piece_store = [[] for layer_index in range(layers_here)]
    for tick_index in range(micro_count + 1):
        live_flag = jnp.where(
            is_last, 1.0 if tick_index < micro_count else 0.0, 1.0 if tick_index >= 1 else 0.0
        ).astype(jnp.float32)
        grad_now = (
            jnp.where(is_last, local_in[min(tick_index, micro_count - 1)], incoming) * live_flag
        )
        chosen = jax.tree.map(
            lambda upper_item, lower_item: jnp.where(is_last, upper_item, lower_item),
            kept_ticks[min(tick_index + 1, micro_count)],
            kept_ticks[max(tick_index - 1, 0)],
        )
        kept_layers, query_places, key_places = chosen
        for layer_index in reversed(range(layers_here)):
            weights = gathered_all[layer_index]
            grad_now, norm_grads, grad_pieces = backward_layer(
                grad_now, weights, kept_layers[layer_index], query_places, key_places
            )
            if norm_totals[layer_index] is None:
                norm_totals[layer_index] = norm_grads
            else:
                norm_totals[layer_index] = jax.tree.map(
                    jnp.add, norm_totals[layer_index], norm_grads
                )
            piece_store[layer_index].append(grad_pieces)
        input_ticks.append(grad_now)
        if tick_index < micro_count:
            incoming = passed_along(grad_now.astype(jnp.bfloat16), "section", -1).astype(
                jnp.float32
            )
    fsdp_index = lax.axis_index("fsdp")
    fsdp_count = lax.axis_size("fsdp")
    for layer_index in range(layers_here):
        joined = jax.tree.map(lambda *parts: jnp.concatenate(parts, 0), *piece_store[layer_index])
        normed_one, qkv_grad, attended, branch_grad, normed_two, up_grad, activated = joined
        slice_one, slice_attended, slice_two, slice_activated = (
            lax.all_to_all(normed_one, "fsdp", split_axis=1, concat_axis=0, tiled=True),
            lax.all_to_all(attended, "fsdp", split_axis=1, concat_axis=0, tiled=True),
            lax.all_to_all(normed_two, "fsdp", split_axis=1, concat_axis=0, tiled=True),
            lax.all_to_all(activated, "fsdp", split_axis=1, concat_axis=0, tiled=True),
        )
        every_qkv, every_branch, every_up = in_one_piece(
            (qkv_grad, branch_grad, up_grad), "fsdp", 0, 1
        )
        norm_totals_here = norm_totals[layer_index]
        norm_shard = (
            summed_on_arrival(norm_totals_here[0], "fsdp", 0),
            summed_on_arrival(norm_totals_here[1], "fsdp", 0),
            summed_on_arrival(norm_totals_here[2], "fsdp", 0),
            summed_on_arrival(norm_totals_here[3], "fsdp", 0),
        )
        branch_sum = own_columns(
            jnp.sum(every_branch, 0, dtype=jnp.float32), fsdp_index, fsdp_count
        )
        shard_totals[layer_index] = (
            norm_shard[0],
            norm_shard[1],
            norm_shard[2],
            norm_shard[3],
            by_rows(slice_one, every_qkv),
            own_columns(jnp.sum(every_qkv, 0, dtype=jnp.float32), fsdp_index, fsdp_count),
            by_rows(slice_attended, every_branch),
            branch_sum,
            by_rows(slice_two, every_up),
            own_columns(jnp.sum(every_up, 0, dtype=jnp.float32), fsdp_index, fsdp_count),
            by_rows(slice_activated, every_branch),
            branch_sum,
        )
    summed_layers = []
    for layer_index in range(layers_here):
        layer_shard = shard_totals[layer_index]
        summed_layers.append(
            (
                lax.psum(layer_shard[0].astype(jnp.bfloat16), "ctx").astype(jnp.float32),
                lax.psum(layer_shard[1].astype(jnp.bfloat16), "ctx").astype(jnp.float32),
                lax.psum(layer_shard[2].astype(jnp.bfloat16), "ctx").astype(jnp.float32),
                lax.psum(layer_shard[3].astype(jnp.bfloat16), "ctx").astype(jnp.float32),
                lax.psum(layer_shard[4].astype(jnp.bfloat16), "ctx").astype(jnp.float32),
                lax.psum(layer_shard[5].astype(jnp.bfloat16), "ctx").astype(jnp.float32),
                lax.psum(layer_shard[6].astype(jnp.bfloat16), "ctx").astype(jnp.float32),
                lax.psum(layer_shard[7].astype(jnp.bfloat16), "ctx").astype(jnp.float32),
                lax.psum(layer_shard[8].astype(jnp.bfloat16), "ctx").astype(jnp.float32),
                lax.psum(layer_shard[9].astype(jnp.bfloat16), "ctx").astype(jnp.float32),
                lax.psum(layer_shard[10].astype(jnp.bfloat16), "ctx").astype(jnp.float32),
                lax.psum(layer_shard[11].astype(jnp.bfloat16), "ctx").astype(jnp.float32),
            )
        )
    boundary_rows = jnp.stack(
        [
            jnp.where(is_last, final_ticks[micro_index + 1], input_ticks[micro_index + 1])
            for micro_index in range(micro_count)
        ]
    )
    boundary = boundary_rows.reshape(1, micro_count, 1, row_count, D)
    stacked = tuple(
        (
            jnp.stack([summed[member_index] for summed in summed_layers])
            for member_index in range(12)
        )
    )
    return (
        boundary,
        stacked[0],
        stacked[1],
        stacked[2],
        stacked[3],
        stacked[4],
        stacked[5],
        stacked[6],
        stacked[7],
        stacked[8],
        stacked[9],
        stacked[10],
        stacked[11],
    )


def solution(mesh):
    placed = (
        P("section", None, "fsdp", "ctx", None),
        P(),
        P("section", "fsdp"),
        P("section", "fsdp"),
        P("section", "fsdp"),
        P("section", "fsdp"),
        P("section", "fsdp", None),
        P("section", "fsdp"),
        P("section", "fsdp", None),
        P("section", "fsdp"),
        P("section", "fsdp", None),
        P("section", "fsdp"),
        P("section", "fsdp", None),
        P("section", "fsdp"),
    )
    return jax.shard_map(
        body,
        mesh=mesh,
        in_specs=placed,
        out_specs=(
            P("section", None, "fsdp", "ctx", None),
            P("section", "fsdp"),
            P("section", "fsdp"),
            P("section", "fsdp"),
            P("section", "fsdp"),
            P("section", "fsdp", None),
            P("section", "fsdp"),
            P("section", "fsdp", None),
            P("section", "fsdp"),
            P("section", "fsdp", None),
            P("section", "fsdp"),
            P("section", "fsdp", None),
            P("section", "fsdp"),
        ),
        check_vma=False,
    )
```

profile of v0, /device:TPU:0, one launch (start us, length us, event | category | flops | bytes accessed | tf_op | source)
XLA Modules:
  0.0 1816.0 jit_solution(5353991875889386755)
XLA Ops:
  28.2 19.6 %all-reduce.60 = (bf16[768]{0:T(1024)(128)(2,1)S(1)}, bf16[768]{0:T(1024)(128)(2,1)S(1)}, bf16[768]{0:T(1024)(128)(2,1)S(1)}, bf16[2304]{0:T(1024)(128)(2,1)S(1)...) all-reduce(bf16[768]{0:T(1024)(128)(2,1)S(1)} %dynamic-update-slice, ...), channel_id=5, replica_groups=mesh['section'=2,'ctx'=16,'fsdp'=4] {'fsdp'}, use_global_device_ids=true, to_apply=%add.51 | all-reduce | flops 10752 | bytes 43008
  81.6 23.6 %all-gather.33.cloned.1.call-done = bf16[768,2305]{1,0:T(8,128)(2,1)} async-done(((bf16[192,2305]{1,0:T(8,128)(2,1)}), bf16[768,2305]{1,0:T(8,128)(2,1)}) %all-gather.33.cloned.1.call-update) | async-done | bytes 3540496 | tf_op jit(solution)/shard_map/all_gather | solution.py:37
  106.9 60.1 %all-gather.31.cloned.1.call-done = bf16[3072,769]{1,0:T(8,128)(2,1)} async-done(((bf16[768,769]{1,0:T(8,128)(2,1)}), bf16[3072,769]{1,0:T(8,128)(2,1)}) %all-gather.31.cloned.1.call-update) | async-done | bytes 4724752 | tf_op jit(solution)/shard_map/all_gather | solution.py:37
  168.6 65.3 %all-gather.29.cloned.1.call-done = bf16[768,3841]{1,0:T(8,128)(2,1)} async-done(((bf16[192,3841]{1,0:T(8,128)(2,1)}), bf16[768,3841]{1,0:T(8,128)(2,1)}) %all-gather.29.cloned.1.call-update) | async-done | bytes 5899792 | tf_op jit(solution)/shard_map/all_gather | solution.py:37
  235.5 6.7 fusion.165
  244.6 42.7 %all-gather.27.cloned.1.call-done = bf16[1024,1536]{1,0:T(8,128)(2,1)} async-done(((bf16[64,1536]{1,0:T(8,128)(2,1)}), bf16[1024,1536]{1,0:T(8,128)(2,1)}) %all-gather.27.cloned.1.call-update) | async-done | bytes 3145744 | tf_op jit(solution)/shard_map/all_gather | solution.py:18
  306.4 40.6 %all-gather.39.cloned.1.call-done = bf16[3072,769]{1,0:T(8,128)(2,1)} async-done(((bf16[768,769]{1,0:T(8,128)(2,1)}), bf16[3072,769]{1,0:T(8,128)(2,1)}) %all-gather.39.cloned.1.call-update) | async-done | bytes 4724752 | tf_op jit(solution)/shard_map/all_gather | solution.py:37
  348.4 65.5 %all-gather.37.cloned.1.call-done = bf16[768,3841]{1,0:T(8,128)(2,1)} async-done(((bf16[192,3841]{1,0:T(8,128)(2,1)}), bf16[768,3841]{1,0:T(8,128)(2,1)}) %all-gather.37.cloned.1.call-update) | async-done | bytes 5899792 | tf_op jit(solution)/shard_map/all_gather | solution.py:37
  416.6 7.0 fusion.168
  426.1 42.0 %all-gather.35.cloned.1.call-done = bf16[1024,1536]{1,0:T(8,128)(2,1)} async-done(((bf16[64,1536]{1,0:T(8,128)(2,1)}), bf16[1024,1536]{1,0:T(8,128)(2,1)}) %all-gather.35.cloned.1.call-update) | async-done | bytes 3145744 | tf_op jit(solution)/shard_map/all_gather | solution.py:18
  501.8 6.9 broadcast_select_fusion.23
  509.4 5.0 fusion.61
  514.4 36.4 %all-gather.41.cloned.1.call-done = bf16[1024,1536]{1,0:T(8,128)(2,1)} async-done(((bf16[64,1536]{1,0:T(8,128)(2,1)}), bf16[1024,1536]{1,0:T(8,128)(2,1)}) %all-gather.41.cloned.1.call-update) | async-done | bytes 3145744 | tf_op jit(solution)/shard_map/all_gather | solution.py:18
  581.7 45.2 %all-gather.43.cloned.1.call-done = bf16[1024,1536]{1,0:T(8,128)(2,1)} async-done(((bf16[64,1536]{1,0:T(8,128)(2,1)}), bf16[1024,1536]{1,0:T(8,128)(2,1)}) %all-gather.43.cloned.1.call-update) | async-done | bytes 3145744 | tf_op jit(solution)/shard_map/all_gather | solution.py:18
  665.3 6.9 broadcast_select_fusion.20
  672.2 4.9 fusion.40
  677.2 6.9 fusion.179
  692.7 40.2 %reduce-scatter.7.cloned.1.call-done = bf16[64,1536]{1,0:T(8,128)(2,1)} async-done(((bf16[1024,1536]{1,0:T(8,128)(2,1)}), bf16[64,1536]{1,0:T(8,128)(2,1)}) %reduce-scatter.7.cloned.1.call-update) | async-done | bytes 196624 | tf_op jit(solution)/shard_map/reduce_scatter | solution.py:27
  740.1 5.0 multiply_reduce_fusion.8
  762.4 42.8 %all-gather.45.cloned.1.call-done = bf16[1024,1536]{1,0:T(8,128)(2,1)} async-done(((bf16[64,1536]{1,0:T(8,128)(2,1)}), bf16[1024,1536]{1,0:T(8,128)(2,1)}) %all-gather.45.cloned.1.call-update) | async-done | bytes 3145744 | tf_op jit(solution)/shard_map/all_gather | solution.py:18
  832.2 6.8 broadcast_select_fusion.22
  839.0 5.3 fusion.57
  845.2 4.8 broadcast_select_fusion.29
  860.9 7.4 fusion.184
  871.3 34.0 %reduce-scatter.9.cloned.1.call-done = bf16[64,1536]{1,0:T(8,128)(2,1)} async-done(((bf16[1024,1536]{1,0:T(8,128)(2,1)}), bf16[64,1536]{1,0:T(8,128)(2,1)}) %reduce-scatter.9.cloned.1.call-update) | async-done | bytes 196624 | tf_op jit(solution)/shard_map/reduce_scatter | solution.py:27
  923.8 5.0 multiply_reduce_fusion.11
  931.4 4.4 collective-permute-done.1
  941.5 15.7 all-gather.47.cloned.1.call-done
  990.3 6.9 broadcast_select_fusion.19
  997.3 7.3 fusion.192
  1006.7 54.0 %reduce-scatter.11.cloned.1.call-done = bf16[64,1536]{1,0:T(8,128)(2,1)} async-done(((bf16[1024,1536]{1,0:T(8,128)(2,1)}), bf16[64,1536]{1,0:T(8,128)(2,1)}) %reduce-scatter.11.cloned.1.call-update) | async-done | bytes 196624 | tf_op jit(solution)/shard_map/reduce_scatter | solution.py:27
  1079.1 5.0 multiply_reduce_fusion.7
  1111.2 6.8 fusion.197
  1118.0 63.8 %reduce-scatter.13.cloned.1.call-done = bf16[64,1536]{1,0:T(8,128)(2,1)} async-done(((bf16[1024,1536]{1,0:T(8,128)(2,1)}), bf16[64,1536]{1,0:T(8,128)(2,1)}) %reduce-scatter.13.cloned.1.call-update) | async-done | bytes 196624 | tf_op jit(solution)/shard_map/reduce_scatter | solution.py:27
  1187.9 5.0 multiply_reduce_fusion.10
  1195.5 5.0 collective-permute-done.3
  1227.9 7.0 fusion.205
  1234.8 60.0 %reduce-scatter.15.cloned.1.call-done = bf16[64,1536]{1,0:T(8,128)(2,1)} async-done(((bf16[1024,1536]{1,0:T(8,128)(2,1)}), bf16[64,1536]{1,0:T(8,128)(2,1)}) %reduce-scatter.15.cloned.1.call-update) | async-done | bytes 196624 | tf_op jit(solution)/shard_map/reduce_scatter | solution.py:27
  1300.9 5.0 multiply_reduce_fusion.6
  1327.3 6.6 maximum_maximum_fusion.1
  1336.4 6.3 fusion.210
  1342.8 57.9 %reduce-scatter.17.cloned.1.call-done = bf16[64,1536]{1,0:T(8,128)(2,1)} async-done(((bf16[1024,1536]{1,0:T(8,128)(2,1)}), bf16[64,1536]{1,0:T(8,128)(2,1)}) %reduce-scatter.17.cloned.1.call-update) | async-done | bytes 196624 | tf_op jit(solution)/shard_map/reduce_scatter | solution.py:27
  1404.4 18.5 %maximum_maximum_fusion = bf16[192,6144]{1,0:T(8,128)(2,1)} fusion(bf16[64,3072]{1,0:T(8,128)(2,1)S(1)} %fusion.210, bf16[64,3072]{1,0:T(8,128)(2,1)S(1)} %copy-done.144, bf16[64,3072]{1,0:T(8,128)(2,1)S(1)} %copy-done.139, bf16[64,768]{1,0:T(8,128)(2,1)S(1)} %copy-done.210, bf16[64,768]{1,0:T(8,128)(2,1)S(1)} %copy-done.178, ...), kind=kLoop, calls=%fused_computation.91 | loop fusion | flops 35389440 | bytes 4718592 | tf_op jit(solution)/shard_map/concatenate | solution.py:17
  1424.0 4.5 all-to-all-start.8
  1429.5 11.8 all-to-all-done.8
  1447.7 9.6 all-to-all-done.12
  1461.8 11.1 all-to-all-done.10
  1479.2 8.9 all-to-all-done.9
  1497.0 6.8 all-to-all-done.13
  1509.7 9.1 all-to-all-done.11
  1518.8 4.5 all-to-all-start.15
  1530.7 5.4 all-to-all-done.15
  1539.8 4.1 fusion.123
  1550.3 13.5 all-to-all-done.14
  1563.9 59.8 %all-gather.49.cloned.1.call-done = bf16[768,6144]{1,0:T(8,128)(2,1)} async-done(((bf16[192,6144]{1,0:T(8,128)(2,1)}), bf16[768,6144]{1,0:T(8,128)(2,1)}) %all-gather.49.cloned.1.call-update) | async-done | bytes 9437200 | tf_op jit(solution)/shard_map/all_gather | solution.py:18
  1639.5 4.6 all-to-all-done.5
  1648.1 4.5 all-to-all-done.1
  1656.6 4.5 all-to-all-done.3
  1664.6 4.2 fusion.34
  1673.6 4.6 multiply_reduce_fusion.9
  1683.8 4.2 all-to-all-done.4
  1692.0 4.6 all-to-all-done
  1709.2 4.4 all-to-all-done.6
  1728.9 65.1 %all-reduce.58 = (bf16[1,192]{1,0:T(2,128)(2,1)S(1)}, bf16[1,192]{1,0:T(2,128)(2,1)S(1)}, bf16[1,192]{1,0:T(2,128)(2,1)S(1)}, bf16[1,192]{1,0:T(2,128)(2,1)S(1)}...) all-reduce(bf16[1,192]{1,0:T(2,128)(2,1)S(1)} %stack.170, ...), channel_id=1, replica_groups=mesh['section'=2,'ctx'=16,'fsdp'=4] {'ctx'}, use_global_device_ids=true, to_apply=%region_81.82 | all-reduce | flops 4608 | bytes 18432 | tf_op jit(solution)/shard_map/psum | solution.py:425
  (1477 shorter events, 571.7 us)
Async XLA Ops:
  7.2 51.8 %all-gather.25.cloned.1.call-start = ((), (), s32[]{:S(2)}) async-start(), calls=%async_computation.22 | async-start | bytes 4669440 | tf_op jit(solution)/shard_map/all_gather | solution.py:37
  11.0 94.2 %all-gather.33.cloned.1.call-start = ((), (), s32[]{:S(2)}) async-start(), calls=%async_computation.26 | async-start | bytes 4669440 | tf_op jit(solution)/shard_map/all_gather | solution.py:37
  12.6 154.4 %all-gather.31.cloned.1.call-start = ((), (), s32[]{:S(2)}) async-start(), calls=%async_computation.25 | async-start | bytes 6881280 | tf_op jit(solution)/shard_map/all_gather | solution.py:37
  16.5 217.4 %all-gather.29.cloned.1.call-start = ((), (), s32[]{:S(2)}) async-start(), calls=%async_computation.24 | async-start | bytes 7618560 | tf_op jit(solution)/shard_map/all_gather | solution.py:37
  23.8 263.4 %all-gather.27.cloned.1.call-start = ((), (), s32[]{:S(2)}) async-start(), calls=%async_computation.23 | async-start | bytes 3342336 | tf_op jit(solution)/shard_map/all_gather | solution.py:18
  60.6 174.9 %copy-start.114 = (bf16[64,768]{1,0:T(8,128)(2,1)}, bf16[64,768]{1,0:T(8,128)(2,1)S(1)}, u32[]{:S(2)}) copy-start(bf16[64,768]{1,0:T(8,128)(2,1)S(1)} %get-tuple-element.320) | copy-start | bytes 294916
  71.0 276.0 %all-gather.39.cloned.1.call-start = ((), (), s32[]{:S(2)}) async-start(), calls=%async_computation.29 | async-start | bytes 6881280 | tf_op jit(solution)/shard_map/all_gather | solution.py:37
  73.0 340.9 %all-gather.37.cloned.1.call-start = ((), (), s32[]{:S(2)}) async-start(), calls=%async_computation.28 | async-start | bytes 7618560 | tf_op jit(solution)/shard_map/all_gather | solution.py:37
  77.0 391.1 %all-gather.35.cloned.1.call-start = ((), (), s32[]{:S(2)}) async-start(), calls=%async_computation.27 | async-start | bytes 3342336 | tf_op jit(solution)/shard_map/all_gather | solution.py:18
  79.8 162.4 %copy-start.282 = (s32[1024]{0:T(1024)}, s32[1024]{0:T(1024)S(1)}, u32[]{:S(2)}) copy-start(s32[1024]{0:T(1024)S(1)} %get-tuple-element.79) | copy-start | bytes 12292
  79.8 162.4 %copy-start.287 = (s32[1024]{0:T(1024)}, s32[1024]{0:T(1024)S(1)}, u32[]{:S(2)}) copy-start(s32[1024]{0:T(1024)S(1)} %get-tuple-element.78) | copy-start | bytes 12292
  167.0 75.2 %slice-start.6 = ((s8[5505024]{0:T(1024)(128)(4,1)}), s8[1310720]{0:T(1024)(128)(4,1)S(1)}, s32[]{:S(2)}) async-start(s8[5505024]{0:T(1024)(128)(4,1)} %bitcast.500), calls=%async_computation.49 | async-start | bytes 2621440
  168.6 73.6 %copy-start.313 = (f32[3072]{0:T(1024)}, f32[3072]{0:T(1024)S(1)}, u32[]{:S(2)}) copy-start(f32[3072]{0:T(1024)S(1)} %convert_reduce_fusion.7) | copy-start | bytes 36868
  301.0 115.6 %copy-start.108 = (bf16[64,768]{1,0:T(8,128)(2,1)}, bf16[64,768]{1,0:T(8,128)(2,1)S(1)}, u32[]{:S(2)}) copy-start(bf16[64,768]{1,0:T(8,128)(2,1)S(1)} %get-tuple-element.349) | copy-start | bytes 294916
  305.6 245.3 %all-gather.41.cloned.1.call-start = ((), (), s32[]{:S(2)}) async-start(), calls=%async_computation.30 | async-start | bytes 3342336 | tf_op jit(solution)/shard_map/all_gather | solution.py:18
  348.4 75.3 %copy-start.312 = (f32[3072]{0:T(1024)}, f32[3072]{0:T(1024)S(1)}, u32[]{:S(2)}) copy-start(f32[3072]{0:T(1024)S(1)} %convert_reduce_fusion.6) | copy-start | bytes 36868
  472.1 219.2 %copy-start.8 = (bf16[1024,768]{0,1:T(8,128)(2,1)}, bf16[1024,768]{0,1:T(8,128)(2,1)S(1)}, u32[]{:S(2)}) copy-start(bf16[1024,768]{0,1:T(8,128)(2,1)S(1)} %copy.607) | copy-start | bytes 4718596
  480.5 4.9 collective-permute-start
  499.4 127.5 %all-gather.43.cloned.1.call-start = ((), (), s32[]{:S(2)}) async-start(), calls=%async_computation.31 | async-start | bytes 3342336 | tf_op jit(solution)/shard_map/all_gather | solution.py:18
  577.3 155.6 %reduce-scatter.7.cloned.1.call-start = ((), (), s32[]{:S(2)}) async-start(), calls=%async_computation.32 | async-start | bytes 3342336 | tf_op jit(solution)/shard_map/reduce_scatter | solution.py:27
  657.2 148.0 %all-gather.45.cloned.1.call-start = ((), (), s32[]{:S(2)}) async-start(), calls=%async_computation.34 | async-start | bytes 3342336 | tf_op jit(solution)/shard_map/all_gather | solution.py:18
  687.8 57.7 %collective-permute-start.2 = (bf16[64,768]{1,0:T(8,128)(2,1)}, bf16[64,768]{1,0:T(8,128)(2,1)}, u32[]{:S(2)}, u32[]{:S(2)}) collective-permute-start(bf16[64,768]{1,0:T(8,128)(2,1)} %get-tuple-element.493), channel_id=1, source_target_pairs={{0,64},{1,65},{2,66},{3,67},{4,68},{5,69},{6,70},{7,71},{8,72},{9,... | collective-permute-start | bytes 294920 | tf_op jit(solution)/shard_map/ppermute | solution.py:48
  755.6 149.8 %reduce-scatter.9.cloned.1.call-start = ((), (), s32[]{:S(2)}) async-start(), calls=%async_computation.33 | async-start | bytes 3342336 | tf_op jit(solution)/shard_map/reduce_scatter | solution.py:27
  831.2 126.0 %all-gather.47.cloned.1.call-start = ((), (), s32[]{:S(2)}) async-start(), calls=%async_computation.35 | async-start | bytes 3342336 | tf_op jit(solution)/shard_map/all_gather | solution.py:18
  859.6 201.0 %reduce-scatter.11.cloned.1.call-start = ((), (), s32[]{:S(2)}) async-start(), calls=%async_computation.36 | async-start | bytes 3342336 | tf_op jit(solution)/shard_map/reduce_scatter | solution.py:27
  929.2 6.5 collective-permute-start.1
  986.4 195.4 %reduce-scatter.13.cloned.1.call-start = ((), (), s32[]{:S(2)}) async-start(), calls=%async_computation.37 | async-start | bytes 3342336 | tf_op jit(solution)/shard_map/reduce_scatter | solution.py:27
  1107.6 187.2 %reduce-scatter.15.cloned.1.call-start = ((), (), s32[]{:S(2)}) async-start(), calls=%async_computation.38 | async-start | bytes 3342336 | tf_op jit(solution)/shard_map/reduce_scatter | solution.py:27
  1111.2 71.8 %copy-start.98 = (f32[64,12,64]{0,2,1:T(8,128)S(1)}, f32[64,12,64]{0,2,1:T(8,128)}, u32[]{:S(2)}) copy-start(f32[64,12,64]{0,2,1:T(8,128)} %copy-done.97) | copy-start | bytes 589828
  1111.2 71.8 %copy-start.257 = (f32[64,16]{0,1:T(8,128)S(1)}, f32[64,16]{0,1:T(8,128)}, u32[]{:S(2)}) copy-start(f32[64,16]{0,1:T(8,128)} %get-tuple-element.533) | copy-start | bytes 12292
  1118.0 65.8 %slice-start = ((f32[64,12,64]{0,2,1:T(8,128)}), f32[64,12,48]{0,2,1:T(8,128)S(1)}, s32[]{:S(2)}) async-start(f32[64,12,64]{0,2,1:T(8,128)} %copy-done.97), calls=%async_computation.43 | async-start | bytes 589824 | tf_op jit(solution)/shard_map/transpose(jvp())/split | solution.py:78
  1194.1 6.5 collective-permute-start.3
  1220.7 180.0 %reduce-scatter.17.cloned.1.call-start = ((), (), s32[]{:S(2)}) async-start(), calls=%async_computation.39 | async-start | bytes 3342336 | tf_op jit(solution)/shard_map/reduce_scatter | solution.py:27
  1227.8 68.2 %copy-start.101 = (f32[64,12,64]{0,2,1:T(8,128)S(1)}, f32[64,12,64]{0,2,1:T(8,128)}, u32[]{:S(2)}) copy-start(f32[64,12,64]{0,2,1:T(8,128)} %copy-done.100) | copy-start | bytes 589828
  1227.8 68.2 %copy-start.255 = (f32[64,16]{0,1:T(8,128)S(1)}, f32[64,16]{0,1:T(8,128)}, u32[]{:S(2)}) copy-start(f32[64,16]{0,1:T(8,128)} %get-tuple-element.535) | copy-start | bytes 12292
  1234.8 62.0 %slice-start.2 = ((f32[64,12,64]{0,2,1:T(8,128)}), f32[64,12,48]{0,2,1:T(8,128)S(1)}, s32[]{:S(2)}) async-start(f32[64,12,64]{0,2,1:T(8,128)} %copy-done.100), calls=%async_computation.45 | async-start | bytes 589824 | tf_op jit(solution)/shard_map/transpose(jvp())/split | solution.py:78
  1326.4 213.4 %all-gather.51.cloned.1.call-start = ((), (), s32[]{:S(2)}) async-start(), calls=%async_computation.41 | async-start | bytes 11796480 | tf_op jit(solution)/shard_map/all_gather | solution.py:18
  1334.0 289.7 %all-gather.49.cloned.1.call-start = ((), (), s32[]{:S(2)}) async-start(), calls=%async_computation.40 | async-start | bytes 11796480 | tf_op jit(solution)/shard_map/all_gather | solution.py:18
  1336.4 65.6 %copy-start.256 = (f32[64,16]{0,1:T(8,128)S(1)}, f32[64,16]{0,1:T(8,128)}, u32[]{:S(2)}) copy-start(f32[64,16]{0,1:T(8,128)} %get-tuple-element.535) | copy-start | bytes 12292
  1336.4 66.5 %copy-start.245 = (f32[64,16]{0,1:T(8,128)S(1)}, f32[64,16]{0,1:T(8,128)}, u32[]{:S(2)}) copy-start(f32[64,16]{0,1:T(8,128)} %get-tuple-element.534) | copy-start | bytes 12292
  1342.7 80.1 %copy-start.141 = (bf16[64,3072]{1,0:T(8,128)(2,1)}, bf16[64,3072]{1,0:T(8,128)(2,1)S(1)}, u32[]{:S(2)}) copy-start(bf16[64,3072]{1,0:T(8,128)(2,1)S(1)} %fusion.210) | copy-start | bytes 1179652
  1342.7 61.5 %copy-start.139 = (bf16[64,3072]{1,0:T(8,128)(2,1)S(1)}, bf16[64,3072]{1,0:T(8,128)(2,1)}, u32[]{:S(2)}) copy-start(bf16[64,3072]{1,0:T(8,128)(2,1)} %fusion.184) | copy-start | bytes 1179652
  1342.7 61.5 %copy-start.144 = (bf16[64,3072]{1,0:T(8,128)(2,1)S(1)}, bf16[64,3072]{1,0:T(8,128)(2,1)}, u32[]{:S(2)}) copy-start(bf16[64,3072]{1,0:T(8,128)(2,1)} %fusion.197) | copy-start | bytes 1179652
  1342.8 61.5 %copy-start.175 = (bf16[64,768]{1,0:T(8,128)(2,1)S(1)}, bf16[64,768]{1,0:T(8,128)(2,1)}, u32[]{:S(2)}) copy-start(bf16[64,768]{1,0:T(8,128)(2,1)} %copy-done.174) | copy-start | bytes 294916
  1342.8 61.5 %copy-start.178 = (bf16[64,768]{1,0:T(8,128)(2,1)S(1)}, bf16[64,768]{1,0:T(8,128)(2,1)}, u32[]{:S(2)}) copy-start(bf16[64,768]{1,0:T(8,128)(2,1)} %copy-done.176) | copy-start | bytes 294916
  1342.8 61.5 %copy-start.183 = (bf16[64,768]{1,0:T(8,128)(2,1)S(1)}, bf16[64,768]{1,0:T(8,128)(2,1)}, u32[]{:S(2)}) copy-start(bf16[64,768]{1,0:T(8,128)(2,1)} %copy.737) | copy-start | bytes 294916
  1342.8 61.5 %copy-start.184 = (bf16[64,768]{1,0:T(8,128)(2,1)S(1)}, bf16[64,768]{1,0:T(8,128)(2,1)}, u32[]{:S(2)}) copy-start(bf16[64,768]{1,0:T(8,128)(2,1)} %copy.738) | copy-start | bytes 294916
  1424.0 17.3 all-to-all-start.8
  1441.3 16.0 all-to-all-start.12
  1457.3 15.6 all-to-all-start.10
  1472.9 15.2 all-to-all-start.9
  1488.1 15.7 all-to-all-start.13
  1503.8 15.0 all-to-all-start.11
  1518.8 17.4 all-to-all-start.15
  1536.2 27.7 %all-to-all-start.14 = ((bf16[192,4,768]{2,0,1:T(8,128)(2,1)}), bf16[192,4,768]{2,0,1:T(8,128)(2,1)S(1)}, u32[]{:S(2)}, u32[]{:S(2)}) async-start(bf16[192,4,768]{2,0,1:T(8,128)(2,1)} %bitcast.349), calls=%async_computation.20 | async-start | bytes 2359296 | tf_op jit(solution)/shard_map/all_to_all | solution.py:391
  1539.7 257.9 %all-reduce.63.cloned.1.call-start = ((), (), s32[]{:S(2)}) async-start(), calls=%async_computation.42 | async-start | bytes 14155776 | tf_op jit(solution)/shard_map/psum | solution.py:429
  1634.9 9.2 all-to-all-start.5
  1644.1 8.5 all-to-all-start.1
  1652.6 8.5 all-to-all-start.3
  1661.1 8.7 all-to-all-start.7
  1678.9 9.1 all-to-all-start.4
  1688.1 8.5 all-to-all-start
  1696.6 8.5 all-to-all-start.2
  1705.1 8.5 all-to-all-start.6
  (389 other events, 2840.3 us)
Sparse Core Ops, SparseCore 0:
  11.1 47.7 all-gather.24
  60.6 44.6 all-gather.32
  107.5 59.4 all-gather.30
  169.1 64.6 all-gather.28
  236.1 51.0 all-gather.26
  288.8 58.2 all-gather.38
  349.3 64.6 all-gather.36
  417.0 51.0 all-gather.34
  499.5 51.3 all-gather.40
  577.4 49.4 all-gather.42
  657.3 75.5 reduce-scatter.6
  755.7 49.4 all-gather.44
  831.3 73.9 reduce-scatter.8
  907.7 49.4 all-gather.46
  986.5 74.0 reduce-scatter.10
  1107.8 74.0 reduce-scatter.12
  1220.8 74.0 reduce-scatter.14
  1326.5 74.1 reduce-scatter.16
  1402.9 116.7 all-gather.50
  1521.8 101.7 all-gather.48
  1633.8 160.1 all-reduce.62
where the time goes:
time: 1830 us; the launch traced here: 1820 us
  waiting for transfers between devices  971 us (53%)
  matrix products  294 us (16%)
  other arithmetic  194 us (11%)
  local copies, waits for them, and re-layouts  180 us (10%)
  blocking collectives  84.6 us (5%)
  starting transfers between devices  69.6 us (4%)
  between operations  22.5 us (1%)
    reduce_scatter x6, waiting for transfers between devices, in_one_piece_2(): lax.psum_scatter(both, axis, scatter_dimension=dim, tiled=True)  310 us
    all_gather x8, waiting for transfers between devices, in_one_piece(): lax.all_gather(both, axis, axis=dim, tiled=True)  285 us
    all_gather x6, waiting for transfers between devices, side_by_side(): lax.all_gather(both, axis, axis=dim, tiled=True)  259 us
    dot_general x24, matrix products, by_cols(): lax.dot_general(left_side, right_side, (((1,), (1,)), ((), ())), preferre...  105 us
    dot_general x24, matrix products, matmul(): return jnp.dot(left_side, right_side, preferred_element_type=jnp.float32)  91.3 us
    psum x1, blocking collectives, body(): lax.psum(layer_shard[0].astype(jnp.bfloat16), 'ctx').astype(jnp.float32)  65.1 us
    slice x18, local copies, waits for them, and re-layouts, in_one_piece(): lax.slice_in_dim(whole, at, at + a.shape[along], axis=along)  46.2 us
  transfers between devices with their start and end apart: 41, of which 38 were waited for; matrix products, arithmetic and copies ran while one was open for 21% of the time, Pallas kernels for 0%

commit v1 on v0

v1 whole, which is shorter than its diff:
```python
import functools

import jax
import jax.numpy as jnp
from jax import lax
from jax.experimental import pallas as pl
from jax.experimental.pallas import tpu as pltpu
from jax.sharding import Mesh, PartitionSpec as P

D = 768
H = 12
HD = 64
FF = 3072
ROT = 16
LAYERS = 4
EPSILON = 1e-05
SCORE_SCALE = 0.125
CHIPS = ("xh", "y")
CTX = ("xh", "y", "c")
EVERY = ("s", "xh", "y", "c", "z")
BF = jnp.bfloat16
F32 = jnp.float32
ROWS = 64
SEQ = 1024
HALF = SEQ // 2
BLOCK = 256
UNITS = 192
SHARE = 416
PACK = 432
VMEM = pltpu.VMEM
ROOM = 56 * 1024 * 1024


def shifted(block, axis, distance):
    size = lax.axis_size(axis)
    return lax.ppermute(block, axis, [(i, (i + distance) % size) for i in range(size)])


def dot(left, right, left_dim=1, right_dim=0):
    return lax.dot_general(
        left, right, (((left_dim,), (right_dim,)), ((), ())), preferred_element_type=F32
    )


def call(kernel, outs, *args, scratch=(), smem=0):
    specs = [pl.BlockSpec(memory_space=pltpu.SMEM)] * smem
    specs += [pl.BlockSpec(memory_space=VMEM)] * (len(args) - smem)
    return pl.pallas_call(
        kernel,
        out_shape=[jax.ShapeDtypeStruct(shape, dtype) for shape, dtype in outs],
        in_specs=specs,
        out_specs=[pl.BlockSpec(memory_space=VMEM)] * len(outs),
        scratch_shapes=list(scratch),
        compiler_params=pltpu.CompilerParams(vmem_limit_bytes=ROOM),
    )(*args)


def centred(x):
    offset = x - jnp.mean(x, -1, keepdims=True)
    scale = lax.rsqrt(jnp.mean(offset * offset, -1, keepdims=True) + EPSILON)
    return offset * scale, scale


def start_kernel(x, n_out):
    n = centred(x[...])[0].astype(BF)
    for k in range(8):
        n_out[k] = n


def finish_kernel(rounded, got, x, bias, x_out, n_out):
    total = got[0].astype(F32)
    for k in range(1, 8):
        total = total + got[k].astype(F32)
    x_next = x[...] + (total + bias[...])
    if rounded:
        x_next = x_next.astype(BF).astype(F32)
    x_out[...] = x_next
    n = centred(x_next)[0].astype(BF)
    for k in range(8):
        n_out[k] = n


def finish_back_kernel(rounded, got, x, dx, dx_out, branch_out):
    gy = got[0].astype(F32)
    for k in range(1, 8):
        gy = gy + got[k].astype(F32)
    n, scale = centred(x[...])
    inner = jnp.mean(gy * n, -1, keepdims=True)
    dx_next = dx[...] + scale * (gy - jnp.mean(gy, -1, keepdims=True) - n * inner)
    if rounded:
        dx_next = dx_next.astype(BF).astype(F32)
    dx_out[...] = dx_next
    branch = dx_next.astype(BF)
    for k in range(8):
        branch_out[k] = branch


def share_weights(owner, share, w_qkv, w_up, w_down, w_out):
    for z in range(4):
        w_qkv[pl.ds(z * 192, 192), :] = share[z, 0:192, 0:192]
        w_up[pl.ds(z * 192, 192), :] = share[z, 0:192, 192:384]
        w_down[pl.ds(z * 48, 48), 0:384] = share[z, 192:240, :]
        w_down[pl.ds(z * 48, 48), 384:768] = share[z, 304:352, :]
    at = owner[0]
    w_out[:, 0:384] = share[at, 240:304, :]
    w_out[:, 384:768] = share[at, 352:416, :]


WEIGHT_SCRATCH = (
    VMEM((D, UNITS), BF),
    VMEM((D, UNITS), BF),
    VMEM((UNITS, D), BF),
    VMEM((HD, D), BF),
)


def scored(q, k, query_places, key_places):
    scores = dot(q, k, 1, 1) * SCORE_SCALE
    scores = jnp.where(query_places >= key_places, scores, -1e30)
    raised = jnp.exp(scores - jnp.max(scores, -1, keepdims=True))
    return raised / jnp.sum(raised, -1, keepdims=True)


def turn(v, tables, rows, sign):
    cosine, ahead, behind = tables
    return v * cosine[rows, :] + sign * (
        pltpu.roll(v, 120, 1) * ahead[rows, :] + pltpu.roll(v, 8, 1) * behind[rows, :]
    )


def forward_kernel(
    owner, own, other, vec, bias, share, cosine, ahead, behind, p_col, p_row,
    part_own, part_other, qkv, pre, act,
    w_qkv, w_up, w_down, w_out,
):
    share_weights(owner, share, w_qkv, w_up, w_down, w_out)
    tables = (cosine, ahead, behind)
    for half, source in enumerate((own, other)):

        @pl.loop(0, HALF // BLOCK)
        def _(step):
            here = pl.ds(step * BLOCK, BLOCK)
            rows = pl.ds(half * HALF + step * BLOCK, BLOCK)
            n = source[here, :].astype(F32)
            one = (n * vec[0:1, :] + vec[1:2, :]).astype(BF)
            two = (n * vec[2:3, :] + vec[3:4, :]).astype(BF)
            merged = dot(one, w_qkv[...]) + bias[0:1, 0:192]
            qkv[rows, 0:128] = turn(merged[:, 0:128], tables, rows, 1.0).astype(BF)
            qkv[rows, 128:192] = merged[:, 128:192].astype(BF)
            up = dot(two, w_up[...]) + bias[1:2, 0:192]
            pre[rows, :] = up
            act[rows, 0:192] = (0.5 * up * (1.0 + lax.erf(up * 0.7071067811865476))).astype(BF)

    k, v = qkv[:, 64:128], qkv[:, 128:192]
    for half, target in enumerate((part_own, part_other)):

        @pl.loop(0, HALF // BLOCK)
        def _(step):
            here = pl.ds(step * BLOCK, BLOCK)
            rows = pl.ds(half * HALF + step * BLOCK, BLOCK)
            probs = scored(qkv[rows, 0:64], k, p_col[rows, :], p_row[...]).astype(BF)
            attended = dot(probs, v).astype(BF)
            act[rows, 192:256] = attended
            part = dot(attended, w_out[...]) + dot(act[rows, 0:192], w_down[...])
            target[here, :] = part.astype(BF)


def backward_kernel(
    owner, b_own, b_other, n_own, n_other, vec, share, cosine, ahead, behind, p_col, p_row, qkv, pre,
    gy_own, gy_other, d_qkv, d_up, sums,
    w_qkv, w_up, w_down, w_out, dq, dk, dv,
):
    share_weights(owner, share, w_qkv, w_up, w_down, w_out)
    tables = (cosine, ahead, behind)
    dk[...] = jnp.zeros_like(dk)
    dv[...] = jnp.zeros_like(dv)
    sums[...] = jnp.zeros_like(sums)
    k, v = qkv[:, 64:128], qkv[:, 128:192]
    for half, source in enumerate((b_own, b_other)):

        @pl.loop(0, HALF // BLOCK)
        def _(step):
            rows = pl.ds(half * HALF + step * BLOCK, BLOCK)
            branch = source[pl.ds(step * BLOCK, BLOCK), :]
            sums[5:6, :] += jnp.sum(branch.astype(F32), 0, keepdims=True)
            hidden = dot(branch, w_down[...], 1, 1)
            up = pre[rows, :]
            slope = 0.5 * (1.0 + lax.erf(up * 0.7071067811865476)) + up * (
                jnp.exp(-0.5 * up * up) * 0.3989422804014327
            )
            d_up[rows, :] = (slope * hidden).astype(BF)
            grad = dot(branch, w_out[...], 1, 1).astype(BF)
            q = qkv[rows, 0:64]
            probs = scored(q, k, p_col[rows, :], p_row[...])
            prob_grad = dot(grad, v, 1, 1)
            inner = jnp.sum(probs * prob_grad, -1, keepdims=True)
            score_grad = (probs * (prob_grad - inner)).astype(BF)
            dq[rows, :] = dot(score_grad, k)
            dk[...] += dot(score_grad, q, 0, 0)
            dv[...] += dot(probs.astype(BF), grad, 0, 0)

    for half, (source, target) in enumerate(((n_own, gy_own), (n_other, gy_other))):

        @pl.loop(0, HALF // BLOCK)
        def _(step):
            here = pl.ds(step * BLOCK, BLOCK)
            rows = pl.ds(half * HALF + step * BLOCK, BLOCK)
            both = jnp.concatenate([dq[rows, :], dk[rows, :]], 1) * SCORE_SCALE
            d_qkv[rows, 0:128] = turn(both, tables, rows, -1.0).astype(BF)
            d_qkv[rows, 128:192] = dv[rows, :].astype(BF)
            g_qkv, g_up = d_qkv[rows, :], d_up[rows, :]
            one = dot(g_qkv, w_qkv[...], 1, 1)
            two = dot(g_up, w_up[...], 1, 1)
            target[here, :] = (one * vec[0:1, :] + two * vec[2:3, :]).astype(BF)
            n = source[here, :].astype(F32)
            for at, part in enumerate((one * n, one, two * n, two)):
                sums[at : at + 1, :] += jnp.sum(part, 0, keepdims=True)
            sums[4:5, 0:192] += jnp.sum(g_qkv.astype(F32), 0, keepdims=True)
            sums[6:7, 0:192] += jnp.sum(g_up.astype(F32), 0, keepdims=True)


def product_kernel(b_own, b_other, n_own, n_other, vec, act, d_qkv, d_up, sums, pack, in_qkv, in_up, in_act):
    in_qkv[...] = jnp.zeros_like(in_qkv)
    in_up[...] = jnp.zeros_like(in_up)
    in_act[...] = jnp.zeros_like(in_act)
    for half, (branch, normal) in enumerate(((b_own, n_own), (b_other, n_other))):

        @pl.loop(0, HALF // BLOCK)
        def _(step):
            here = pl.ds(step * BLOCK, BLOCK)
            rows = pl.ds(half * HALF + step * BLOCK, BLOCK)
            n = normal[here, :].astype(F32)
            one = (n * vec[0:1, :] + vec[1:2, :]).astype(BF)
            two = (n * vec[2:3, :] + vec[3:4, :]).astype(BF)
            in_qkv[...] += dot(one, d_qkv[rows, :], 0, 0)
            in_up[...] += dot(two, d_up[rows, :], 0, 0)
            in_act[...] += dot(act[rows, :], branch[here, :], 0, 0)

    blank = jnp.zeros((12, 384), F32)
    out = in_act[192:256, :].astype(BF)
    for z in range(4):
        pack[z, 0:192, 0:192] = in_qkv[z * 192 : (z + 1) * 192, :].astype(BF)
        pack[z, 0:192, 192:384] = in_up[z * 192 : (z + 1) * 192, :].astype(BF)
        down = in_act[z * 48 : (z + 1) * 48, :].astype(BF)
        pack[z, 192:240, :] = down[:, 0:384]
        pack[z, 240:304, :] = out[:, 0:384]
        pack[z, 304:352, :] = down[:, 384:768]
        pack[z, 352:416, :] = out[:, 384:768]
        cut = sums[:, z * 192 : (z + 1) * 192]
        left = jnp.concatenate([cut[0:1], cut[2:3], sums[4:5, 0:192], cut[5:6]], 0)
        right = jnp.concatenate([cut[1:2], cut[3:4], sums[6:7, 0:192], jnp.zeros((1, 192), F32)], 0)
        rows = jnp.concatenate([left, right], 1)
        pack[z, 416:432, :] = jnp.concatenate([rows, blank], 0).astype(BF)


def unpack_kernel(place, own_a, other_a, own_b, other_b, g_qkv, g_out, g_up, g_down, rest):
    low = place[0] == 0
    z = place[1]
    for j, (own, other) in enumerate(((own_a, other_a), (own_b, other_b))):
        for i in range(16):
            k = i // 2
            mine, theirs = (own, other) if i % 2 == 0 else (other, own)
            block = jnp.where(low, mine[k].astype(F32), theirs[k].astype(F32))
            if i < H:
                for t in range(3):
                    g_qkv[j, :, t * D + i * HD : t * D + (i + 1) * HD] = block[0:192, t * HD : (t + 1) * HD]
            for t in range(4):
                at = t * D + i * 48
                g_up[j, :, at : at + 48] = block[0:192, 192 + t * 48 : 240 + t * 48]
            g_down[j, i * 48 : (i + 1) * 48, 0:384] = block[192:240, :]
            g_down[j, i * 48 : (i + 1) * 48, 384:768] = block[304:352, :]
            rest[j, i] = block[416:432, :]
        for h in range(3):
            i = 3 * z + h
            k = i // 2
            mine = (i % 2) == place[0]
            out = jnp.where(mine, own[k].astype(F32), other[k].astype(F32))
            g_out[j, h * HD : (h + 1) * HD, 0:384] = out[240:304, :]
            g_out[j, h * HD : (h + 1) * HD, 384:768] = out[352:416, :]


def body(ends, blocks, g1, h1, g2, h2, wq, bq, wo, bo, wu, bu, wd, bd):
    s = lax.axis_index("s")
    c = lax.axis_index("c")
    z = lax.axis_index("z")
    first = s == 0
    unit = lax.axis_index(CTX)
    has_head = unit < H
    owner = jnp.minimum(unit // 3, 3).astype(jnp.int32)

    keep = jnp.where(first, ends[0, 0, 0], ends[0, 1, 0])
    received = shifted(jnp.where(first, ends[0, 1, 0], ends[0, 0, 0]), "s", 1)
    x = jnp.where(first, keep, received).astype(F32)
    dx = jnp.where(first, received, keep)

    def from_chips(sent):
        own = lax.all_to_all(sent, CHIPS, 0, 0, tiled=True)
        return own.reshape(HALF, D), shifted(own, "c", 1).reshape(HALF, D)

    def to_chips(own, other):
        part = own + shifted(other, "c", 1)
        return lax.all_to_all(part.reshape(8, ROWS, D), CHIPS, 0, 0, tiled=True)

    n_sent = call(start_kernel, [((8, ROWS, D), BF)], x)[0]
    normals = from_chips(n_sent)

    def share_of(j):
        mask = has_head.astype(BF)
        cols = [lax.dynamic_slice_in_dim(wq[j], t * D + unit * HD, HD, 1) * mask for t in range(3)]
        cols += [lax.dynamic_slice_in_dim(wu[j], t * D + unit * 48, 48, 1) for t in range(4)]
        down = lax.dynamic_slice_in_dim(wd[j], unit * 48, 48, 0)
        out = lax.dynamic_slice_in_dim(wo[j], (unit % 3) * HD, HD, 0) * mask
        rows = jnp.concatenate([down, out], 0)
        return jnp.concatenate([jnp.concatenate(cols, 1), rows[:, :384], rows[:, 384:]], 0)

    def joined_sections(mine):
        theirs = shifted(mine, "s", 1)
        return jnp.where(first, mine, theirs), jnp.where(first, theirs, mine)

    def round_z(block):
        whole = jnp.zeros((4,) + block.shape, BF)
        whole = lax.dynamic_update_slice_in_dim(whole, block[None], z, 0)
        for k in range(1, 4):
            whole = lax.dynamic_update_slice_in_dim(
                whole, shifted(block, "z", k)[None], (z - k) % 4, 0
            )
        return whole

    vectors = jnp.concatenate([g1, h1, g2, h2, bq, bo, bu, bd], 1)
    vectors = round_z(jnp.concatenate(joined_sections(vectors), 0))
    layer_vec, layer_bias, layer_add = [], [], []
    for l in range(LAYERS):
        at, members = 0, []
        for width in (192, 192, 192, 192, 576, 192, 768, 192):
            members.append(vectors[:, l, at : at + width].reshape(1, -1).astype(F32))
            at += width
        layer_vec.append(jnp.concatenate(members[:4] + [jnp.zeros((4, D), F32)], 0))
        head = [lax.dynamic_slice_in_dim(members[4], t * D + unit * HD, HD, 1) for t in range(3)]
        units = [lax.dynamic_slice_in_dim(members[6], t * D + unit * 48, 48, 1) for t in range(4)]
        layer_bias.append(
            jnp.concatenate(
                [jnp.concatenate(head, 1), jnp.concatenate(units, 1), jnp.zeros((6, UNITS), F32)], 0
            )
        )
        layer_add.append(members[5] + members[7])

    early = joined_sections(share_of(0))
    later = joined_sections(share_of(1))
    layer_share = [round_z(early[0])]
    rest = round_z(jnp.stack([later[0], early[1], later[1]]))
    layer_share += [rest[:, i] for i in range(3)]

    blk = ROWS // 2
    offsets = jnp.arange(SEQ, dtype=jnp.int32)
    row_blocks = jnp.where(first, blocks[0], blocks[1])
    places = (jnp.repeat(row_blocks, blk) * blk + offsets % blk).reshape(8, 2, ROWS)
    places = jnp.where(c == 0, places, places[:, ::-1]).transpose(1, 0, 2).reshape(SEQ)
    half = ROT // 2
    frequencies = 10000.0 ** (-jnp.arange(half, dtype=F32) * 2.0 / ROT)
    angles = places.astype(F32)[:, None] * frequencies[None, :]
    cos, sin = jnp.cos(angles), jnp.sin(angles)
    none = jnp.zeros((SEQ, half), F32)
    still = jnp.zeros((SEQ, HD - ROT), F32)
    cosine = jnp.concatenate([cos, cos, still + 1.0] * 2, 1)
    ahead = jnp.concatenate([-sin, none, still] * 2, 1)
    behind = jnp.concatenate([none, sin, still] * 2, 1)
    tables = (cosine, ahead, behind, places[:, None], places[None, :])
    owner = owner.reshape(1)

    kept = []
    for l in range(LAYERS):
        own, other, qkv, pre, act = call(
            forward_kernel,
            [((HALF, D), BF), ((HALF, D), BF), ((SEQ, UNITS), BF), ((SEQ, UNITS), F32), ((SEQ, 256), BF)],
            owner, *normals, layer_vec[l], layer_bias[l], layer_share[l], *tables,
            scratch=WEIGHT_SCRATCH, smem=1,
        )
        kept.append((x, normals, qkv, pre, act))
        got = to_chips(own, other)
        x, n_sent = call(
            functools.partial(finish_kernel, l == 1),
            [((ROWS, D), F32), ((8, ROWS, D), BF)], got, x, layer_add[l],
        )
        if l + 1 < LAYERS:
            normals = from_chips(n_sent)
    final = x

    branches = from_chips(jnp.broadcast_to(dx[None], (8, ROWS, D)))
    dx = dx.astype(F32)
    shares = [None] * LAYERS
    for l in reversed(range(LAYERS)):
        x, normals, qkv, pre, act = kept[l]
        own, other, d_qkv, d_up, sums = call(
            backward_kernel,
            [((HALF, D), BF), ((HALF, D), BF), ((SEQ, UNITS), BF), ((SEQ, UNITS), BF), ((8, D), F32)],
            owner, *branches, *normals, layer_vec[l], layer_share[l], *tables, qkv, pre,
            scratch=WEIGHT_SCRATCH + (VMEM((SEQ, HD), F32),) * 3, smem=1,
        )
        got = to_chips(own, other)
        pack = call(
            product_kernel, [((4, PACK, 384), BF)],
            *branches, *normals, layer_vec[l], act, d_qkv, d_up, sums,
            scratch=(VMEM((D, UNITS), F32), VMEM((D, UNITS), F32), VMEM((256, D), F32)),
        )[0]
        total = lax.dynamic_index_in_dim(pack, z, 0, False).astype(F32)
        for k in range(1, 4):
            sent = lax.dynamic_index_in_dim(pack, (z + k) % 4, 0, False)
            total = total + shifted(sent, "z", k).astype(F32)
        shares[l] = total.astype(BF)
        dx, branch_sent = call(
            functools.partial(finish_back_kernel, l == 2),
            [((ROWS, D), F32), ((8, ROWS, D), BF)], got, x, dx,
        )
        if l > 0:
            branches = from_chips(branch_sent)

    def spread(j):
        mine = jnp.where(first, shares[j], shares[j + 2])
        theirs = shifted(jnp.where(first, shares[j + 2], shares[j]), "s", 1)
        part = (mine.astype(F32) + theirs.astype(F32)).astype(BF)
        sent = jnp.broadcast_to(part[None], (8, PACK, 384))
        own = lax.all_to_all(sent, CHIPS, 0, 0, tiled=True)
        return own, shifted(own, "c", 1)

    second, initial = spread(1), spread(0)
    grad_qkv, grad_out, grad_up, grad_down, extra = call(
        unpack_kernel,
        [((2, 192, 3 * D), F32), ((2, 192, D), F32), ((2, 192, FF), F32), ((2, D, D), F32), ((2, 16, 16, 384), F32)],
        jnp.stack([c, z]).astype(jnp.int32), *initial, *second, smem=1,
    )
    norm_sums = jnp.sum(extra[:, :, 0:2], 1)
    v_g1, v_h1 = norm_sums[:, 0, :192], norm_sums[:, 0, 192:]
    v_g2, v_h2 = norm_sums[:, 1, :192], norm_sums[:, 1, 192:]
    v_qkv = extra[:, :H, 2, :192].reshape(2, H, 3, HD).transpose(0, 2, 1, 3).reshape(2, 3 * D)
    v_qkv = lax.dynamic_slice_in_dim(v_qkv, z * 576, 576, 1)
    v_up = extra[:, :, 2, 192:].reshape(2, 16, 4, 48).transpose(0, 2, 1, 3).reshape(2, 4, D)
    v_up = lax.dynamic_index_in_dim(v_up, z, 1, False)
    v_branch = extra[:, 0, 3, :192]

    came = shifted(jnp.where(first, final, dx), "s", 1)
    have = jnp.where(first, dx, final)
    boundary = jnp.stack([jnp.where(first, have, came), jnp.where(first, came, have)])
    boundary = boundary.reshape(1, 2, 1, ROWS, D)
    return (
        boundary, v_g1, v_h1, v_g2, v_h2, grad_qkv, v_qkv, grad_out, v_branch,
        grad_up, v_up, grad_down, v_branch,
    )


def solution(mesh):
    wide = Mesh(mesh.devices.reshape(2, 2, 4, 2, 4), EVERY)
    acts = P("s", None, "z", CTX, None)
    vec = P("s", "z")
    mat = P("s", "z", None)
    placed = (acts, P(), vec, vec, vec, vec, mat, vec, mat, vec, mat, vec, mat, vec)
    outs = (acts, vec, vec, vec, vec, mat, vec, mat, vec, mat, vec, mat, vec)
    return jax.shard_map(body, mesh=wide, in_specs=placed, out_specs=outs, check_vma=False)
```

time: 1830 us -> 702 us (0.38)
  waiting for transfers between devices: 971 us -> 201 us
  matrix products: 294 us -> 0 us
  Pallas kernels: 0 us -> 156 us
  other arithmetic: 194 us -> 39 us
  local copies, waits for them, and re-layouts: 180 us -> 79.8 us
  starting transfers between devices: 69.6 us -> 111 us
  blocking collectives: 84.6 us -> 108 us
  between operations: 22.5 us -> 1.9 us
    all_gather x14 -> x0, waiting for transfers between devices: 543 us -> none  [the longest x8 285 us: in_one_piece(): lax.all_gather(both, axis, axis=dim, tiled=True)]
    reduce_scatter x6 -> x0, waiting for transfers between devices: 310 us -> none  [in_one_piece_2(): lax.psum_scatter(both, axis, scatter_dimension=dim, tiled=True)]
    dot_general x98 -> x0, matrix products: 294 us -> none  [the longest x24 105 us: by_cols(): lax.dot_general(left_side, right_side, (((1,), (1,)), ((), ())), preferre...]
    pallas_call x0 -> x22, Pallas kernels: none -> 156 us  [call(): pl.pallas_call(kernel, out_shape=[jax.ShapeDtypeStruct(shape, dtype) for...]
    all_to_all x0 -> x6, blocking collectives: none -> 108 us  [the longest x4 71.4 us: from_chips(): own = lax.all_to_all(sent, CHIPS, 0, 0, tiled=True)]
    ppermute x4 -> x46, waiting for transfers between devices: 10.1 us -> 93.7 us  [shifted(): lax.ppermute(block, axis, [(i, (i + distance) % size) for i in range(size)])]
    concatenate x44 -> x7, other arithmetic: 75.2 us -> 3.83 us  [the longest x2 2.33 us: body(): jnp.concatenate([jnp.concatenate(head, 1), jnp.concatenate(units, 1), jnp...]
    psum x1 -> x0, blocking collectives: 65.1 us -> none  [body(): lax.psum(layer_shard[0].astype(jnp.bfloat16), 'ctx').astype(jnp.float32)]
  transfers between devices with their start and end apart: 41 -> 58, of which waited for: 38 -> 25; matrix products, arithmetic and copies ran while one was open for 21% -> 12% of each run, Pallas kernels for 0% -> 9%
where the time goes in v1:
time: 702 us; the launch traced here: 696 us
  waiting for transfers between devices  201 us (29%)
  Pallas kernels  156 us (22%)
  starting transfers between devices  111 us (16%)
  blocking collectives  108 us (15%)
  local copies, waits for them, and re-layouts  79.8 us (11%)
  other arithmetic  39 us (6%)
    pallas_call x22, Pallas kernels, call(): pl.pallas_call(kernel, out_shape=[jax.ShapeDtypeStruct(shape, dtype) for...  156 us
    ppermute x46, waiting for transfers between devices, shifted(): lax.ppermute(block, axis, [(i, (i + distance) % size) for i in range(size)])  93.7 us
    all_to_all x4, blocking collectives, from_chips(): own = lax.all_to_all(sent, CHIPS, 0, 0, tiled=True)  71.4 us
    all_to_all x6, waiting for transfers between devices, to_chips(): return lax.all_to_all(part.reshape(8, ROWS, D), CHIPS, 0, 0, tiled=True)  55.9 us
    ppermute x46, starting transfers between devices, shifted(): lax.ppermute(block, axis, [(i, (i + distance) % size) for i in range(size)])  38.9 us
    all_to_all x6, starting transfers between devices, to_chips(): return lax.all_to_all(part.reshape(8, ROWS, D), CHIPS, 0, 0, tiled=True)  36.9 us
    all_to_all x2, blocking collectives, to_chips(): return lax.all_to_all(part.reshape(8, ROWS, D), CHIPS, 0, 0, tiled=True)  36.2 us
    all_to_all x2, waiting for transfers between devices, spread(): own = lax.all_to_all(sent, CHIPS, 0, 0, tiled=True)  31.3 us
  transfers between devices with their start and end apart: 58, of which 25 were waited for; matrix products, arithmetic and copies ran while one was open for 12% of the time, Pallas kernels for 9%

profile of v1, /device:TPU:0, one launch (start us, length us, event | category | flops | bytes accessed | tf_op | source)
XLA Modules:
  0.0 695.8 jit_solution(14943082753081852755)
XLA Ops:
  7.1 2.9 fusion.32
  26.2 3.6 collective-permute-start.5
  50.1 6.6 all-to-all-start.1
  60.6 8.1 %all-to-all-done.1 = bf16[8,64,768]{2,1,0:T(8,128)(2,1)S(1)} async-done(((bf16[8,64,768]{2,1,0:T(8,128)(2,1)}), bf16[8,64,768]{2,1,0:T(8,128)(2,1)S(1)}, u32[]{:S(2)}, u32[]{:S(2)}) %all-to-all-start.1) | async-done | bytes 786464 | tf_op jit(solution)/shard_map/all_to_all | solution.py:297
  76.3 7.6 %collective-permute-done.10 = bf16[416,384]{1,0:T(8,128)(2,1)S(1)} collective-permute-done((bf16[416,384]{1,0:T(8,128)(2,1)}, bf16[416,384]{1,0:T(8,128)(2,1)S(1)}, u32[]{:S(2)}, u32[]{:S(2)}) %collective-permute-start.10) | collective-permute-done | bytes 319520 | tf_op jit(solution)/shard_map/ppermute | solution.py:36
  85.3 11.1 %shard_map.238 = (bf16[512,768]{1,0:T(8,128)(2,1)}, bf16[512,768]{1,0:T(8,128)(2,1)}, bf16[1024,192]{1,0:T(8,128)(2,1)}, f32[1024,192]{1,0:T(8,128)}, bf16[1024,256]{1,0:T(8,128)(2,1)}) custom-call(s32[1]{0:T(128)} %bitcast.owner, bf16[512,768]{1,0:T(8,128)(2,1)} %bitcast.255, bf16[512,768]{1,0:T(8,128)(2,1)} %bitcast.275, f32[8,768]{1,0:T(8,128)} %concatenate.83.vec, ...), custom_call_target="tpu_custom_call" | custom-call | tf_op jit(solution)/shard_map/pallas_call | solution.py:48
  97.0 9.6 %collective-permute-done.13 = bf16[416,384]{1,0:T(8,128)(2,1)S(1)} collective-permute-done((bf16[416,384]{1,0:T(8,128)(2,1)S(1)}, bf16[416,384]{1,0:T(8,128)(2,1)S(1)}, u32[]{:S(2)}, u32[]{:S(2)}) %collective-permute-start.13) | collective-permute-done | bytes 319520 | tf_op jit(solution)/shard_map/ppermute | solution.py:36
  107.7 3.5 all-to-all-start.2
  116.1 8.7 %all-to-all-done.2.got = bf16[8,64,768]{2,1,0:T(8,128)(2,1)S(1)} async-done(((bf16[8,64,768]{2,1,0:T(8,128)(2,1)}), bf16[8,64,768]{2,1,0:T(8,128)(2,1)S(1)}, u32[]{:S(2)}, u32[]{:S(2)}) %all-to-all-start.2) | async-done | bytes 786464 | tf_op jit(solution)/shard_map/all_to_all | solution.py:302
  125.6 2.4 shard_map.239
  128.1 3.7 all-to-all-start.3
  138.4 17.9 %collective-permute-done.14 = bf16[3,416,384]{2,1,0:T(8,128)(2,1)} collective-permute-done((bf16[3,416,384]{2,1,0:T(8,128)(2,1)S(1)}, bf16[3,416,384]{2,1,0:T(8,128)(2,1)}, u32[]{:S(2)}, u32[]{:S(2)}) %collective-permute-start.14) | collective-permute-done | bytes 958496 | tf_op jit(solution)/shard_map/ppermute | solution.py:36
  158.5 2.5 bitcast_dynamic-update-slice_fusion.1
  163.2 4.1 slice_bitcast_fusion
  168.2 11.0 %shard_map.240 = (bf16[512,768]{1,0:T(8,128)(2,1)}, bf16[512,768]{1,0:T(8,128)(2,1)}, bf16[1024,192]{1,0:T(8,128)(2,1)}, f32[1024,192]{1,0:T(8,128)}, bf16[1024,256]{1,0:T(8,128)(2,1)}) custom-call(s32[1]{0:T(128)} %bitcast.owner, bf16[512,768]{1,0:T(8,128)(2,1)} %bitcast.258, bf16[512,768]{1,0:T(8,128)(2,1)} %bitcast.281, f32[8,768]{1,0:T(8,128)} %concatenate.93.vec, ...), custom_call_target="tpu_custom_call" | custom-call | tf_op jit(solution)/shard_map/pallas_call | solution.py:48
  184.0 17.1 %all-to-all-start.4 = ((bf16[8,64,768]{2,1,0:T(8,128)(2,1)}), bf16[8,64,768]{2,1,0:T(8,128)(2,1)S(1)}, u32[]{:S(2)}, u32[]{:S(2)}) async-start(bf16[8,64,768]{2,1,0:T(8,128)(2,1)} %bitcast.49), calls=%async_computation.4 | async-start | bytes 1572864 | tf_op jit(solution)/shard_map/all_to_all | solution.py:302
  201.8 13.0 %all-to-all-done.4.got = bf16[8,64,768]{2,1,0:T(8,128)(2,1)S(1)} async-done(((bf16[8,64,768]{2,1,0:T(8,128)(2,1)}), bf16[8,64,768]{2,1,0:T(8,128)(2,1)S(1)}, u32[]{:S(2)}, u32[]{:S(2)}) %all-to-all-start.4) | async-done | bytes 786464 | tf_op jit(solution)/shard_map/all_to_all | solution.py:302
  215.7 2.4 shard_map.241
  218.1 18.2 %all_to_all.90 = bf16[8,64,768]{2,1,0:T(8,128)(2,1)S(1)} all-to-all(bf16[8,64,768]{2,1,0:T(8,128)(2,1)} %get-tuple-element.78), channel_id=1, replica_groups=mesh['s'=2,'xh'=2,'y'=4,'c'=2,'z'=4] {'xh','y'}, dimensions={0} | all-to-all | bytes 1572864 | tf_op jit(solution)/shard_map/all_to_all | solution.py:297
  239.6 11.0 %shard_map.242 = (bf16[512,768]{1,0:T(8,128)(2,1)}, bf16[512,768]{1,0:T(8,128)(2,1)}, bf16[1024,192]{1,0:T(8,128)(2,1)}, f32[1024,192]{1,0:T(8,128)}, bf16[1024,256]{1,0:T(8,128)(2,1)}) custom-call(s32[1]{0:T(128)} %bitcast.owner, bf16[512,768]{1,0:T(8,128)(2,1)} %bitcast.261, bf16[512,768]{1,0:T(8,128)(2,1)} %bitcast.278, f32[8,768]{1,0:T(8,128)} %concatenate.100.vec, ...), custom_call_target="tpu_custom_call" | custom-call | tf_op jit(solution)/shard_map/pallas_call | solution.py:48
  255.3 3.5 all-to-all-start.6
  259.5 13.0 %all-to-all-done.6.got = bf16[8,64,768]{2,1,0:T(8,128)(2,1)S(1)} async-done(((bf16[8,64,768]{2,1,0:T(8,128)(2,1)}), bf16[8,64,768]{2,1,0:T(8,128)(2,1)S(1)}, u32[]{:S(2)}, u32[]{:S(2)}) %all-to-all-start.6) | async-done | bytes 786464 | tf_op jit(solution)/shard_map/all_to_all | solution.py:302
  273.4 2.4 shard_map.243
  275.8 18.5 %all_to_all.91 = bf16[8,64,768]{2,1,0:T(8,128)(2,1)S(1)} all-to-all(bf16[8,64,768]{2,1,0:T(8,128)(2,1)} %get-tuple-element.82), channel_id=1, replica_groups=mesh['s'=2,'xh'=2,'y'=4,'c'=2,'z'=4] {'xh','y'}, dimensions={0} | all-to-all | bytes 1572864 | tf_op jit(solution)/shard_map/all_to_all | solution.py:297
  295.3 3.5 all-to-all-start
  298.9 12.0 %all-to-all-done = bf16[8,64,768]{2,1,0:T(8,128)(2,1)S(1)} async-done(((bf16[8,64,768]{2,1,0:T(8,128)(2,1)}), bf16[8,64,768]{2,1,0:T(8,128)(2,1)S(1)}, u32[]{:S(2)}, u32[]{:S(2)}) %all-to-all-start) | async-done | bytes 786464 | tf_op jit(solution)/shard_map/all_to_all | solution.py:297
  312.8 11.0 %shard_map.244 = (bf16[512,768]{1,0:T(8,128)(2,1)}, bf16[512,768]{1,0:T(8,128)(2,1)}, bf16[1024,192]{1,0:T(8,128)(2,1)}, f32[1024,192]{1,0:T(8,128)}, bf16[1024,256]{1,0:T(8,128)(2,1)}) custom-call(s32[1]{0:T(128)} %bitcast.owner, bf16[512,768]{1,0:T(8,128)(2,1)} %bitcast.264, bf16[512,768]{1,0:T(8,128)(2,1)} %bitcast.284, f32[8,768]{1,0:T(8,128)} %concatenate.104.vec, ...), custom_call_target="tpu_custom_call" | custom-call | tf_op jit(solution)/shard_map/pallas_call | solution.py:48
  324.8 13.3 %shard_map.245 = (bf16[512,768]{1,0:T(8,128)(2,1)}, bf16[512,768]{1,0:T(8,128)(2,1)}, bf16[1024,192]{1,0:T(8,128)(2,1)}, bf16[1024,192]{1,0:T(8,128)(2,1)}, f32[8,768]{1,0:T(8,128)}) custom-call(s32[1]{0:T(128)} %bitcast.owner, bf16[512,768]{1,0:T(8,128)(2,1)} %bitcast.269, bf16[512,768]{1,0:T(8,128)(2,1)} %bitcast.289, bf16[512,768]{1,0:T(8,128)(2,1)} %bitcast.265, ...), custom_call_target="tpu_custom_call" | custom-call | tf_op jit(solution)/shard_map/pallas_call | solution.py:48
  342.0 18.2 %all_to_all.92.got = bf16[8,64,768]{2,1,0:T(8,128)(2,1)} all-to-all(bf16[8,64,768]{2,1,0:T(8,128)(2,1)S(1)} %bitcast.297), channel_id=1, replica_groups=mesh['s'=2,'xh'=2,'y'=4,'c'=2,'z'=4] {'xh','y'}, dimensions={0} | all-to-all | bytes 1572864 | tf_op jit(solution)/shard_map/all_to_all | solution.py:302
  360.2 2.5 shard_map.246
  362.7 17.3 %all_to_all.93 = bf16[8,64,768]{2,1,0:T(8,128)(2,1)S(1)} all-to-all(bf16[8,64,768]{2,1,0:T(8,128)(2,1)} %get-tuple-element.88), channel_id=1, replica_groups=mesh['s'=2,'xh'=2,'y'=4,'c'=2,'z'=4] {'xh','y'}, dimensions={0} | all-to-all | bytes 1572864 | tf_op jit(solution)/shard_map/all_to_all | solution.py:297
  383.4 13.2 %shard_map.247 = (bf16[512,768]{1,0:T(8,128)(2,1)}, bf16[512,768]{1,0:T(8,128)(2,1)}, bf16[1024,192]{1,0:T(8,128)(2,1)}, bf16[1024,192]{1,0:T(8,128)(2,1)}, f32[8,768]{1,0:T(8,128)}) custom-call(s32[1]{0:T(128)} %bitcast.owner, bf16[512,768]{1,0:T(8,128)(2,1)} %bitcast.267, bf16[512,768]{1,0:T(8,128)(2,1)} %bitcast.287, bf16[512,768]{1,0:T(8,128)(2,1)} %bitcast.262, ...), custom_call_target="tpu_custom_call" | custom-call | tf_op jit(solution)/shard_map/pallas_call | solution.py:48
  396.8 2.4 collective-permute-done.23
  400.4 17.9 %all_to_all.94.got = bf16[8,64,768]{2,1,0:T(8,128)(2,1)} all-to-all(bf16[8,64,768]{2,1,0:T(8,128)(2,1)S(1)} %bitcast.298), channel_id=1, replica_groups=mesh['s'=2,'xh'=2,'y'=4,'c'=2,'z'=4] {'xh','y'}, dimensions={0} | all-to-all | bytes 1572864 | tf_op jit(solution)/shard_map/all_to_all | solution.py:302
  418.4 2.5 shard_map.248
  420.9 17.4 %all_to_all.95 = bf16[8,64,768]{2,1,0:T(8,128)(2,1)S(1)} all-to-all(bf16[8,64,768]{2,1,0:T(8,128)(2,1)} %get-tuple-element.94), channel_id=1, replica_groups=mesh['s'=2,'xh'=2,'y'=4,'c'=2,'z'=4] {'xh','y'}, dimensions={0} | all-to-all | bytes 1572864 | tf_op jit(solution)/shard_map/all_to_all | solution.py:297
  441.5 13.2 %shard_map.249 = (bf16[512,768]{1,0:T(8,128)(2,1)}, bf16[512,768]{1,0:T(8,128)(2,1)}, bf16[1024,192]{1,0:T(8,128)(2,1)}, bf16[1024,192]{1,0:T(8,128)(2,1)}, f32[8,768]{1,0:T(8,128)}) custom-call(s32[1]{0:T(128)} %bitcast.owner, bf16[512,768]{1,0:T(8,128)(2,1)} %bitcast.271, bf16[512,768]{1,0:T(8,128)(2,1)} %bitcast.291, bf16[512,768]{1,0:T(8,128)(2,1)} %bitcast.259, ...), custom_call_target="tpu_custom_call" | custom-call | tf_op jit(solution)/shard_map/pallas_call | solution.py:48
  455.2 6.1 shard_map.257
  462.4 3.7 all-to-all-start.12
  469.1 6.1 shard_map.256
  477.3 2.7 collective-permute-start.40
  483.8 2.5 shard_map.250
  486.3 7.1 %all-to-all-start.13 = ((bf16[8,64,768]{2,1,0:T(8,128)(2,1)}), bf16[8,64,768]{2,1,0:T(8,128)(2,1)S(1)}, u32[]{:S(2)}, u32[]{:S(2)}) async-start(bf16[8,64,768]{2,1,0:T(8,128)(2,1)} %get-tuple-element.100), calls=%async_computation.13 | async-start | bytes 1572864 | tf_op jit(solution)/shard_map/all_to_all | solution.py:297
  493.8 6.5 collective-permute-done.38
  503.2 8.8 %collective-permute-done.44 = bf16[432,384]{1,0:T(8,128)(2,1)S(1)} collective-permute-done((bf16[432,384]{1,0:T(8,128)(2,1)S(1)}, bf16[432,384]{1,0:T(8,128)(2,1)S(1)}, u32[]{:S(2)}, u32[]{:S(2)}) %collective-permute-start.44) | collective-permute-done | bytes 331808 | tf_op jit(solution)/shard_map/ppermute | solution.py:36
  513.9 6.8 all-to-all-start.17
  520.8 6.1 shard_map.255
  531.3 13.3 %shard_map.251 = (bf16[512,768]{1,0:T(8,128)(2,1)}, bf16[512,768]{1,0:T(8,128)(2,1)}, bf16[1024,192]{1,0:T(8,128)(2,1)}, bf16[1024,192]{1,0:T(8,128)(2,1)}, f32[8,768]{1,0:T(8,128)}) custom-call(s32[1]{0:T(128)} %bitcast.owner, bf16[512,768]{1,0:T(8,128)(2,1)} %bitcast.273, bf16[512,768]{1,0:T(8,128)(2,1)} %bitcast.293, bf16[512,768]{1,0:T(8,128)(2,1)} %bitcast.256, ...), custom_call_target="tpu_custom_call" | custom-call | tf_op jit(solution)/shard_map/pallas_call | solution.py:48
  544.6 6.1 shard_map.254
  551.9 2.8 collective-permute-start.32
  557.5 11.4 %collective-permute-done.32 = bf16[432,384]{1,0:T(8,128)(2,1)S(1)} collective-permute-done((bf16[432,384]{1,0:T(8,128)(2,1)S(1)}, bf16[432,384]{1,0:T(8,128)(2,1)S(1)}, u32[]{:S(2)}, u32[]{:S(2)}) %collective-permute-start.32) | collective-permute-done | bytes 331808 | tf_op jit(solution)/shard_map/ppermute | solution.py:36
  568.9 3.7 collective-permute-done.30
  575.1 8.8 %collective-permute-done.36 = bf16[432,384]{1,0:T(8,128)(2,1)S(1)} collective-permute-done((bf16[432,384]{1,0:T(8,128)(2,1)S(1)}, bf16[432,384]{1,0:T(8,128)(2,1)S(1)}, u32[]{:S(2)}, u32[]{:S(2)}) %collective-permute-start.36) | collective-permute-done | bytes 331808 | tf_op jit(solution)/shard_map/ppermute | solution.py:36
  585.9 7.3 %all-to-all-start.16 = ((bf16[8,432,384]{2,1,0:T(8,128)(2,1)}), bf16[8,432,384]{2,1,0:T(8,128)(2,1)}, u32[]{:S(2)}, u32[]{:S(2)}) async-start(bf16[8,432,384]{2,1,0:T(8,128)(2,1)} %broadcast_in_dim.93), calls=%async_computation.16 | async-start | bytes 5308416 | tf_op jit(solution)/shard_map/all_to_all | solution.py:422
  593.7 31.3 %all-to-all-done.16.own_a = bf16[8,432,384]{2,1,0:T(8,128)(2,1)} async-done(((bf16[8,432,384]{2,1,0:T(8,128)(2,1)}), bf16[8,432,384]{2,1,0:T(8,128)(2,1)}, u32[]{:S(2)}, u32[]{:S(2)}) %all-to-all-start.16) | async-done | bytes 2654240 | tf_op jit(solution)/shard_map/all_to_all | solution.py:422
  627.7 4.8 all-to-all-start.15
  632.5 2.4 add.366
  634.9 11.1 %all-to-all-done.15.got = bf16[8,64,768]{2,1,0:T(8,128)(2,1)S(1)} async-done(((bf16[8,64,768]{2,1,0:T(8,128)(2,1)}), bf16[8,64,768]{2,1,0:T(8,128)(2,1)S(1)}, u32[]{:S(2)}, u32[]{:S(2)}) %all-to-all-start.15) | async-done | bytes 786464 | tf_op jit(solution)/shard_map/all_to_all | solution.py:302
  646.0 4.2 all-to-all-start.14
  650.9 2.4 shard_map.253
  653.3 10.1 %all-to-all-done.14.got = bf16[8,64,768]{2,1,0:T(8,128)(2,1)} async-done(((bf16[8,64,768]{2,1,0:T(8,128)(2,1)}), bf16[8,64,768]{2,1,0:T(8,128)(2,1)}, u32[]{:S(2)}, u32[]{:S(2)}) %all-to-all-start.14) | async-done | bytes 786464 | tf_op jit(solution)/shard_map/all_to_all | solution.py:302
  663.5 2.5 shard_map.252
  668.8 4.1 collective-permute-done.29
  674.7 12.4 %shard_map.258 = (f32[2,192,2304]{2,1,0:T(8,128)}, f32[2,192,768]{2,1,0:T(8,128)}, f32[2,192,3072]{2,1,0:T(8,128)}, f32[2,768,768]{2,1,0:T(8,128)}, f32[2,16,16,384]{3,2,1,0:T(8,128)}) custom-call(s32[2]{0:T(128)} %pad_add_fusion.place, bf16[8,432,384]{2,1,0:T(8,128)(2,1)} %all-to-all-done.16.own_a, bf16[8,432,384]{2,1,0:T(8,128)(2,1)} %collective-permute-done.37.other_a, ...), custom_call_target="tpu_custom_call" | custom-call | tf_op jit(solution)/shard_map/pallas_call | solution.py:48
  (345 shorter events, 151.8 us)
Async XLA Ops:
  2.2 44.1 %collective-permute-start = (bf16[64,768]{1,0:T(8,128)(2,1)}, bf16[64,768]{1,0:T(8,128)(2,1)}, u32[]{:S(2)}, u32[]{:S(2)}) collective-permute-start(bf16[64,768]{1,0:T(8,128)(2,1)} %select_bitcast_fusion.5), channel_id=1, source_target_pairs={{0,64},{64,0},{1,65},{65,1},{2,66},{66,2},{3,67},{67,3},{4,68},{68... | collective-permute-start | bytes 294920 | tf_op jit(solution)/shard_map/ppermute | solution.py:36
  4.7 18.2 %collective-permute-start.3 = (bf16[2,2496]{1,0:T(2,128)(2,1)S(1)}, bf16[2,2496]{1,0:T(2,128)(2,1)}, u32[]{:S(2)}, u32[]{:S(2)}) collective-permute-start(bf16[2,2496]{1,0:T(2,128)(2,1)S(1)} %concatenate.81), channel_id=1, source_target_pairs={{0,64},{64,0},{1,65},{65,1},{2,66},{66,2},{3,67},{67,3},{4,68},{68... | collective-permute-start | bytes 29960 | tf_op jit(solution)/shard_map/ppermute | solution.py:36
  15.7 41.8 %collective-permute-start.7 = (bf16[416,384]{1,0:T(8,128)(2,1)S(1)}, bf16[416,384]{1,0:T(8,128)(2,1)S(1)}, u32[]{:S(2)}, u32[]{:S(2)}) collective-permute-start(bf16[416,384]{1,0:T(8,128)(2,1)S(1)} %fusion.13), channel_id=1, source_target_pairs={{0,64},{64,0},{1,65},{65,1},{2,66},{66,2},{3,67},{67,3},{4,68},{68... | collective-permute-start | bytes 958472 | tf_op jit(solution)/shard_map/ppermute | solution.py:36
  24.3 17.1 %collective-permute-start.4 = (bf16[4,2496]{1,0:T(4,128)(2,1)}, bf16[4,2496]{1,0:T(4,128)(2,1)}, u32[]{:S(2)}, u32[]{:S(2)}) collective-permute-start(bf16[4,2496]{1,0:T(4,128)(2,1)} %get-tuple-element.265), channel_id=1, source_target_pairs={{0,1},{1,2},{2,3},{3,0},{4,5},{5,6},{6,7},{7,4},{8,9},{9,10},{10,1... | collective-permute-start | bytes 59912 | tf_op jit(solution)/shard_map/ppermute | solution.py:36
  26.2 16.0 %collective-permute-start.5 = (bf16[4,2496]{1,0:T(4,128)(2,1)}, bf16[4,2496]{1,0:T(4,128)(2,1)}, u32[]{:S(2)}, u32[]{:S(2)}) collective-permute-start(bf16[4,2496]{1,0:T(4,128)(2,1)} %get-tuple-element.265), channel_id=1, source_target_pairs={{0,2},{1,3},{2,0},{3,1},{4,6},{5,7},{6,4},{7,5},{8,10},{9,11},{10,... | collective-permute-start | bytes 59912 | tf_op jit(solution)/shard_map/ppermute | solution.py:36
  29.8 13.2 %collective-permute-start.6 = (bf16[4,2496]{1,0:T(4,128)(2,1)}, bf16[4,2496]{1,0:T(4,128)(2,1)}, u32[]{:S(2)}, u32[]{:S(2)}) collective-permute-start(bf16[4,2496]{1,0:T(4,128)(2,1)} %get-tuple-element.265), channel_id=1, source_target_pairs={{0,3},{1,0},{2,1},{3,2},{4,7},{5,4},{6,5},{7,6},{8,11},{9,8},{10,9... | collective-permute-start | bytes 59912 | tf_op jit(solution)/shard_map/ppermute | solution.py:36
  50.1 18.6 %all-to-all-start.1 = ((bf16[8,64,768]{2,1,0:T(8,128)(2,1)}), bf16[8,64,768]{2,1,0:T(8,128)(2,1)S(1)}, u32[]{:S(2)}, u32[]{:S(2)}) async-start(bf16[8,64,768]{2,1,0:T(8,128)(2,1)} %shard_map.237), calls=%async_computation.1 | async-start | bytes 1572864 | tf_op jit(solution)/shard_map/all_to_all | solution.py:297
  58.5 15.8 %collective-permute-start.8 = (bf16[416,384]{1,0:T(8,128)(2,1)}, bf16[416,384]{1,0:T(8,128)(2,1)}, u32[]{:S(2)}, u32[]{:S(2)}) collective-permute-start(bf16[416,384]{1,0:T(8,128)(2,1)} %get-tuple-element.194), channel_id=1, source_target_pairs={{0,1},{1,2},{2,3},{3,0},{4,5},{5,6},{6,7},{7,4},{8,9},{9,10},{10,1... | collective-permute-start | bytes 958472 | tf_op jit(solution)/shard_map/ppermute | solution.py:36
  60.1 15.1 %collective-permute-start.9 = (bf16[416,384]{1,0:T(8,128)(2,1)}, bf16[416,384]{1,0:T(8,128)(2,1)}, u32[]{:S(2)}, u32[]{:S(2)}) collective-permute-start(bf16[416,384]{1,0:T(8,128)(2,1)} %get-tuple-element.194), channel_id=1, source_target_pairs={{0,2},{1,3},{2,0},{3,1},{4,6},{5,7},{6,4},{7,5},{8,10},{9,11},{10,... | collective-permute-start | bytes 958472 | tf_op jit(solution)/shard_map/ppermute | solution.py:36
  68.7 15.3 %collective-permute-start.2 = (bf16[8,64,768]{2,1,0:T(8,128)(2,1)S(1)}, bf16[8,64,768]{2,1,0:T(8,128)(2,1)S(1)}, u32[]{:S(2)}, u32[]{:S(2)}) collective-permute-start(bf16[8,64,768]{2,1,0:T(8,128)(2,1)S(1)} %all-to-all-done.1), channel_id=1, source_target_pairs={{0,4},{4,0},{1,5},{5,1},{2,6},{6,2},{3,7},{7,3},{8,12},{12,8},{9,1... | collective-permute-start | bytes 2359304 | tf_op jit(solution)/shard_map/ppermute | solution.py:36
  73.7 10.2 %collective-permute-start.10 = (bf16[416,384]{1,0:T(8,128)(2,1)}, bf16[416,384]{1,0:T(8,128)(2,1)S(1)}, u32[]{:S(2)}, u32[]{:S(2)}) collective-permute-start(bf16[416,384]{1,0:T(8,128)(2,1)} %get-tuple-element.194), channel_id=1, source_target_pairs={{0,3},{1,0},{2,1},{3,2},{4,7},{5,4},{6,5},{7,6},{8,11},{9,8},{10,9... | collective-permute-start | bytes 958472 | tf_op jit(solution)/shard_map/ppermute | solution.py:36
  96.5 10.2 %collective-permute-start.11 = (bf16[512,768]{1,0:T(8,128)(2,1)}, bf16[512,768]{1,0:T(8,128)(2,1)S(1)}, u32[]{:S(2)}, u32[]{:S(2)}) collective-permute-start(bf16[512,768]{1,0:T(8,128)(2,1)} %get-tuple-element.73), channel_id=1, source_target_pairs={{0,4},{4,0},{1,5},{5,1},{2,6},{6,2},{3,7},{7,3},{8,12},{12,8},{9,1... | collective-permute-start | bytes 2359304 | tf_op jit(solution)/shard_map/ppermute | solution.py:36
  96.6 10.0 %collective-permute-start.13 = (bf16[416,384]{1,0:T(8,128)(2,1)S(1)}, bf16[416,384]{1,0:T(8,128)(2,1)S(1)}, u32[]{:S(2)}, u32[]{:S(2)}) collective-permute-start(bf16[416,384]{1,0:T(8,128)(2,1)S(1)} %fusion.12), channel_id=1, source_target_pairs={{0,64},{64,0},{1,65},{65,1},{2,66},{66,2},{3,67},{67,3},{4,68},{68... | collective-permute-start | bytes 958472 | tf_op jit(solution)/shard_map/ppermute | solution.py:36
  107.7 17.0 %all-to-all-start.2 = ((bf16[8,64,768]{2,1,0:T(8,128)(2,1)}), bf16[8,64,768]{2,1,0:T(8,128)(2,1)S(1)}, u32[]{:S(2)}, u32[]{:S(2)}) async-start(bf16[8,64,768]{2,1,0:T(8,128)(2,1)} %bitcast.25), calls=%async_computation.2 | async-start | bytes 1572864 | tf_op jit(solution)/shard_map/all_to_all | solution.py:302
  111.5 44.8 %collective-permute-start.14 = (bf16[3,416,384]{2,1,0:T(8,128)(2,1)S(1)}, bf16[3,416,384]{2,1,0:T(8,128)(2,1)}, u32[]{:S(2)}, u32[]{:S(2)}) collective-permute-start(bf16[3,416,384]{2,1,0:T(8,128)(2,1)S(1)} %pad_maximum_fusion), channel_id=1, source_target_pairs={{0,1},{1,2},{2,3},{3,0},{4,5},{5,6},{6,7},{7,4},{8,9},{9,10},{10,1... | collective-permute-start | bytes 2875400 | tf_op jit(solution)/shard_map/ppermute | solution.py:36
  112.6 45.9 %collective-permute-start.15 = (bf16[3,416,384]{2,1,0:T(8,128)(2,1)S(1)}, bf16[3,416,384]{2,1,0:T(8,128)(2,1)}, u32[]{:S(2)}, u32[]{:S(2)}) collective-permute-start(bf16[3,416,384]{2,1,0:T(8,128)(2,1)S(1)} %pad_maximum_fusion), channel_id=1, source_target_pairs={{0,2},{1,3},{2,0},{3,1},{4,6},{5,7},{6,4},{7,5},{8,10},{9,11},{10,... | collective-permute-start | bytes 2875400 | tf_op jit(solution)/shard_map/ppermute | solution.py:36
  116.0 18.3 %copy-start.44 = (f32[1,48]{1,0:T(1,128)S(1)}, f32[1,48]{1,0:T(1,128)}, u32[]{:S(2)}) copy-start(f32[1,48]{1,0:T(1,128)} %get-tuple-element.272) | copy-start | bytes 580
  116.0 18.3 %copy-start.45 = (f32[1,48]{1,0:T(1,128)S(1)}, f32[1,48]{1,0:T(1,128)}, u32[]{:S(2)}) copy-start(f32[1,48]{1,0:T(1,128)} %get-tuple-element.277) | copy-start | bytes 580
  116.0 18.3 %copy-start.46 = (f32[1,48]{1,0:T(1,128)S(1)}, f32[1,48]{1,0:T(1,128)}, u32[]{:S(2)}) copy-start(f32[1,48]{1,0:T(1,128)} %get-tuple-element.278) | copy-start | bytes 580
  128.1 30.4 %all-to-all-start.3 = ((bf16[8,64,768]{2,1,0:T(8,128)(2,1)}), bf16[8,64,768]{2,1,0:T(8,128)(2,1)S(1)}, u32[]{:S(2)}, u32[]{:S(2)}) async-start(bf16[8,64,768]{2,1,0:T(8,128)(2,1)} %get-tuple-element.74), calls=%async_computation.3 | async-start | bytes 1572864 | tf_op jit(solution)/shard_map/all_to_all | solution.py:297
  131.8 29.2 %collective-permute-start.16 = (bf16[3,416,384]{2,1,0:T(8,128)(2,1)S(1)}, bf16[3,416,384]{2,1,0:T(8,128)(2,1)}, u32[]{:S(2)}, u32[]{:S(2)}) collective-permute-start(bf16[3,416,384]{2,1,0:T(8,128)(2,1)S(1)} %pad_maximum_fusion), channel_id=1, source_target_pairs={{0,3},{1,0},{2,1},{3,2},{4,7},{5,4},{6,5},{7,6},{8,11},{9,8},{10,9... | collective-permute-start | bytes 2875400 | tf_op jit(solution)/shard_map/ppermute | solution.py:36
  158.5 8.9 %collective-permute-start.12 = (bf16[8,64,768]{2,1,0:T(8,128)(2,1)S(1)}, bf16[8,64,768]{2,1,0:T(8,128)(2,1)S(1)}, u32[]{:S(2)}, u32[]{:S(2)}) collective-permute-start(bf16[8,64,768]{2,1,0:T(8,128)(2,1)S(1)} %all-to-all-done.3), channel_id=1, source_target_pairs={{0,4},{4,0},{1,5},{5,1},{2,6},{6,2},{3,7},{7,3},{8,12},{12,8},{9,1... | collective-permute-start | bytes 2359304 | tf_op jit(solution)/shard_map/ppermute | solution.py:36
  179.3 2.5 collective-permute-start.17
  184.0 30.8 %all-to-all-start.4 = ((bf16[8,64,768]{2,1,0:T(8,128)(2,1)}), bf16[8,64,768]{2,1,0:T(8,128)(2,1)S(1)}, u32[]{:S(2)}, u32[]{:S(2)}) async-start(bf16[8,64,768]{2,1,0:T(8,128)(2,1)} %bitcast.49), calls=%async_computation.4 | async-start | bytes 1572864 | tf_op jit(solution)/shard_map/all_to_all | solution.py:302
  236.4 2.3 collective-permute-start.18
  250.6 2.5 collective-permute-start.19
  255.3 17.2 %all-to-all-start.6 = ((bf16[8,64,768]{2,1,0:T(8,128)(2,1)}), bf16[8,64,768]{2,1,0:T(8,128)(2,1)S(1)}, u32[]{:S(2)}, u32[]{:S(2)}) async-start(bf16[8,64,768]{2,1,0:T(8,128)(2,1)} %bitcast.53), calls=%async_computation.6 | async-start | bytes 1572864 | tf_op jit(solution)/shard_map/all_to_all | solution.py:302
  258.8 35.5 %copy-start.35 = (bf16[64,768]{1,0:T(8,128)(2,1)S(1)}, bf16[64,768]{1,0:T(8,128)(2,1)}, u32[]{:S(2)}) copy-start(bf16[64,768]{1,0:T(8,128)(2,1)} %get-tuple-element.190) | copy-start | bytes 294916
  295.3 15.6 %all-to-all-start = ((bf16[8,64,768]{2,1,0:T(8,128)(2,1)}), bf16[8,64,768]{2,1,0:T(8,128)(2,1)S(1)}, u32[]{:S(2)}, u32[]{:S(2)}) async-start(bf16[8,64,768]{2,1,0:T(8,128)(2,1)} %broadcast_in_dim.74), calls=%async_computation | async-start | bytes 1572864 | tf_op jit(solution)/shard_map/all_to_all | solution.py:297
  298.9 13.1 %collective-permute-start.20 = (bf16[8,64,768]{2,1,0:T(8,128)(2,1)S(1)}, bf16[8,64,768]{2,1,0:T(8,128)(2,1)S(1)}, u32[]{:S(2)}, u32[]{:S(2)}) collective-permute-start(bf16[8,64,768]{2,1,0:T(8,128)(2,1)S(1)} %all_to_all.91), channel_id=1, source_target_pairs={{0,4},{4,0},{1,5},{5,1},{2,6},{6,2},{3,7},{7,3},{8,12},{12,8},{9,1... | collective-permute-start | bytes 2359304 | tf_op jit(solution)/shard_map/ppermute | solution.py:36
  310.9 12.9 %collective-permute-start.1 = (bf16[8,64,768]{2,1,0:T(8,128)(2,1)S(1)}, bf16[8,64,768]{2,1,0:T(8,128)(2,1)S(1)}, u32[]{:S(2)}, u32[]{:S(2)}) collective-permute-start(bf16[8,64,768]{2,1,0:T(8,128)(2,1)S(1)} %all-to-all-done), channel_id=1, source_target_pairs={{0,4},{4,0},{1,5},{5,1},{2,6},{6,2},{3,7},{7,3},{8,12},{12,8},{9,1... | collective-permute-start | bytes 2359304 | tf_op jit(solution)/shard_map/ppermute | solution.py:36
  338.0 2.6 collective-permute-start.21
  380.0 2.5 collective-permute-start.22
  396.6 2.5 collective-permute-start.23
  438.3 2.3 collective-permute-start.24
  454.7 6.7 collective-permute-start.25
  462.4 20.5 %all-to-all-start.12 = ((bf16[8,64,768]{2,1,0:T(8,128)(2,1)}), bf16[8,64,768]{2,1,0:T(8,128)(2,1)S(1)}, u32[]{:S(2)}, u32[]{:S(2)}) async-start(bf16[8,64,768]{2,1,0:T(8,128)(2,1)} %bitcast.63), calls=%async_computation.12 | async-start | bytes 1572864 | tf_op jit(solution)/shard_map/all_to_all | solution.py:302
  467.1 14.4 %collective-permute-start.43 = (bf16[432,384]{1,0:T(8,128)(2,1)S(1)}, bf16[432,384]{1,0:T(8,128)(2,1)S(1)}, u32[]{:S(2)}, u32[]{:S(2)}) collective-permute-start(bf16[432,384]{1,0:T(8,128)(2,1)S(1)} %get-tuple-element.205), channel_id=1, source_target_pairs={{0,3},{1,0},{2,1},{3,2},{4,7},{5,4},{6,5},{7,6},{8,11},{9,8},{10,9... | collective-permute-start | bytes 995336 | tf_op jit(solution)/shard_map/ppermute | solution.py:36
  467.1 26.4 %collective-permute-start.42 = (bf16[432,384]{1,0:T(8,128)(2,1)}, bf16[432,384]{1,0:T(8,128)(2,1)}, u32[]{:S(2)}, u32[]{:S(2)}) collective-permute-start(bf16[432,384]{1,0:T(8,128)(2,1)} %get-tuple-element.206), channel_id=1, source_target_pairs={{0,2},{1,3},{2,0},{3,1},{4,6},{5,7},{6,4},{7,5},{8,10},{9,11},{10,... | collective-permute-start | bytes 995336 | tf_op jit(solution)/shard_map/ppermute | solution.py:36
  467.1 26.4 %collective-permute-start.41 = (bf16[432,384]{1,0:T(8,128)(2,1)}, bf16[432,384]{1,0:T(8,128)(2,1)}, u32[]{:S(2)}, u32[]{:S(2)}) collective-permute-start(bf16[432,384]{1,0:T(8,128)(2,1)} %get-tuple-element.204), channel_id=1, source_target_pairs={{0,1},{1,2},{2,3},{3,0},{4,5},{5,6},{6,7},{7,4},{8,9},{9,10},{10,1... | collective-permute-start | bytes 995336 | tf_op jit(solution)/shard_map/ppermute | solution.py:36
  477.3 16.1 %collective-permute-start.40 = (bf16[432,384]{1,0:T(8,128)(2,1)}, bf16[432,384]{1,0:T(8,128)(2,1)}, u32[]{:S(2)}, u32[]{:S(2)}) collective-permute-start(bf16[432,384]{1,0:T(8,128)(2,1)} %get-tuple-element.208), channel_id=1, source_target_pairs={{0,3},{1,0},{2,1},{3,2},{4,7},{5,4},{6,5},{7,6},{8,11},{9,8},{10,9... | collective-permute-start | bytes 995336 | tf_op jit(solution)/shard_map/ppermute | solution.py:36
  480.0 13.8 %collective-permute-start.39 = (bf16[432,384]{1,0:T(8,128)(2,1)}, bf16[432,384]{1,0:T(8,128)(2,1)}, u32[]{:S(2)}, u32[]{:S(2)}) collective-permute-start(bf16[432,384]{1,0:T(8,128)(2,1)} %get-tuple-element.209), channel_id=1, source_target_pairs={{0,2},{1,3},{2,0},{3,1},{4,6},{5,7},{6,4},{7,5},{8,10},{9,11},{10,... | collective-permute-start | bytes 995336 | tf_op jit(solution)/shard_map/ppermute | solution.py:36
  481.5 18.8 %collective-permute-start.38 = (bf16[432,384]{1,0:T(8,128)(2,1)}, bf16[432,384]{1,0:T(8,128)(2,1)}, u32[]{:S(2)}, u32[]{:S(2)}) collective-permute-start(bf16[432,384]{1,0:T(8,128)(2,1)} %get-tuple-element.207), channel_id=1, source_target_pairs={{0,1},{1,2},{2,3},{3,0},{4,5},{5,6},{6,7},{7,4},{8,9},{9,10},{10,1... | collective-permute-start | bytes 995336 | tf_op jit(solution)/shard_map/ppermute | solution.py:36
  486.3 25.8 %all-to-all-start.13 = ((bf16[8,64,768]{2,1,0:T(8,128)(2,1)}), bf16[8,64,768]{2,1,0:T(8,128)(2,1)S(1)}, u32[]{:S(2)}, u32[]{:S(2)}) async-start(bf16[8,64,768]{2,1,0:T(8,128)(2,1)} %get-tuple-element.100), calls=%async_computation.13 | async-start | bytes 1572864 | tf_op jit(solution)/shard_map/all_to_all | solution.py:297
  502.2 9.8 %collective-permute-start.44 = (bf16[432,384]{1,0:T(8,128)(2,1)S(1)}, bf16[432,384]{1,0:T(8,128)(2,1)S(1)}, u32[]{:S(2)}, u32[]{:S(2)}) collective-permute-start(bf16[432,384]{1,0:T(8,128)(2,1)S(1)} %get-tuple-element.183), channel_id=1, source_target_pairs={{0,64},{64,0},{1,65},{65,1},{2,66},{66,2},{3,67},{67,3},{4,68},{68... | collective-permute-start | bytes 995336 | tf_op jit(solution)/shard_map/ppermute | solution.py:36
  513.9 70.1 %all-to-all-start.17 = ((bf16[8,432,384]{2,1,0:T(8,128)(2,1)}), bf16[8,432,384]{2,1,0:T(8,128)(2,1)S(1)}, u32[]{:S(2)}, u32[]{:S(2)}) async-start(bf16[8,432,384]{2,1,0:T(8,128)(2,1)} %broadcast_in_dim.94), calls=%async_computation.17 | async-start | bytes 5308416 | tf_op jit(solution)/shard_map/all_to_all | solution.py:422
  520.7 9.7 %collective-permute-start.26 = (bf16[8,64,768]{2,1,0:T(8,128)(2,1)S(1)}, bf16[8,64,768]{2,1,0:T(8,128)(2,1)S(1)}, u32[]{:S(2)}, u32[]{:S(2)}) collective-permute-start(bf16[8,64,768]{2,1,0:T(8,128)(2,1)S(1)} %all-to-all-done.13), channel_id=1, source_target_pairs={{0,4},{4,0},{1,5},{5,1},{2,6},{6,2},{3,7},{7,3},{8,12},{12,8},{9,1... | collective-permute-start | bytes 2359304 | tf_op jit(solution)/shard_map/ppermute | solution.py:36
  528.2 28.0 %collective-permute-start.35 = (bf16[432,384]{1,0:T(8,128)(2,1)S(1)}, bf16[432,384]{1,0:T(8,128)(2,1)S(1)}, u32[]{:S(2)}, u32[]{:S(2)}) collective-permute-start(bf16[432,384]{1,0:T(8,128)(2,1)S(1)} %get-tuple-element.211), channel_id=1, source_target_pairs={{0,3},{1,0},{2,1},{3,2},{4,7},{5,4},{6,5},{7,6},{8,11},{9,8},{10,9... | collective-permute-start | bytes 995336 | tf_op jit(solution)/shard_map/ppermute | solution.py:36
  528.5 29.1 %collective-permute-start.34 = (bf16[432,384]{1,0:T(8,128)(2,1)S(1)}, bf16[432,384]{1,0:T(8,128)(2,1)S(1)}, u32[]{:S(2)}, u32[]{:S(2)}) collective-permute-start(bf16[432,384]{1,0:T(8,128)(2,1)S(1)} %get-tuple-element.212), channel_id=1, source_target_pairs={{0,2},{1,3},{2,0},{3,1},{4,6},{5,7},{6,4},{7,5},{8,10},{9,11},{10,... | collective-permute-start | bytes 995336 | tf_op jit(solution)/shard_map/ppermute | solution.py:36
  529.1 28.4 %collective-permute-start.33 = (bf16[432,384]{1,0:T(8,128)(2,1)S(1)}, bf16[432,384]{1,0:T(8,128)(2,1)S(1)}, u32[]{:S(2)}, u32[]{:S(2)}) collective-permute-start(bf16[432,384]{1,0:T(8,128)(2,1)S(1)} %get-tuple-element.210), channel_id=1, source_target_pairs={{0,1},{1,2},{2,3},{3,0},{4,5},{5,6},{6,7},{7,4},{8,9},{9,10},{10,1... | collective-permute-start | bytes 995336 | tf_op jit(solution)/shard_map/ppermute | solution.py:36
  551.9 17.1 %collective-permute-start.32 = (bf16[432,384]{1,0:T(8,128)(2,1)S(1)}, bf16[432,384]{1,0:T(8,128)(2,1)S(1)}, u32[]{:S(2)}, u32[]{:S(2)}) collective-permute-start(bf16[432,384]{1,0:T(8,128)(2,1)S(1)} %get-tuple-element.214), channel_id=1, source_target_pairs={{0,3},{1,0},{2,1},{3,2},{4,7},{5,4},{6,5},{7,6},{8,11},{9,8},{10,9... | collective-permute-start | bytes 995336 | tf_op jit(solution)/shard_map/ppermute | solution.py:36
  554.6 14.3 %collective-permute-start.31 = (bf16[432,384]{1,0:T(8,128)(2,1)S(1)}, bf16[432,384]{1,0:T(8,128)(2,1)S(1)}, u32[]{:S(2)}, u32[]{:S(2)}) collective-permute-start(bf16[432,384]{1,0:T(8,128)(2,1)S(1)} %get-tuple-element.215), channel_id=1, source_target_pairs={{0,2},{1,3},{2,0},{3,1},{4,6},{5,7},{6,4},{7,5},{8,10},{9,11},{10,... | collective-permute-start | bytes 995336 | tf_op jit(solution)/shard_map/ppermute | solution.py:36
  556.2 16.4 %collective-permute-start.30 = (bf16[432,384]{1,0:T(8,128)(2,1)S(1)}, bf16[432,384]{1,0:T(8,128)(2,1)S(1)}, u32[]{:S(2)}, u32[]{:S(2)}) collective-permute-start(bf16[432,384]{1,0:T(8,128)(2,1)S(1)} %get-tuple-element.213), channel_id=1, source_target_pairs={{0,1},{1,2},{2,3},{3,0},{4,5},{5,6},{6,7},{7,4},{8,9},{9,10},{10,1... | collective-permute-start | bytes 995336 | tf_op jit(solution)/shard_map/ppermute | solution.py:36
  574.1 9.8 %collective-permute-start.36 = (bf16[432,384]{1,0:T(8,128)(2,1)S(1)}, bf16[432,384]{1,0:T(8,128)(2,1)S(1)}, u32[]{:S(2)}, u32[]{:S(2)}) collective-permute-start(bf16[432,384]{1,0:T(8,128)(2,1)S(1)} %get-tuple-element.186), channel_id=1, source_target_pairs={{0,64},{64,0},{1,65},{65,1},{2,66},{66,2},{3,67},{67,3},{4,68},{68... | collective-permute-start | bytes 995336 | tf_op jit(solution)/shard_map/ppermute | solution.py:36
  585.9 39.6 %copy-start.29 = (bf16[512,768]{1,0:T(8,128)(2,1)S(1)}, bf16[512,768]{1,0:T(8,128)(2,1)}, u32[]{:S(2)}) copy-start(bf16[512,768]{1,0:T(8,128)(2,1)} %get-tuple-element.107) | copy-start | bytes 2359300
  585.9 39.1 %all-to-all-start.16 = ((bf16[8,432,384]{2,1,0:T(8,128)(2,1)}), bf16[8,432,384]{2,1,0:T(8,128)(2,1)}, u32[]{:S(2)}, u32[]{:S(2)}) async-start(bf16[8,432,384]{2,1,0:T(8,128)(2,1)} %broadcast_in_dim.93), calls=%async_computation.16 | async-start | bytes 5308416 | tf_op jit(solution)/shard_map/all_to_all | solution.py:422
  593.2 32.3 %collective-permute-start.28 = (bf16[512,768]{1,0:T(8,128)(2,1)}, bf16[512,768]{1,0:T(8,128)(2,1)}, u32[]{:S(2)}, u32[]{:S(2)}) collective-permute-start(bf16[512,768]{1,0:T(8,128)(2,1)} %get-tuple-element.108), channel_id=1, source_target_pairs={{0,4},{4,0},{1,5},{5,1},{2,6},{6,2},{3,7},{7,3},{8,12},{12,8},{9,1... | collective-permute-start | bytes 2359304 | tf_op jit(solution)/shard_map/ppermute | solution.py:36
  593.2 81.5 %collective-permute-start.45 = (bf16[8,432,384]{2,1,0:T(8,128)(2,1)S(1)}, bf16[8,432,384]{2,1,0:T(8,128)(2,1)}, u32[]{:S(2)}, u32[]{:S(2)}) collective-permute-start(bf16[8,432,384]{2,1,0:T(8,128)(2,1)S(1)} %all-to-all-done.17.own_b), channel_id=1, source_target_pairs={{0,4},{4,0},{1,5},{5,1},{2,6},{6,2},{3,7},{7,3},{8,12},{12,8},{9,1... | collective-permute-start | bytes 7962632 | tf_op jit(solution)/shard_map/ppermute | solution.py:36
  625.0 49.7 %collective-permute-start.37 = (bf16[8,432,384]{2,1,0:T(8,128)(2,1)}, bf16[8,432,384]{2,1,0:T(8,128)(2,1)}, u32[]{:S(2)}, u32[]{:S(2)}) collective-permute-start(bf16[8,432,384]{2,1,0:T(8,128)(2,1)} %all-to-all-done.16.own_a), channel_id=1, source_target_pairs={{0,4},{4,0},{1,5},{5,1},{2,6},{6,2},{3,7},{7,3},{8,12},{12,8},{9,1... | collective-permute-start | bytes 7962632 | tf_op jit(solution)/shard_map/ppermute | solution.py:36
  625.0 7.5 %collective-permute-start.27 = (bf16[512,768]{1,0:T(8,128)(2,1)}, bf16[512,768]{1,0:T(8,128)(2,1)}, u32[]{:S(2)}, u32[]{:S(2)}) collective-permute-start(bf16[512,768]{1,0:T(8,128)(2,1)} %get-tuple-element.104), channel_id=1, source_target_pairs={{0,4},{4,0},{1,5},{5,1},{2,6},{6,2},{3,7},{7,3},{8,12},{12,8},{9,1... | collective-permute-start | bytes 2359304 | tf_op jit(solution)/shard_map/ppermute | solution.py:36
  627.7 18.3 %all-to-all-start.15 = ((bf16[8,64,768]{2,1,0:T(8,128)(2,1)}), bf16[8,64,768]{2,1,0:T(8,128)(2,1)S(1)}, u32[]{:S(2)}, u32[]{:S(2)}) async-start(bf16[8,64,768]{2,1,0:T(8,128)(2,1)} %bitcast.296), calls=%async_computation.15 | async-start | bytes 1572864 | tf_op jit(solution)/shard_map/all_to_all | solution.py:302
  646.0 17.4 %all-to-all-start.14 = ((bf16[8,64,768]{2,1,0:T(8,128)(2,1)}), bf16[8,64,768]{2,1,0:T(8,128)(2,1)}, u32[]{:S(2)}, u32[]{:S(2)}) async-start(bf16[8,64,768]{2,1,0:T(8,128)(2,1)} %bitcast.295), calls=%async_computation.14 | async-start | bytes 1572864 | tf_op jit(solution)/shard_map/all_to_all | solution.py:302
  653.3 19.6 %copy-start.27 = (f32[64,768]{1,0:T(8,128)S(1)}, f32[64,768]{1,0:T(8,128)}, u32[]{:S(2)}) copy-start(f32[64,768]{1,0:T(8,128)} %get-tuple-element.109) | copy-start | bytes 589828
  666.9 6.0 collective-permute-start.29
  (50 other events, 401.8 us)

commit v2 on v1

--- a/solution.py
+++ b/solution.py
@@ -28,7 +28,7 @@
 SHARE = 416
 PACK = 432
 VMEM = pltpu.VMEM
-ROOM = 56 * 1024 * 1024
+MIB = 1024 * 1024
 
 
 def shifted(block, axis, distance):
@@ -42,16 +42,34 @@
     )
 
 
-def call(kernel, outs, *args, scratch=(), smem=0):
+def cost(microseconds):
+    return pl.CostEstimate(
+        flops=int(microseconds * 1e9), bytes_accessed=int(microseconds * 3.5e6), transcendentals=0
+    )
+
+
+def whole(shape):
+    return pl.BlockSpec(shape, lambda _: (0,) * len(shape))
+
+
+def call(kernel, outs, *args, scratch=(), smem=0, room=12, takes=2):
     specs = [pl.BlockSpec(memory_space=pltpu.SMEM)] * smem
-    specs += [pl.BlockSpec(memory_space=VMEM)] * (len(args) - smem)
+    for i in range(smem, len(args)):
+        if isinstance(args[i], tuple):
+            block, at = args[i]
+            specs.append(pl.BlockSpec((None,) + block.shape[1:], lambda _, at=at: (at, 0, 0)))
+        else:
+            specs.append(whole(args[i].shape))
+    args = [a[0] if isinstance(a, tuple) else a for a in args]
     return pl.pallas_call(
         kernel,
         out_shape=[jax.ShapeDtypeStruct(shape, dtype) for shape, dtype in outs],
         in_specs=specs,
-        out_specs=[pl.BlockSpec(memory_space=VMEM)] * len(outs),
+        out_specs=[whole(shape) for shape, _ in outs],
+        grid=(1,),
         scratch_shapes=list(scratch),
-        compiler_params=pltpu.CompilerParams(vmem_limit_bytes=ROOM),
+        cost_estimate=cost(takes),
+        compiler_params=pltpu.CompilerParams(vmem_limit_bytes=room * MIB),
     )(*args)
 
 
@@ -95,15 +113,18 @@
         branch_out[k] = branch
 
 
-def share_weights(owner, share, w_qkv, w_up, w_down, w_out):
-    for z in range(4):
-        w_qkv[pl.ds(z * 192, 192), :] = share[z, 0:192, 0:192]
-        w_up[pl.ds(z * 192, 192), :] = share[z, 0:192, 192:384]
-        w_down[pl.ds(z * 48, 48), 0:384] = share[z, 192:240, :]
-        w_down[pl.ds(z * 48, 48), 384:768] = share[z, 304:352, :]
-    at = owner[0]
-    w_out[:, 0:384] = share[at, 240:304, :]
-    w_out[:, 384:768] = share[at, 352:416, :]
+def share_weights(place, pieces, w_qkv, w_up, w_down, w_out):
+    for k, piece in enumerate(pieces):
+        at = lax.rem(place[0] + (4 - k), 4)
+        w_qkv[pl.ds(pl.multiple_of(at * 192, 64), 192), :] = piece[0:192, 0:192]
+        w_up[pl.ds(pl.multiple_of(at * 192, 64), 192), :] = piece[0:192, 192:384]
+        w_down[pl.ds(pl.multiple_of(at * 48, 16), 48), 0:384] = piece[192:240, :]
+        w_down[pl.ds(pl.multiple_of(at * 48, 16), 48), 384:768] = piece[304:352, :]
+
+        @pl.when(at == place[1])
+        def _():
+            w_out[:, 0:384] = piece[240:304, :]
+            w_out[:, 384:768] = piece[352:416, :]
 
 
 WEIGHT_SCRATCH = (
@@ -115,10 +136,10 @@
 
 
 def scored(q, k, query_places, key_places):
-    scores = dot(q, k, 1, 1) * SCORE_SCALE
+    scores = dot(q * SCORE_SCALE, k, 1, 1)
     scores = jnp.where(query_places >= key_places, scores, -1e30)
     raised = jnp.exp(scores - jnp.max(scores, -1, keepdims=True))
-    return raised / jnp.sum(raised, -1, keepdims=True)
+    return raised * (1.0 / jnp.sum(raised, -1, keepdims=True))
 
 
 def turn(v, tables, rows, sign):
@@ -129,11 +150,11 @@
 
 
 def forward_kernel(
-    owner, own, other, vec, bias, share, cosine, ahead, behind, p_col, p_row,
+    place, own, other, vec, bias, s0, s1, s2, s3, cosine, ahead, behind, p_col, p_row,
     part_own, part_other, qkv, pre, act,
     w_qkv, w_up, w_down, w_out,
 ):
-    share_weights(owner, share, w_qkv, w_up, w_down, w_out)
+    share_weights(place, (s0, s1, s2, s3), w_qkv, w_up, w_down, w_out)
     tables = (cosine, ahead, behind)
     for half, source in enumerate((own, other)):
 
@@ -166,11 +187,11 @@
 
 
 def backward_kernel(
-    owner, b_own, b_other, n_own, n_other, vec, share, cosine, ahead, behind, p_col, p_row, qkv, pre,
+    place, b_own, b_other, n_own, n_other, vec, s0, s1, s2, s3, cosine, ahead, behind, p_col, p_row, qkv, pre,
     gy_own, gy_other, d_qkv, d_up, sums,
     w_qkv, w_up, w_down, w_out, dq, dk, dv,
 ):
-    share_weights(owner, share, w_qkv, w_up, w_down, w_out)
+    share_weights(place, (s0, s1, s2, s3), w_qkv, w_up, w_down, w_out)
     tables = (cosine, ahead, behind)
     dk[...] = jnp.zeros_like(dk)
     dv[...] = jnp.zeros_like(dv)
@@ -253,30 +274,55 @@
         pack[z, 416:432, :] = jnp.concatenate([rows, blank], 0).astype(BF)
 
 
-def unpack_kernel(place, own_a, other_a, own_b, other_b, g_qkv, g_out, g_up, g_down, rest):
+def unpack_kernel(place, own, other, *refs):
+    g_qkv, g_out, g_up, g_down, rest = refs[-5:]
     low = place[0] == 0
     z = place[1]
-    for j, (own, other) in enumerate(((own_a, other_a), (own_b, other_b))):
-        for i in range(16):
-            k = i // 2
-            mine, theirs = (own, other) if i % 2 == 0 else (other, own)
-            block = jnp.where(low, mine[k].astype(F32), theirs[k].astype(F32))
-            if i < H:
-                for t in range(3):
-                    g_qkv[j, :, t * D + i * HD : t * D + (i + 1) * HD] = block[0:192, t * HD : (t + 1) * HD]
-            for t in range(4):
-                at = t * D + i * 48
-                g_up[j, :, at : at + 48] = block[0:192, 192 + t * 48 : 240 + t * 48]
-            g_down[j, i * 48 : (i + 1) * 48, 0:384] = block[192:240, :]
-            g_down[j, i * 48 : (i + 1) * 48, 384:768] = block[304:352, :]
-            rest[j, i] = block[416:432, :]
-        for h in range(3):
-            i = 3 * z + h
-            k = i // 2
-            mine = (i % 2) == place[0]
-            out = jnp.where(mine, own[k].astype(F32), other[k].astype(F32))
-            g_out[j, h * HD : (h + 1) * HD, 0:384] = out[240:304, :]
-            g_out[j, h * HD : (h + 1) * HD, 384:768] = out[352:416, :]
+    for i in range(16):
+        k = i // 2
+        mine, theirs = (own, other) if i % 2 == 0 else (other, own)
+        block = jnp.where(low, mine[k], theirs[k]).astype(F32)
+        if i < H:
+            for t in range(3):
+                g_qkv[0, :, t * D + i * HD : t * D + (i + 1) * HD] = block[0:192, t * HD : (t + 1) * HD]
+        for t in range(4):
+            at = t * D + i * 48
+            g_up[0, :, at : at + 48] = block[0:192, 192 + t * 48 : 240 + t * 48]
+        g_down[0, i * 48 : (i + 1) * 48, 0:384] = block[192:240, :]
+        g_down[0, i * 48 : (i + 1) * 48, 384:768] = block[304:352, :]
+        rest[0, i] = block[416:432, :]
+    for h in range(3):
+        i = 3 * z + h
+        k = i // 2
+        mine = (i % 2) == place[0]
+        out = jnp.where(mine, own[k], other[k]).astype(F32)
+        g_out[0, h * HD : (h + 1) * HD, 0:384] = out[240:304, :]
+        g_out[0, h * HD : (h + 1) * HD, 384:768] = out[352:416, :]
+
+
+UNPACKED = ((192, 3 * D), (192, D), (192, FF), (D, D), (16, 16, 384))
+
+
+def unpacked(j, place, own, other, earlier):
+    specs = [pl.BlockSpec(memory_space=pltpu.SMEM)]
+    specs += [pl.BlockSpec((8, PACK, 384), lambda i: (0, 0, 0))] * 2
+    specs += [pl.BlockSpec(memory_space=pl.ANY)] * len(earlier)
+    return pl.pallas_call(
+        unpack_kernel,
+        grid=(1,),
+        out_shape=[jax.ShapeDtypeStruct((2,) + shape, F32) for shape in UNPACKED],
+        in_specs=specs,
+        out_specs=[
+            pl.BlockSpec((1,) + shape, lambda i, n=len(shape): (j,) + (0,) * n) for shape in UNPACKED
+        ],
+        input_output_aliases={3 + i: i for i in range(len(earlier))},
+        cost_estimate=cost(7),
+        compiler_params=pltpu.CompilerParams(vmem_limit_bytes=40 * MIB),
+    )(place, own, other, *earlier)
+
+
+def after(earlier, later):
+    return lax.optimization_barrier((earlier, later))[1]
 
 
 def body(ends, blocks, g1, h1, g2, h2, wq, bq, wo, bo, wu, bu, wd, bd):
@@ -293,40 +339,56 @@
     x = jnp.where(first, keep, received).astype(F32)
     dx = jnp.where(first, received, keep)
 
-    def from_chips(sent):
-        own = lax.all_to_all(sent, CHIPS, 0, 0, tiled=True)
+    def exchanged(sent, beside=None):
+        got = lax.all_to_all(sent, CHIPS, 0, 0, tiled=True)
+        return got if beside is None else lax.optimization_barrier((got, beside))
+
+    def both_cores(own):
         return own.reshape(HALF, D), shifted(own, "c", 1).reshape(HALF, D)
 
-    def to_chips(own, other):
-        part = own + shifted(other, "c", 1)
-        return lax.all_to_all(part.reshape(8, ROWS, D), CHIPS, 0, 0, tiled=True)
+    def halves_joined(own, other):
+        return (own + shifted(other, "c", 1)).reshape(8, ROWS, D)
 
     n_sent = call(start_kernel, [((8, ROWS, D), BF)], x)[0]
-    normals = from_chips(n_sent)
-
-    def share_of(j):
-        mask = has_head.astype(BF)
-        cols = [lax.dynamic_slice_in_dim(wq[j], t * D + unit * HD, HD, 1) * mask for t in range(3)]
-        cols += [lax.dynamic_slice_in_dim(wu[j], t * D + unit * 48, 48, 1) for t in range(4)]
-        down = lax.dynamic_slice_in_dim(wd[j], unit * 48, 48, 0)
-        out = lax.dynamic_slice_in_dim(wo[j], (unit % 3) * HD, HD, 0) * mask
-        rows = jnp.concatenate([down, out], 0)
-        return jnp.concatenate([jnp.concatenate(cols, 1), rows[:, :384], rows[:, 384:]], 0)
+    mask = has_head.astype(BF)
+
+    def cut(w, at, sizes):
+        return lax.dynamic_slice(w, at, sizes)
+
+    zero = jnp.int32(0)
+    cols = [cut(wq, (zero, zero, t * D + unit * HD), (2, 192, HD)) * mask for t in range(3)]
+    cols += [cut(wu, (zero, zero, t * D + unit * 48), (2, 192, 48)) for t in range(4)]
+    down = cut(wd, (zero, unit * 48, zero), (2, 48, D))
+    out = cut(wo, (zero, (unit % 3) * HD, zero), (2, HD, D)) * mask
+    rows = jnp.concatenate([down, out], 1)
+    shares = jnp.concatenate([jnp.concatenate(cols, 2), rows[..., :384], rows[..., 384:]], 1)
 
     def joined_sections(mine):
         theirs = shifted(mine, "s", 1)
         return jnp.where(first, mine, theirs), jnp.where(first, theirs, mine)
 
+    def pieces_round_z(block):
+        return [block] + [shifted(block, "z", k) for k in range(1, 4)]
+
     def round_z(block):
-        whole = jnp.zeros((4,) + block.shape, BF)
-        whole = lax.dynamic_update_slice_in_dim(whole, block[None], z, 0)
-        for k in range(1, 4):
-            whole = lax.dynamic_update_slice_in_dim(
-                whole, shifted(block, "z", k)[None], (z - k) % 4, 0
+        pieces = pieces_round_z(block)
+        order = [pieces[0]] * 4
+        for at in range(4):
+            order[at] = jnp.where(
+                z == at,
+                pieces[0],
+                jnp.where(
+                    z == (at + 1) % 4, pieces[1], jnp.where(z == (at + 2) % 4, pieces[2], pieces[3])
+                ),
             )
-        return whole
-
-    vectors = jnp.concatenate([g1, h1, g2, h2, bq, bo, bu, bd], 1)
+        return jnp.stack(order)
+
+    early = joined_sections(shares[0])
+    early = after(n_sent, early)
+    layer_share = [[(piece, 0) for piece in pieces_round_z(early[0][None])]]
+    later = joined_sections(after(early, shares[1]))
+
+    vectors = after(early, jnp.concatenate([g1, h1, g2, h2, bq, bo, bu, bd], 1))
     vectors = round_z(jnp.concatenate(joined_sections(vectors), 0))
     layer_vec, layer_bias, layer_add = [], [], []
     for l in range(LAYERS):
@@ -344,14 +406,9 @@
         )
         layer_add.append(members[5] + members[7])
 
-    early = joined_sections(share_of(0))
-    later = joined_sections(share_of(1))
-    layer_share = [round_z(early[0])]
-    rest = round_z(jnp.stack([later[0], early[1], later[1]]))
-    layer_share += [rest[:, i] for i in range(3)]
-
     blk = ROWS // 2
     offsets = jnp.arange(SEQ, dtype=jnp.int32)
+    blocks = after(early, blocks)
     row_blocks = jnp.where(first, blocks[0], blocks[1])
     places = (jnp.repeat(row_blocks, blk) * blk + offsets % blk).reshape(8, 2, ROWS)
     places = jnp.where(c == 0, places, places[:, ::-1]).transpose(1, 0, 2).reshape(SEQ)
@@ -365,68 +422,100 @@
     ahead = jnp.concatenate([-sin, none, still] * 2, 1)
     behind = jnp.concatenate([none, sin, still] * 2, 1)
     tables = (cosine, ahead, behind, places[:, None], places[None, :])
-    owner = owner.reshape(1)
+    own, (tables, layer_vec, layer_bias, layer_add, layer_share[0]) = exchanged(
+        n_sent, (tables, layer_vec, layer_bias, layer_add, [piece for piece, _ in layer_share[0]])
+    )
+    layer_share[0] = [(piece, 0) for piece in layer_share[0]]
+    normals = both_cores(own)
+    place = jnp.stack([z.astype(jnp.int32), owner])
 
     kept = []
     for l in range(LAYERS):
         own, other, qkv, pre, act = call(
             forward_kernel,
             [((HALF, D), BF), ((HALF, D), BF), ((SEQ, UNITS), BF), ((SEQ, UNITS), F32), ((SEQ, 256), BF)],
-            owner, *normals, layer_vec[l], layer_bias[l], layer_share[l], *tables,
-            scratch=WEIGHT_SCRATCH, smem=1,
+            place, *normals, layer_vec[l], layer_bias[l], *layer_share[l], *tables,
+            scratch=WEIGHT_SCRATCH, smem=1, room=56, takes=11,
         )
+        if l == 1:
+            sent = after(normals, jnp.broadcast_to(dx[None], (8, ROWS, D)))
+            branches, (own, other) = exchanged(sent, (own, other))
+            branches = both_cores(branches)
         kept.append((x, normals, qkv, pre, act))
-        got = to_chips(own, other)
-        x, n_sent = call(
-            functools.partial(finish_kernel, l == 1),
-            [((ROWS, D), F32), ((8, ROWS, D), BF)], got, x, layer_add[l],
-        )
         if l + 1 < LAYERS:
-            normals = from_chips(n_sent)
-    final = x
-
-    branches = from_chips(jnp.broadcast_to(dx[None], (8, ROWS, D)))
+            got = exchanged(halves_joined(own, other))
+            x, n_sent = call(
+                functools.partial(finish_kernel, l == 1),
+                [((ROWS, D), F32), ((8, ROWS, D), BF)], got, x, layer_add[l],
+            )
+            if l == 0:
+                block = after(normals, jnp.stack([later[0], early[1], later[1]]))
+                own, pieces = exchanged(n_sent, pieces_round_z(block))
+                layer_share += [[(piece, i) for piece in pieces] for i in range(3)]
+                normals = both_cores(own)
+            else:
+                normals = both_cores(exchanged(n_sent))
+    last = halves_joined(own, other)
+
     dx = dx.astype(F32)
-    shares = [None] * LAYERS
+    packs, shares = [None] * LAYERS, [None] * LAYERS
+    def sent_round(pack):
+        parts = [lax.dynamic_index_in_dim(pack, (z + k) % 4, 0, False) for k in range(4)]
+        return [parts[0]] + [shifted(parts[k], "z", k) for k in range(1, 4)]
+
+    def summed(parts):
+        return sum(part.astype(F32) for part in parts).astype(BF)
+
+    def both_sections(j):
+        mine = jnp.where(first, shares[j], shares[j + 2])
+        theirs = shifted(jnp.where(first, shares[j + 2], shares[j]), "s", 1)
+        return (mine.astype(F32) + theirs.astype(F32)).astype(BF)
+
     for l in reversed(range(LAYERS)):
         x, normals, qkv, pre, act = kept[l]
         own, other, d_qkv, d_up, sums = call(
             backward_kernel,
             [((HALF, D), BF), ((HALF, D), BF), ((SEQ, UNITS), BF), ((SEQ, UNITS), BF), ((8, D), F32)],
-            owner, *branches, *normals, layer_vec[l], layer_share[l], *tables, qkv, pre,
-            scratch=WEIGHT_SCRATCH + (VMEM((SEQ, HD), F32),) * 3, smem=1,
+            place, *branches, *normals, layer_vec[l], *layer_share[l], *tables, qkv, pre,
+            scratch=WEIGHT_SCRATCH + (VMEM((SEQ, HD), F32),) * 3, smem=1, room=56, takes=13,
         )
-        got = to_chips(own, other)
+        if l + 1 == LAYERS:
+            got, (own, other) = exchanged(last, (own, other))
+            final = call(
+                functools.partial(finish_kernel, False),
+                [((ROWS, D), F32), ((8, ROWS, D), BF)], got, x, layer_add[l],
+            )[0]
+        else:
+            own, other, parts = lax.optimization_barrier((own, other, parts))
+            shares[l + 1] = summed(parts)
         pack = call(
             product_kernel, [((4, PACK, 384), BF)],
             *branches, *normals, layer_vec[l], act, d_qkv, d_up, sums,
             scratch=(VMEM((D, UNITS), F32), VMEM((D, UNITS), F32), VMEM((256, D), F32)),
+            room=56, takes=6,
         )[0]
-        total = lax.dynamic_index_in_dim(pack, z, 0, False).astype(F32)
-        for k in range(1, 4):
-            sent = lax.dynamic_index_in_dim(pack, (z + k) % 4, 0, False)
-            total = total + shifted(sent, "z", k).astype(F32)
-        shares[l] = total.astype(BF)
+        got, pack = exchanged(halves_joined(own, other), pack)
         dx, branch_sent = call(
             functools.partial(finish_back_kernel, l == 2),
             [((ROWS, D), F32), ((8, ROWS, D), BF)], got, x, dx,
         )
         if l > 0:
-            branches = from_chips(branch_sent)
-
-    def spread(j):
-        mine = jnp.where(first, shares[j], shares[j + 2])
-        theirs = shifted(jnp.where(first, shares[j + 2], shares[j]), "s", 1)
-        part = (mine.astype(F32) + theirs.astype(F32)).astype(BF)
-        sent = jnp.broadcast_to(part[None], (8, PACK, 384))
-        own = lax.all_to_all(sent, CHIPS, 0, 0, tiled=True)
-        return own, shifted(own, "c", 1)
-
-    second, initial = spread(1), spread(0)
-    grad_qkv, grad_out, grad_up, grad_down, extra = call(
-        unpack_kernel,
-        [((2, 192, 3 * D), F32), ((2, 192, D), F32), ((2, 192, FF), F32), ((2, D, D), F32), ((2, 16, 16, 384), F32)],
-        jnp.stack([c, z]).astype(jnp.int32), *initial, *second, smem=1,
+            parts = sent_round(pack)
+            branches, parts[2] = exchanged(branch_sent, parts[2])
+            branches = both_cores(branches)
+
+    sent = jnp.broadcast_to(after(got, both_sections(1))[None], (8, PACK, 384))
+    shares[0] = summed(sent_round(pack))
+    own, initial = exchanged(sent, (both_sections(0), dx))
+    initial, dx = initial
+
+    corner = jnp.stack([c, z]).astype(jnp.int32)
+    earlier = unpacked(1, corner, own, shifted(own, "c", 1), ())
+    sent = jnp.broadcast_to(initial[None], (8, PACK, 384))
+    came = shifted(jnp.where(first, final, dx), "s", 1)
+    own, (earlier, came) = exchanged(sent, (earlier, came))
+    grad_qkv, grad_out, grad_up, grad_down, extra = unpacked(
+        0, corner, own, shifted(own, "c", 1), earlier
     )
     norm_sums = jnp.sum(extra[:, :, 0:2], 1)
     v_g1, v_h1 = norm_sums[:, 0, :192], norm_sums[:, 0, 192:]
@@ -437,7 +526,6 @@
     v_up = lax.dynamic_index_in_dim(v_up, z, 1, False)
     v_branch = extra[:, 0, 3, :192]
 
-    came = shifted(jnp.where(first, final, dx), "s", 1)
     have = jnp.where(first, dx, final)
     boundary = jnp.stack([jnp.where(first, have, came), jnp.where(first, came, have)])
     boundary = boundary.reshape(1, 2, 1, ROWS, D)

time: 702 us -> 600 us (0.85)
  blocking collectives: 108 us -> 69.8 us
  local copies, waits for them, and re-layouts: 79.8 us -> 46.7 us
  waiting for transfers between devices: 201 us -> 182 us
  Pallas kernels: 156 us -> 145 us
  other arithmetic: 39 us -> 29.4 us
    all_to_all x12 -> x14, waiting for transfers between devices: 107 us -> 46.2 us  [exchanged(): got = lax.all_to_all(sent, CHIPS, 0, 0, tiled=True)]
    ppermute x46, waiting for transfers between devices: 93.7 us -> 136 us  [shifted(): lax.ppermute(block, axis, [(i, (i + distance) % size) for i in range(size)])]
    all_to_all x6 -> x4, blocking collectives: 108 us -> 69.8 us  [exchanged(): got = lax.all_to_all(sent, CHIPS, 0, 0, tiled=True)]
    pallas_call x22 -> x21, Pallas kernels: 156 us -> 132 us  [call(): pl.pallas_call(kernel, out_shape=[jax.ShapeDtypeStruct(shape, dtype) for...]
    pallas_call x0 -> x2, Pallas kernels: none -> 12.3 us  [unpacked(): pl.pallas_call(unpack_kernel, grid=(1,), out_shape=[jax.ShapeDtypeStruct(...]
    dynamic_update_slice x10 -> x0, local copies, waits for them, and re-layouts: 9.94 us -> none  [the longest x9 9.72 us: round_z(): lax.dynamic_update_slice_in_dim(whole, shifted(block, 'z', k)[None], (z -...]
    all_to_all x12 -> x14, starting transfers between devices: 72 us -> 77.9 us  [exchanged(): got = lax.all_to_all(sent, CHIPS, 0, 0, tiled=True)]
    unnamed x123 -> x135, local copies, waits for them, and re-layouts: 15.8 us -> 17.8 us
  transfers between devices with their start and end apart: 58 -> 60, of which waited for: 25 -> 36; matrix products, arithmetic and copies ran while one was open for 12% -> 7% of each run, Pallas kernels for 9% -> 17%
where the time goes in v2:
time: 600 us; the launch traced here: 590 us
  waiting for transfers between devices  182 us (30%)
  Pallas kernels  145 us (24%)
  starting transfers between devices  115 us (19%)
  blocking collectives  69.8 us (12%)
  local copies, waits for them, and re-layouts  46.7 us (8%)
  other arithmetic  29.4 us (5%)
    ppermute x46, waiting for transfers between devices, shifted(): lax.ppermute(block, axis, [(i, (i + distance) % size) for i in range(size)])  136 us
    pallas_call x21, Pallas kernels, call(): pl.pallas_call(kernel, out_shape=[jax.ShapeDtypeStruct(shape, dtype) for...  132 us
    all_to_all x14, starting transfers between devices, exchanged(): got = lax.all_to_all(sent, CHIPS, 0, 0, tiled=True)  77.9 us
    all_to_all x4, blocking collectives, exchanged(): got = lax.all_to_all(sent, CHIPS, 0, 0, tiled=True)  69.8 us
    all_to_all x14, waiting for transfers between devices, exchanged(): got = lax.all_to_all(sent, CHIPS, 0, 0, tiled=True)  46.2 us
    ppermute x46, starting transfers between devices, shifted(): lax.ppermute(block, axis, [(i, (i + distance) % size) for i in range(size)])  37 us
    unnamed x135, local copies, waits for them, and re-layouts  17.8 us
    add x8, other arithmetic, halves_joined(): return (own + shifted(other, 'c', 1)).reshape(8, ROWS, D)  14.8 us
  transfers between devices with their start and end apart: 60, of which 36 were waited for; matrix products, arithmetic and copies ran while one was open for 7% of the time, Pallas kernels for 17%

profile of v2, /device:TPU:0, one launch (start us, length us, event | category | flops | bytes accessed | tf_op | source)
XLA Modules:
  0.0 589.6 jit_solution(7076881913712136356)
XLA Ops:
  10.3 7.0 %all-to-all-start = ((bf16[8,64,768]{2,1,0:T(8,128)(2,1)}), bf16[8,64,768]{2,1,0:T(8,128)(2,1)}, u32[]{:S(2)}, u32[]{:S(2)}) async-start(bf16[8,64,768]{2,1,0:T(8,128)(2,1)} %shard_map.237), calls=%async_computation | async-start | bytes 1572864 | tf_op jit(solution)/shard_map/all_to_all | solution.py:343
  20.2 4.0 collective-permute-start.8
  24.3 2.3 collective-permute-done.2
  26.7 4.1 collective-permute-start.5
  52.2 11.3 %shard_map.238 = (bf16[512,768]{1,0:T(8,128)(2,1)}, bf16[512,768]{1,0:T(8,128)(2,1)}, bf16[1024,192]{1,0:T(8,128)(2,1)}, f32[1024,192]{1,0:T(8,128)}, bf16[1024,256]{1,0:T(8,128)(2,1)}) custom-call(s32[2]{0:T(128)} %pad_add_fusion.place, bf16[512,768]{1,0:T(8,128)(2,1)} %bitcast.19.own.n_own, bf16[512,768]{1,0:T(8,128)(2,1)} %bitcast.167, ...), custom_call_target="tpu_custom_call" | custom-call | flops 11000000512 | bytes 38500000 | tf_op jit(solution)/shard_map/pallas_call | solution.py:64
  68.2 7.8 %all-to-all-start.1 = ((bf16[8,64,768]{2,1,0:T(8,128)(2,1)}), bf16[8,64,768]{2,1,0:T(8,128)(2,1)S(1)}, u32[]{:S(2)}, u32[]{:S(2)}) async-start(bf16[8,64,768]{2,1,0:T(8,128)(2,1)} %bitcast.21), calls=%async_computation.1 | async-start | bytes 1572864 | tf_op jit(solution)/shard_map/all_to_all | solution.py:343
  78.9 10.7 %all-to-all-done.1.got = bf16[8,64,768]{2,1,0:T(8,128)(2,1)S(1)} async-done(((bf16[8,64,768]{2,1,0:T(8,128)(2,1)}), bf16[8,64,768]{2,1,0:T(8,128)(2,1)S(1)}, u32[]{:S(2)}, u32[]{:S(2)}) %all-to-all-start.1) | async-done | bytes 786464 | tf_op jit(solution)/shard_map/all_to_all | solution.py:343
  90.8 3.7 all-to-all-start.2
  94.6 5.8 collective-permute-done.14.s3
  100.4 2.7 collective-permute-done.13.s2
  103.1 19.1 %collective-permute-done.12.s1 = bf16[3,416,384]{2,1,0:T(8,128)(2,1)} collective-permute-done((bf16[3,416,384]{2,1,0:T(8,128)(2,1)S(1)}, bf16[3,416,384]{2,1,0:T(8,128)(2,1)}, u32[]{:S(2)}, u32[]{:S(2)}) %collective-permute-start.12) | collective-permute-done | bytes 958496 | tf_op jit(solution)/shard_map/ppermute | solution.py:36
  122.1 2.3 collective-permute-done.15
  125.5 6.9 %all-to-all-start.3 = ((bf16[8,64,768]{2,1,0:T(8,128)(2,1)}), bf16[8,64,768]{2,1,0:T(8,128)(2,1)}, u32[]{:S(2)}, u32[]{:S(2)}) async-start(bf16[8,64,768]{2,1,0:T(8,128)(2,1)} %broadcast_in_dim.36), calls=%async_computation.3 | async-start | bytes 1572864 | tf_op jit(solution)/shard_map/all_to_all | solution.py:343
  132.4 11.1 %shard_map.240 = (bf16[512,768]{1,0:T(8,128)(2,1)}, bf16[512,768]{1,0:T(8,128)(2,1)}, bf16[1024,192]{1,0:T(8,128)(2,1)}, f32[1024,192]{1,0:T(8,128)}, bf16[1024,256]{1,0:T(8,128)(2,1)}) custom-call(s32[2]{0:T(128)} %pad_add_fusion.place, bf16[512,768]{1,0:T(8,128)(2,1)} %bitcast.141, bf16[512,768]{1,0:T(8,128)(2,1)} %bitcast.170, f32[8,768]{1,0:T(8,128)} %concatenate.81.vec, ...), custom_call_target="tpu_custom_call" | custom-call | flops 11000000512 | bytes 38500000 | tf_op jit(solution)/shard_map/pallas_call | solution.py:64
  143.6 2.6 all-to-all-done.3
  146.2 2.5 collective-permute-done.16
  150.1 19.1 %all_to_all.90.got = bf16[8,64,768]{2,1,0:T(8,128)(2,1)S(1)} all-to-all(bf16[8,64,768]{2,1,0:T(8,128)(2,1)S(1)} %bitcast.138), channel_id=1, replica_groups=mesh['s'=2,'xh'=2,'y'=4,'c'=2,'z'=4] {'xh','y'}, dimensions={0} | all-to-all | bytes 1572864 | tf_op jit(solution)/shard_map/all_to_all | solution.py:343
  169.5 16.5 %all_to_all.91 = bf16[8,64,768]{2,1,0:T(8,128)(2,1)S(1)} all-to-all(bf16[8,64,768]{2,1,0:T(8,128)(2,1)S(1)} %get-tuple-element.196), channel_id=1, replica_groups=mesh['s'=2,'xh'=2,'y'=4,'c'=2,'z'=4] {'xh','y'}, dimensions={0} | all-to-all | bytes 1572864 | tf_op jit(solution)/shard_map/all_to_all | solution.py:343
  186.0 2.3 collective-permute-done.17
  189.1 11.3 %shard_map.242 = (bf16[512,768]{1,0:T(8,128)(2,1)}, bf16[512,768]{1,0:T(8,128)(2,1)}, bf16[1024,192]{1,0:T(8,128)(2,1)}, f32[1024,192]{1,0:T(8,128)}, bf16[1024,256]{1,0:T(8,128)(2,1)}) custom-call(s32[2]{0:T(128)} %pad_add_fusion.place, bf16[512,768]{1,0:T(8,128)(2,1)} %bitcast.144, bf16[512,768]{1,0:T(8,128)(2,1)} %bitcast.173, f32[8,768]{1,0:T(8,128)} %concatenate.82.vec, ...), custom_call_target="tpu_custom_call" | custom-call | flops 11000000512 | bytes 38500000 | tf_op jit(solution)/shard_map/pallas_call | solution.py:64
  200.6 2.4 collective-permute-done.18
  204.3 17.3 %all_to_all.92.got = bf16[8,64,768]{2,1,0:T(8,128)(2,1)S(1)} all-to-all(bf16[8,64,768]{2,1,0:T(8,128)(2,1)S(1)} %bitcast.139), channel_id=1, replica_groups=mesh['s'=2,'xh'=2,'y'=4,'c'=2,'z'=4] {'xh','y'}, dimensions={0} | all-to-all | bytes 1572864 | tf_op jit(solution)/shard_map/all_to_all | solution.py:343
  221.9 16.9 %all_to_all.93 = bf16[8,64,768]{2,1,0:T(8,128)(2,1)S(1)} all-to-all(bf16[8,64,768]{2,1,0:T(8,128)(2,1)S(1)} %get-tuple-element.203), channel_id=1, replica_groups=mesh['s'=2,'xh'=2,'y'=4,'c'=2,'z'=4] {'xh','y'}, dimensions={0} | all-to-all | bytes 1572864 | tf_op jit(solution)/shard_map/all_to_all | solution.py:343
  238.8 2.3 collective-permute-done.19
  242.0 11.1 %shard_map.244 = (bf16[512,768]{1,0:T(8,128)(2,1)}, bf16[512,768]{1,0:T(8,128)(2,1)}, bf16[1024,192]{1,0:T(8,128)(2,1)}, f32[1024,192]{1,0:T(8,128)}, bf16[1024,256]{1,0:T(8,128)(2,1)}) custom-call(s32[2]{0:T(128)} %pad_add_fusion.place, bf16[512,768]{1,0:T(8,128)(2,1)} %bitcast.151, bf16[512,768]{1,0:T(8,128)(2,1)} %bitcast.178, f32[8,768]{1,0:T(8,128)} %concatenate.83.vec, ...), custom_call_target="tpu_custom_call" | custom-call | flops 11000000512 | bytes 38500000 | tf_op jit(solution)/shard_map/pallas_call | solution.py:64
  257.8 3.5 all-to-all-start.8
  262.3 13.6 %shard_map.245 = (bf16[512,768]{1,0:T(8,128)(2,1)}, bf16[512,768]{1,0:T(8,128)(2,1)}, bf16[1024,192]{1,0:T(8,128)(2,1)}, bf16[1024,192]{1,0:T(8,128)(2,1)}, f32[8,768]{1,0:T(8,128)}) custom-call(s32[2]{0:T(128)} %pad_add_fusion.place, bf16[512,768]{1,0:T(8,128)(2,1)} %bitcast.35.b_own, bf16[512,768]{1,0:T(8,128)(2,1)} %bitcast.183, ...), custom_call_target="tpu_custom_call" | custom-call | flops 12999999488 | bytes 45500000 | tf_op jit(solution)/shard_map/pallas_call | solution.py:64
  276.1 2.4 collective-permute-done.22
  280.7 7.1 %all-to-all-start.9 = ((bf16[8,64,768]{2,1,0:T(8,128)(2,1)}), bf16[8,64,768]{2,1,0:T(8,128)(2,1)S(1)}, u32[]{:S(2)}, u32[]{:S(2)}) async-start(bf16[8,64,768]{2,1,0:T(8,128)(2,1)} %bitcast.37), calls=%async_computation.9 | async-start | bytes 1572864 | tf_op jit(solution)/shard_map/all_to_all | solution.py:343
  287.8 6.1 %shard_map.246 = bf16[4,432,384]{2,1,0:T(8,128)(2,1)} custom-call(bf16[512,768]{1,0:T(8,128)(2,1)} %bitcast.35.b_own, bf16[512,768]{1,0:T(8,128)(2,1)} %bitcast.184, bf16[512,768]{1,0:T(8,128)(2,1)} %bitcast.153, bf16[512,768]{1,0:T(8,128)(2,1)} %bitcast.180, f32[8,768]{1,0:T(8,128)} %concatenate.83.vec, bf16[1024,256]{1,0:T(8,128)(2,1)} %get-tuple-element.215.act, ...), custom_call_target="tpu_custom_call" | custom-call | flops 6000000000 | bytes 21000000 | tf_op jit(solution)/shard_map/pallas_call | solution.py:64
  293.9 7.6 %all-to-all-done.9.got = bf16[8,64,768]{2,1,0:T(8,128)(2,1)S(1)} async-done(((bf16[8,64,768]{2,1,0:T(8,128)(2,1)}), bf16[8,64,768]{2,1,0:T(8,128)(2,1)S(1)}, u32[]{:S(2)}, u32[]{:S(2)}) %all-to-all-start.9) | async-done | bytes 786464 | tf_op jit(solution)/shard_map/all_to_all | solution.py:343
  302.7 3.7 all-to-all-start.10
  309.8 9.8 %collective-permute-done.23 = bf16[432,384]{1,0:T(8,128)(2,1)S(1)} collective-permute-done((bf16[432,384]{1,0:T(8,128)(2,1)S(1)}, bf16[432,384]{1,0:T(8,128)(2,1)S(1)}, u32[]{:S(2)}, u32[]{:S(2)}) %collective-permute-start.23) | collective-permute-done | bytes 331808 | tf_op jit(solution)/shard_map/ppermute | solution.py:36
  323.2 13.8 %shard_map.248 = (bf16[512,768]{1,0:T(8,128)(2,1)}, bf16[512,768]{1,0:T(8,128)(2,1)}, bf16[1024,192]{1,0:T(8,128)(2,1)}, bf16[1024,192]{1,0:T(8,128)(2,1)}, f32[8,768]{1,0:T(8,128)}) custom-call(s32[2]{0:T(128)} %pad_add_fusion.place, bf16[512,768]{1,0:T(8,128)(2,1)} %bitcast.147, bf16[512,768]{1,0:T(8,128)(2,1)} %bitcast.185, bf16[512,768]{1,0:T(8,128)(2,1)} %bitcast.145, ...), custom_call_target="tpu_custom_call" | custom-call | flops 12999999488 | bytes 45500000 | tf_op jit(solution)/shard_map/pallas_call | solution.py:64
  337.3 2.4 collective-permute-done.27
  341.8 6.6 %all-to-all-start.11 = ((bf16[8,64,768]{2,1,0:T(8,128)(2,1)}), bf16[8,64,768]{2,1,0:T(8,128)(2,1)S(1)}, u32[]{:S(2)}, u32[]{:S(2)}) async-start(bf16[8,64,768]{2,1,0:T(8,128)(2,1)} %bitcast.44), calls=%async_computation.11 | async-start | bytes 1572864 | tf_op jit(solution)/shard_map/all_to_all | solution.py:343
  348.5 6.1 %shard_map.249 = bf16[4,432,384]{2,1,0:T(8,128)(2,1)} custom-call(bf16[512,768]{1,0:T(8,128)(2,1)} %bitcast.148, bf16[512,768]{1,0:T(8,128)(2,1)} %bitcast.186, bf16[512,768]{1,0:T(8,128)(2,1)} %bitcast.146, bf16[512,768]{1,0:T(8,128)(2,1)} %bitcast.175, f32[8,768]{1,0:T(8,128)} %concatenate.82.vec, bf16[1024,256]{1,0:T(8,128)(2,1)} %get-tuple-element.231.act, ...), custom_call_target="tpu_custom_call" | custom-call | flops 6000000000 | bytes 21000000 | tf_op jit(solution)/shard_map/pallas_call | solution.py:64
  354.5 7.6 %all-to-all-done.11.got = bf16[8,64,768]{2,1,0:T(8,128)(2,1)S(1)} async-done(((bf16[8,64,768]{2,1,0:T(8,128)(2,1)}), bf16[8,64,768]{2,1,0:T(8,128)(2,1)S(1)}, u32[]{:S(2)}, u32[]{:S(2)}) %all-to-all-start.11) | async-done | bytes 786464 | tf_op jit(solution)/shard_map/all_to_all | solution.py:343
  363.4 3.7 all-to-all-start.12
  367.1 2.3 dynamic-slice_bitcast_fusion.7
  370.5 9.8 %collective-permute-done.28 = bf16[432,384]{1,0:T(8,128)(2,1)S(1)} collective-permute-done((bf16[432,384]{1,0:T(8,128)(2,1)S(1)}, bf16[432,384]{1,0:T(8,128)(2,1)S(1)}, u32[]{:S(2)}, u32[]{:S(2)}) %collective-permute-start.28) | collective-permute-done | bytes 331808 | tf_op jit(solution)/shard_map/ppermute | solution.py:36
  383.9 13.5 %shard_map.251 = (bf16[512,768]{1,0:T(8,128)(2,1)}, bf16[512,768]{1,0:T(8,128)(2,1)}, bf16[1024,192]{1,0:T(8,128)(2,1)}, bf16[1024,192]{1,0:T(8,128)(2,1)}, f32[8,768]{1,0:T(8,128)}) custom-call(s32[2]{0:T(128)} %pad_add_fusion.place, bf16[512,768]{1,0:T(8,128)(2,1)} %bitcast.149, bf16[512,768]{1,0:T(8,128)(2,1)} %bitcast.181, bf16[512,768]{1,0:T(8,128)(2,1)} %bitcast.142, ...), custom_call_target="tpu_custom_call" | custom-call | flops 12999999488 | bytes 45500000 | tf_op jit(solution)/shard_map/pallas_call | solution.py:64
  397.7 2.4 collective-permute-done.32
  402.2 6.7 %all-to-all-start.13 = ((bf16[8,64,768]{2,1,0:T(8,128)(2,1)}), bf16[8,64,768]{2,1,0:T(8,128)(2,1)S(1)}, u32[]{:S(2)}, u32[]{:S(2)}) async-start(bf16[8,64,768]{2,1,0:T(8,128)(2,1)} %bitcast.51), calls=%async_computation.13 | async-start | bytes 1572864 | tf_op jit(solution)/shard_map/all_to_all | solution.py:343
  408.9 6.1 %shard_map.252 = bf16[4,432,384]{2,1,0:T(8,128)(2,1)} custom-call(bf16[512,768]{1,0:T(8,128)(2,1)} %bitcast.150, bf16[512,768]{1,0:T(8,128)(2,1)} %bitcast.182, bf16[512,768]{1,0:T(8,128)(2,1)} %bitcast.143, bf16[512,768]{1,0:T(8,128)(2,1)} %bitcast.172, f32[8,768]{1,0:T(8,128)} %concatenate.81.vec, bf16[1024,256]{1,0:T(8,128)(2,1)} %get-tuple-element.247.act, ...), custom_call_target="tpu_custom_call" | custom-call | flops 6000000000 | bytes 21000000 | tf_op jit(solution)/shard_map/pallas_call | solution.py:64
  414.9 7.6 %all-to-all-done.13.got = bf16[8,64,768]{2,1,0:T(8,128)(2,1)S(1)} async-done(((bf16[8,64,768]{2,1,0:T(8,128)(2,1)}), bf16[8,64,768]{2,1,0:T(8,128)(2,1)S(1)}, u32[]{:S(2)}, u32[]{:S(2)}) %all-to-all-start.13) | async-done | bytes 786464 | tf_op jit(solution)/shard_map/all_to_all | solution.py:343
  424.4 4.3 all-to-all-start.14
  430.9 9.4 %collective-permute-done.33 = bf16[432,384]{1,0:T(8,128)(2,1)S(1)} collective-permute-done((bf16[432,384]{1,0:T(8,128)(2,1)S(1)}, bf16[432,384]{1,0:T(8,128)(2,1)S(1)}, u32[]{:S(2)}, u32[]{:S(2)}) %collective-permute-start.33) | collective-permute-done | bytes 331808 | tf_op jit(solution)/shard_map/ppermute | solution.py:36
  442.0 2.7 collective-permute-start.36
  445.6 13.5 %shard_map.254 = (bf16[512,768]{1,0:T(8,128)(2,1)}, bf16[512,768]{1,0:T(8,128)(2,1)}, bf16[1024,192]{1,0:T(8,128)(2,1)}, bf16[1024,192]{1,0:T(8,128)(2,1)}, f32[8,768]{1,0:T(8,128)}) custom-call(s32[2]{0:T(128)} %pad_add_fusion.place, bf16[512,768]{1,0:T(8,128)(2,1)} %bitcast.53.b_own, bf16[512,768]{1,0:T(8,128)(2,1)} %bitcast.176, ...), custom_call_target="tpu_custom_call" | custom-call | flops 12999999488 | bytes 45500000 | tf_op jit(solution)/shard_map/pallas_call | solution.py:64
  462.8 5.2 all-to-all-start.15
  468.1 6.1 %shard_map.255 = bf16[4,432,384]{2,1,0:T(8,128)(2,1)} custom-call(bf16[512,768]{1,0:T(8,128)(2,1)} %bitcast.53.b_own, bf16[512,768]{1,0:T(8,128)(2,1)} %bitcast.177, bf16[512,768]{1,0:T(8,128)(2,1)} %bitcast.19.own.n_own, bf16[512,768]{1,0:T(8,128)(2,1)} %bitcast.169, f32[8,768]{1,0:T(8,128)} %concatenate.80.vec, bf16[1024,256]{1,0:T(8,128)(2,1)} %get-tuple-element.263.act, ...), custom_call_target="tpu_custom_call" | custom-call | flops 6000000000 | bytes 21000000 | tf_op jit(solution)/shard_map/pallas_call | solution.py:64
  474.2 7.5 %all-to-all-done.15.got = bf16[8,64,768]{2,1,0:T(8,128)(2,1)S(1)} async-done(((bf16[8,64,768]{2,1,0:T(8,128)(2,1)}), bf16[8,64,768]{2,1,0:T(8,128)(2,1)S(1)}, u32[]{:S(2)}, u32[]{:S(2)}) %all-to-all-start.15) | async-done | bytes 786464 | tf_op jit(solution)/shard_map/all_to_all | solution.py:343
  483.6 3.8 all-to-all-start.16
  488.8 3.2 collective-permute-start.41
  493.5 6.2 %collective-permute-done.39 = bf16[432,384]{1,0:T(8,128)(2,1)S(1)} collective-permute-done((bf16[432,384]{1,0:T(8,128)(2,1)S(1)}, bf16[432,384]{1,0:T(8,128)(2,1)S(1)}, u32[]{:S(2)}, u32[]{:S(2)}) %collective-permute-start.39) | collective-permute-done | bytes 331808 | tf_op jit(solution)/shard_map/ppermute | solution.py:36
  499.8 6.4 %collective-permute-done.41 = bf16[432,384]{1,0:T(8,128)(2,1)S(1)} collective-permute-done((bf16[432,384]{1,0:T(8,128)(2,1)S(1)}, bf16[432,384]{1,0:T(8,128)(2,1)S(1)}, u32[]{:S(2)}, u32[]{:S(2)}) %collective-permute-start.41) | collective-permute-done | bytes 331808 | tf_op jit(solution)/shard_map/ppermute | solution.py:36
  511.4 12.2 %collective-permute-done.42 = bf16[432,384]{1,0:T(8,128)(2,1)S(1)} collective-permute-done((bf16[432,384]{1,0:T(8,128)(2,1)S(1)}, bf16[432,384]{1,0:T(8,128)(2,1)S(1)}, u32[]{:S(2)}, u32[]{:S(2)}) %collective-permute-start.42) | collective-permute-done | bytes 331808 | tf_op jit(solution)/shard_map/ppermute | solution.py:36
  524.5 2.8 broadcast_in_dim.38
  527.2 7.6 %all-to-all-start.17 = ((bf16[8,432,384]{2,1,0:T(8,128)(2,1)}), bf16[8,432,384]{2,1,0:T(8,128)(2,1)}, u32[]{:S(2)}, u32[]{:S(2)}) async-start(bf16[8,432,384]{2,1,0:T(8,128)(2,1)} %broadcast_in_dim.38), calls=%async_computation.17 | async-start | bytes 5308416 | tf_op jit(solution)/shard_map/all_to_all | solution.py:343
  538.8 6.1 %shard_map.258 = (f32[2,192,2304]{2,1,0:T(8,128)}, f32[2,192,768]{2,1,0:T(8,128)}, f32[2,192,3072]{2,1,0:T(8,128)}, f32[2,768,768]{2,1,0:T(8,128)}, f32[2,16,16,384]{3,2,1,0:T(8,128)S(1)}) custom-call(s32[2]{0:T(128)S(1)} %pad_add_fusion.1.place, bf16[8,432,384]{2,1,0:T(8,128)(2,1)S(1)} %all-to-all-done.16.own, ...), custom_call_target="tpu_custom_call" | custom-call | flops 7000000000 | bytes 24500000 | tf_op jit(solution)/shard_map/pallas_call | solution.py:310
  545.8 23.9 %collective-permute-done.44 = f32[64,768]{1,0:T(8,128)S(1)} collective-permute-done((f32[64,768]{1,0:T(8,128)S(1)}, f32[64,768]{1,0:T(8,128)S(1)}, u32[]{:S(2)}, u32[]{:S(2)}) %collective-permute-start.44) | collective-permute-done | bytes 196640 | tf_op jit(solution)/shard_map/ppermute | solution.py:36
  572.2 2.7 collective-permute-done.45.other
  578.2 6.2 %shard_map.259 = (f32[2,192,2304]{2,1,0:T(8,128)}, f32[2,192,768]{2,1,0:T(8,128)}, f32[2,192,3072]{2,1,0:T(8,128)}, f32[2,768,768]{2,1,0:T(8,128)}, f32[2,16,16,384]{3,2,1,0:T(8,128)S(1)}) custom-call(s32[2]{0:T(128)S(1)} %pad_add_fusion.1.place, ...), custom_call_target="tpu_custom_call", output_to_operand_aliasing={{0}: (3, {}), {1}: (4, {}), {2}: (5, {}), {3}: (6, {}), {4}... | custom-call | flops 7000000000 | bytes 24500000 | tf_op jit(solution)/shard_map/pallas_call | solution.py:310
  (338 shorter events, 112.4 us)
Async XLA Ops:
  1.8 7.3 %collective-permute-start = (bf16[64,768]{1,0:T(8,128)(2,1)S(1)}, bf16[64,768]{1,0:T(8,128)(2,1)S(1)}, u32[]{:S(2)}, u32[]{:S(2)}) collective-permute-start(bf16[64,768]{1,0:T(8,128)(2,1)S(1)} %select_bitcast_fusion.4), channel_id=1, source_target_pairs={{0,64},{64,0},{1,65},{65,1},{2,66},{66,2},{3,67},{67,3},{4,68},{68... | collective-permute-start | bytes 294920 | tf_op jit(solution)/shard_map/ppermute | solution.py:36
  8.3 9.0 %collective-permute-start.1 = (bf16[416,384]{1,0:T(8,128)(2,1)S(1)}, bf16[416,384]{1,0:T(8,128)(2,1)S(1)}, u32[]{:S(2)}, u32[]{:S(2)}) collective-permute-start(bf16[416,384]{1,0:T(8,128)(2,1)S(1)} %get-tuple-element.420), channel_id=1, source_target_pairs={{0,64},{64,0},{1,65},{65,1},{2,66},{66,2},{3,67},{67,3},{4,68},{68... | collective-permute-start | bytes 958472 | tf_op jit(solution)/shard_map/ppermute | solution.py:36
  9.2 80.5 %copy-start.9 = (f32[64,768]{1,0:T(8,128)}, f32[64,768]{1,0:T(8,128)S(1)}, u32[]{:S(2)}) copy-start(f32[64,768]{1,0:T(8,128)S(1)} %get-tuple-element.423.x) | copy-start | bytes 589828
  10.3 38.4 %all-to-all-start = ((bf16[8,64,768]{2,1,0:T(8,128)(2,1)}), bf16[8,64,768]{2,1,0:T(8,128)(2,1)}, u32[]{:S(2)}, u32[]{:S(2)}) async-start(bf16[8,64,768]{2,1,0:T(8,128)(2,1)} %shard_map.237), calls=%async_computation | async-start | bytes 1572864 | tf_op jit(solution)/shard_map/all_to_all | solution.py:343
  18.6 8.0 %collective-permute-start.2 = (bf16[2,2496]{1,0:T(2,128)(2,1)S(1)}, bf16[2,2496]{1,0:T(2,128)(2,1)S(1)}, u32[]{:S(2)}, u32[]{:S(2)}) collective-permute-start(bf16[2,2496]{1,0:T(2,128)(2,1)S(1)} %concatenate.78), channel_id=1, source_target_pairs={{0,64},{64,0},{1,65},{65,1},{2,66},{66,2},{3,67},{67,3},{4,68},{68... | collective-permute-start | bytes 29960 | tf_op jit(solution)/shard_map/ppermute | solution.py:36
  20.2 28.5 %collective-permute-start.8 = (bf16[1,416,384]{2,1,0:T(8,128)(2,1)}, bf16[1,416,384]{2,1,0:T(8,128)(2,1)}, u32[]{:S(2)}, u32[]{:S(2)}) collective-permute-start(bf16[1,416,384]{2,1,0:T(8,128)(2,1)} %bitcast.18.s0), channel_id=1, source_target_pairs={{0,3},{1,0},{2,1},{3,2},{4,7},{5,4},{6,5},{7,6},{8,11},{9,8},{10,9... | collective-permute-start | bytes 958472 | tf_op jit(solution)/shard_map/ppermute | solution.py:36
  24.3 24.4 %collective-permute-start.7 = (bf16[1,416,384]{2,1,0:T(8,128)(2,1)}, bf16[1,416,384]{2,1,0:T(8,128)(2,1)}, u32[]{:S(2)}, u32[]{:S(2)}) collective-permute-start(bf16[1,416,384]{2,1,0:T(8,128)(2,1)} %bitcast.18.s0), channel_id=1, source_target_pairs={{0,2},{1,3},{2,0},{3,1},{4,6},{5,7},{6,4},{7,5},{8,10},{9,11},{10,... | collective-permute-start | bytes 958472 | tf_op jit(solution)/shard_map/ppermute | solution.py:36
  26.7 12.7 %collective-permute-start.5 = (bf16[4,2496]{1,0:T(4,128)(2,1)S(1)}, bf16[4,2496]{1,0:T(4,128)(2,1)S(1)}, u32[]{:S(2)}, u32[]{:S(2)}) collective-permute-start(bf16[4,2496]{1,0:T(4,128)(2,1)S(1)} %pad_maximum_fusion.3), channel_id=1, source_target_pairs={{0,3},{1,0},{2,1},{3,2},{4,7},{5,4},{6,5},{7,6},{8,11},{9,8},{10,9... | collective-permute-start | bytes 59912 | tf_op jit(solution)/shard_map/ppermute | solution.py:36
  30.8 10.8 %collective-permute-start.4 = (bf16[4,2496]{1,0:T(4,128)(2,1)S(1)}, bf16[4,2496]{1,0:T(4,128)(2,1)S(1)}, u32[]{:S(2)}, u32[]{:S(2)}) collective-permute-start(bf16[4,2496]{1,0:T(4,128)(2,1)S(1)} %pad_maximum_fusion.3), channel_id=1, source_target_pairs={{0,2},{1,3},{2,0},{3,1},{4,6},{5,7},{6,4},{7,5},{8,10},{9,11},{10,... | collective-permute-start | bytes 59912 | tf_op jit(solution)/shard_map/ppermute | solution.py:36
  30.8 10.8 %collective-permute-start.3 = (bf16[4,2496]{1,0:T(4,128)(2,1)S(1)}, bf16[4,2496]{1,0:T(4,128)(2,1)S(1)}, u32[]{:S(2)}, u32[]{:S(2)}) collective-permute-start(bf16[4,2496]{1,0:T(4,128)(2,1)S(1)} %pad_maximum_fusion.3), channel_id=1, source_target_pairs={{0,1},{1,2},{2,3},{3,0},{4,5},{5,6},{6,7},{7,4},{8,9},{9,10},{10,1... | collective-permute-start | bytes 59912 | tf_op jit(solution)/shard_map/ppermute | solution.py:36
  39.3 9.3 %collective-permute-start.6 = (bf16[1,416,384]{2,1,0:T(8,128)(2,1)}, bf16[1,416,384]{2,1,0:T(8,128)(2,1)S(1)}, u32[]{:S(2)}, u32[]{:S(2)}) collective-permute-start(bf16[1,416,384]{2,1,0:T(8,128)(2,1)} %bitcast.18.s0), channel_id=1, source_target_pairs={{0,1},{1,2},{2,3},{3,0},{4,5},{5,6},{6,7},{7,4},{8,9},{9,10},{10,1... | collective-permute-start | bytes 958472 | tf_op jit(solution)/shard_map/ppermute | solution.py:36
  48.7 2.6 collective-permute-start.9
  63.5 2.5 collective-permute-start.10
  63.6 12.4 %collective-permute-start.11 = (bf16[416,384]{1,0:T(8,128)(2,1)S(1)}, bf16[416,384]{1,0:T(8,128)(2,1)S(1)}, u32[]{:S(2)}, u32[]{:S(2)}) collective-permute-start(bf16[416,384]{1,0:T(8,128)(2,1)S(1)} %copy-done.21), channel_id=1, source_target_pairs={{0,64},{64,0},{1,65},{65,1},{2,66},{66,2},{3,67},{67,3},{4,68},{68... | collective-permute-start | bytes 958472 | tf_op jit(solution)/shard_map/ppermute | solution.py:36
  68.2 21.5 %all-to-all-start.1 = ((bf16[8,64,768]{2,1,0:T(8,128)(2,1)}), bf16[8,64,768]{2,1,0:T(8,128)(2,1)S(1)}, u32[]{:S(2)}, u32[]{:S(2)}) async-start(bf16[8,64,768]{2,1,0:T(8,128)(2,1)} %bitcast.21), calls=%async_computation.1 | async-start | bytes 1572864 | tf_op jit(solution)/shard_map/all_to_all | solution.py:343
  76.2 24.2 %collective-permute-start.14 = (bf16[3,416,384]{2,1,0:T(8,128)(2,1)S(1)}, bf16[3,416,384]{2,1,0:T(8,128)(2,1)S(1)}, u32[]{:S(2)}, u32[]{:S(2)}) collective-permute-start(bf16[3,416,384]{2,1,0:T(8,128)(2,1)S(1)} %pad_maximum_fusion.s0), channel_id=1, source_target_pairs={{0,3},{1,0},{2,1},{3,2},{4,7},{5,4},{6,5},{7,6},{8,11},{9,8},{10,9... | collective-permute-start | bytes 2875400 | tf_op jit(solution)/shard_map/ppermute | solution.py:36
  77.3 25.8 %collective-permute-start.13 = (bf16[3,416,384]{2,1,0:T(8,128)(2,1)S(1)}, bf16[3,416,384]{2,1,0:T(8,128)(2,1)}, u32[]{:S(2)}, u32[]{:S(2)}) collective-permute-start(bf16[3,416,384]{2,1,0:T(8,128)(2,1)S(1)} %pad_maximum_fusion.s0), channel_id=1, source_target_pairs={{0,2},{1,3},{2,0},{3,1},{4,6},{5,7},{6,4},{7,5},{8,10},{9,11},{10,... | collective-permute-start | bytes 2875400 | tf_op jit(solution)/shard_map/ppermute | solution.py:36
  78.3 43.8 %collective-permute-start.12 = (bf16[3,416,384]{2,1,0:T(8,128)(2,1)S(1)}, bf16[3,416,384]{2,1,0:T(8,128)(2,1)}, u32[]{:S(2)}, u32[]{:S(2)}) collective-permute-start(bf16[3,416,384]{2,1,0:T(8,128)(2,1)S(1)} %pad_maximum_fusion.s0), channel_id=1, source_target_pairs={{0,1},{1,2},{2,3},{3,0},{4,5},{5,6},{6,7},{7,4},{8,9},{9,10},{10,1... | collective-permute-start | bytes 2875400 | tf_op jit(solution)/shard_map/ppermute | solution.py:36
  90.8 31.3 %all-to-all-start.2 = ((bf16[8,64,768]{2,1,0:T(8,128)(2,1)}), bf16[8,64,768]{2,1,0:T(8,128)(2,1)S(1)}, u32[]{:S(2)}, u32[]{:S(2)}) async-start(bf16[8,64,768]{2,1,0:T(8,128)(2,1)} %get-tuple-element.179), calls=%async_computation.2 | async-start | bytes 1572864 | tf_op jit(solution)/shard_map/all_to_all | solution.py:343
  100.4 32.0 %copy-start.54 = (bf16[3,416,384]{2,1,0:T(8,128)(2,1)}, bf16[3,416,384]{2,1,0:T(8,128)(2,1)S(1)}, u32[]{:S(2)}) copy-start(bf16[3,416,384]{2,1,0:T(8,128)(2,1)S(1)} %collective-permute-done.14.s3) | copy-start | bytes 2875396
  122.1 2.3 collective-permute-start.15
  125.5 20.7 %all-to-all-start.3 = ((bf16[8,64,768]{2,1,0:T(8,128)(2,1)}), bf16[8,64,768]{2,1,0:T(8,128)(2,1)}, u32[]{:S(2)}, u32[]{:S(2)}) async-start(bf16[8,64,768]{2,1,0:T(8,128)(2,1)} %broadcast_in_dim.36), calls=%async_computation.3 | async-start | bytes 1572864 | tf_op jit(solution)/shard_map/all_to_all | solution.py:343
  146.2 2.5 collective-permute-start.16
  186.0 2.3 collective-permute-start.17
  200.4 2.5 collective-permute-start.18
  221.9 79.6 %copy-start.15 = (f32[64,768]{1,0:T(8,128)}, f32[64,768]{1,0:T(8,128)S(1)}, u32[]{:S(2)}) copy-start(f32[64,768]{1,0:T(8,128)S(1)} %get-tuple-element.220.x) | copy-start | bytes 589828
  238.8 2.3 collective-permute-start.19
  253.1 2.5 collective-permute-start.20
  253.2 8.1 %collective-permute-start.21 = (bf16[8,64,768]{2,1,0:T(8,128)(2,1)}, bf16[8,64,768]{2,1,0:T(8,128)(2,1)S(1)}, u32[]{:S(2)}, u32[]{:S(2)}) collective-permute-start(bf16[8,64,768]{2,1,0:T(8,128)(2,1)} %all-to-all-done.3), channel_id=1, source_target_pairs={{0,4},{4,0},{1,5},{5,1},{2,6},{6,2},{3,7},{7,3},{8,12},{12,8},{9,1... | collective-permute-start | bytes 2359304 | tf_op jit(solution)/shard_map/ppermute | solution.py:36
  257.8 18.1 %all-to-all-start.8 = ((bf16[8,64,768]{2,1,0:T(8,128)(2,1)}), bf16[8,64,768]{2,1,0:T(8,128)(2,1)S(1)}, u32[]{:S(2)}, u32[]{:S(2)}) async-start(bf16[8,64,768]{2,1,0:T(8,128)(2,1)} %bitcast.34), calls=%async_computation.8 | async-start | bytes 1572864 | tf_op jit(solution)/shard_map/all_to_all | solution.py:343
  275.9 2.6 collective-permute-start.22
  280.7 20.8 %all-to-all-start.9 = ((bf16[8,64,768]{2,1,0:T(8,128)(2,1)}), bf16[8,64,768]{2,1,0:T(8,128)(2,1)S(1)}, u32[]{:S(2)}, u32[]{:S(2)}) async-start(bf16[8,64,768]{2,1,0:T(8,128)(2,1)} %bitcast.37), calls=%async_computation.9 | async-start | bytes 1572864 | tf_op jit(solution)/shard_map/all_to_all | solution.py:343
  302.7 17.3 %all-to-all-start.10 = ((bf16[8,64,768]{2,1,0:T(8,128)(2,1)}), bf16[8,64,768]{2,1,0:T(8,128)(2,1)S(1)}, u32[]{:S(2)}, u32[]{:S(2)}) async-start(bf16[8,64,768]{2,1,0:T(8,128)(2,1)} %get-tuple-element.221), calls=%async_computation.10 | async-start | bytes 1572864 | tf_op jit(solution)/shard_map/all_to_all | solution.py:343
  308.7 10.9 %collective-permute-start.23 = (bf16[432,384]{1,0:T(8,128)(2,1)S(1)}, bf16[432,384]{1,0:T(8,128)(2,1)S(1)}, u32[]{:S(2)}, u32[]{:S(2)}) collective-permute-start(bf16[432,384]{1,0:T(8,128)(2,1)S(1)} %get-tuple-element.414), channel_id=1, source_target_pairs={{0,2},{1,3},{2,0},{3,1},{4,6},{5,7},{6,4},{7,5},{8,10},{9,11},{10,... | collective-permute-start | bytes 995336 | tf_op jit(solution)/shard_map/ppermute | solution.py:36
  320.1 2.3 collective-permute-start.24
  320.1 16.9 %collective-permute-start.26 = (bf16[432,384]{1,0:T(8,128)(2,1)}, bf16[432,384]{1,0:T(8,128)(2,1)S(1)}, u32[]{:S(2)}, u32[]{:S(2)}) collective-permute-start(bf16[432,384]{1,0:T(8,128)(2,1)} %get-tuple-element.411), channel_id=1, source_target_pairs={{0,3},{1,0},{2,1},{3,2},{4,7},{5,4},{6,5},{7,6},{8,11},{9,8},{10,9... | collective-permute-start | bytes 995336 | tf_op jit(solution)/shard_map/ppermute | solution.py:36
  320.7 16.3 %collective-permute-start.25 = (bf16[432,384]{1,0:T(8,128)(2,1)}, bf16[432,384]{1,0:T(8,128)(2,1)S(1)}, u32[]{:S(2)}, u32[]{:S(2)}) collective-permute-start(bf16[432,384]{1,0:T(8,128)(2,1)} %get-tuple-element.412), channel_id=1, source_target_pairs={{0,1},{1,2},{2,3},{3,0},{4,5},{5,6},{6,7},{7,4},{8,9},{9,10},{10,1... | collective-permute-start | bytes 995336 | tf_op jit(solution)/shard_map/ppermute | solution.py:36
  337.0 2.6 collective-permute-start.27
  341.8 20.3 %all-to-all-start.11 = ((bf16[8,64,768]{2,1,0:T(8,128)(2,1)}), bf16[8,64,768]{2,1,0:T(8,128)(2,1)S(1)}, u32[]{:S(2)}, u32[]{:S(2)}) async-start(bf16[8,64,768]{2,1,0:T(8,128)(2,1)} %bitcast.44), calls=%async_computation.11 | async-start | bytes 1572864 | tf_op jit(solution)/shard_map/all_to_all | solution.py:343
  363.4 17.3 %all-to-all-start.12 = ((bf16[8,64,768]{2,1,0:T(8,128)(2,1)}), bf16[8,64,768]{2,1,0:T(8,128)(2,1)S(1)}, u32[]{:S(2)}, u32[]{:S(2)}) async-start(bf16[8,64,768]{2,1,0:T(8,128)(2,1)} %get-tuple-element.237), calls=%async_computation.12 | async-start | bytes 1572864 | tf_op jit(solution)/shard_map/all_to_all | solution.py:343
  369.4 10.9 %collective-permute-start.28 = (bf16[432,384]{1,0:T(8,128)(2,1)S(1)}, bf16[432,384]{1,0:T(8,128)(2,1)S(1)}, u32[]{:S(2)}, u32[]{:S(2)}) collective-permute-start(bf16[432,384]{1,0:T(8,128)(2,1)S(1)} %get-tuple-element.410), channel_id=1, source_target_pairs={{0,2},{1,3},{2,0},{3,1},{4,6},{5,7},{6,4},{7,5},{8,10},{9,11},{10,... | collective-permute-start | bytes 995336 | tf_op jit(solution)/shard_map/ppermute | solution.py:36
  380.7 2.3 collective-permute-start.29
  380.7 16.7 %collective-permute-start.31 = (bf16[432,384]{1,0:T(8,128)(2,1)}, bf16[432,384]{1,0:T(8,128)(2,1)S(1)}, u32[]{:S(2)}, u32[]{:S(2)}) collective-permute-start(bf16[432,384]{1,0:T(8,128)(2,1)} %get-tuple-element.407), channel_id=1, source_target_pairs={{0,3},{1,0},{2,1},{3,2},{4,7},{5,4},{6,5},{7,6},{8,11},{9,8},{10,9... | collective-permute-start | bytes 995336 | tf_op jit(solution)/shard_map/ppermute | solution.py:36
  382.3 15.1 %collective-permute-start.30 = (bf16[432,384]{1,0:T(8,128)(2,1)}, bf16[432,384]{1,0:T(8,128)(2,1)S(1)}, u32[]{:S(2)}, u32[]{:S(2)}) collective-permute-start(bf16[432,384]{1,0:T(8,128)(2,1)} %get-tuple-element.408), channel_id=1, source_target_pairs={{0,1},{1,2},{2,3},{3,0},{4,5},{5,6},{6,7},{7,4},{8,9},{9,10},{10,1... | collective-permute-start | bytes 995336 | tf_op jit(solution)/shard_map/ppermute | solution.py:36
  397.5 2.6 collective-permute-start.32
  402.2 20.3 %all-to-all-start.13 = ((bf16[8,64,768]{2,1,0:T(8,128)(2,1)}), bf16[8,64,768]{2,1,0:T(8,128)(2,1)S(1)}, u32[]{:S(2)}, u32[]{:S(2)}) async-start(bf16[8,64,768]{2,1,0:T(8,128)(2,1)} %bitcast.51), calls=%async_computation.13 | async-start | bytes 1572864 | tf_op jit(solution)/shard_map/all_to_all | solution.py:343
  424.4 17.5 %all-to-all-start.14 = ((bf16[8,64,768]{2,1,0:T(8,128)(2,1)}), bf16[8,64,768]{2,1,0:T(8,128)(2,1)}, u32[]{:S(2)}, u32[]{:S(2)}) async-start(bf16[8,64,768]{2,1,0:T(8,128)(2,1)} %get-tuple-element.253), calls=%async_computation.14 | async-start | bytes 1572864 | tf_op jit(solution)/shard_map/all_to_all | solution.py:343
  429.8 10.5 %collective-permute-start.33 = (bf16[432,384]{1,0:T(8,128)(2,1)S(1)}, bf16[432,384]{1,0:T(8,128)(2,1)S(1)}, u32[]{:S(2)}, u32[]{:S(2)}) collective-permute-start(bf16[432,384]{1,0:T(8,128)(2,1)S(1)} %get-tuple-element.406), channel_id=1, source_target_pairs={{0,2},{1,3},{2,0},{3,1},{4,6},{5,7},{6,4},{7,5},{8,10},{9,11},{10,... | collective-permute-start | bytes 995336 | tf_op jit(solution)/shard_map/ppermute | solution.py:36
  442.0 2.7 collective-permute-start.34
  442.0 17.2 %collective-permute-start.36 = (bf16[432,384]{1,0:T(8,128)(2,1)}, bf16[432,384]{1,0:T(8,128)(2,1)S(1)}, u32[]{:S(2)}, u32[]{:S(2)}) collective-permute-start(bf16[432,384]{1,0:T(8,128)(2,1)} %get-tuple-element.403), channel_id=1, source_target_pairs={{0,3},{1,0},{2,1},{3,2},{4,7},{5,4},{6,5},{7,6},{8,11},{9,8},{10,9... | collective-permute-start | bytes 995336 | tf_op jit(solution)/shard_map/ppermute | solution.py:36
  444.7 14.4 %collective-permute-start.35 = (bf16[432,384]{1,0:T(8,128)(2,1)}, bf16[432,384]{1,0:T(8,128)(2,1)S(1)}, u32[]{:S(2)}, u32[]{:S(2)}) collective-permute-start(bf16[432,384]{1,0:T(8,128)(2,1)} %get-tuple-element.404), channel_id=1, source_target_pairs={{0,1},{1,2},{2,3},{3,0},{4,5},{5,6},{6,7},{7,4},{8,9},{9,10},{10,1... | collective-permute-start | bytes 995336 | tf_op jit(solution)/shard_map/ppermute | solution.py:36
  459.2 2.6 collective-permute-start.37
  460.6 13.5 %collective-permute-start.38 = (bf16[432,384]{1,0:T(8,128)(2,1)}, bf16[432,384]{1,0:T(8,128)(2,1)S(1)}, u32[]{:S(2)}, u32[]{:S(2)}) collective-permute-start(bf16[432,384]{1,0:T(8,128)(2,1)} %get-tuple-element.386), channel_id=1, source_target_pairs={{0,64},{64,0},{1,65},{65,1},{2,66},{66,2},{3,67},{67,3},{4,68},{68... | collective-permute-start | bytes 995336 | tf_op jit(solution)/shard_map/ppermute | solution.py:36
  462.8 19.0 %all-to-all-start.15 = ((bf16[8,64,768]{2,1,0:T(8,128)(2,1)}), bf16[8,64,768]{2,1,0:T(8,128)(2,1)S(1)}, u32[]{:S(2)}, u32[]{:S(2)}) async-start(bf16[8,64,768]{2,1,0:T(8,128)(2,1)} %bitcast.58), calls=%async_computation.15 | async-start | bytes 1572864 | tf_op jit(solution)/shard_map/all_to_all | solution.py:343
  483.6 40.9 %all-to-all-start.16 = ((bf16[8,432,384]{2,1,0:T(8,128)(2,1)}), bf16[8,432,384]{2,1,0:T(8,128)(2,1)S(1)}, u32[]{:S(2)}, u32[]{:S(2)}) async-start(bf16[8,432,384]{2,1,0:T(8,128)(2,1)} %broadcast_in_dim.37), calls=%async_computation.16 | async-start | bytes 5308416 | tf_op jit(solution)/shard_map/all_to_all | solution.py:343
  488.8 11.0 %collective-permute-start.39 = (bf16[432,384]{1,0:T(8,128)(2,1)S(1)}, bf16[432,384]{1,0:T(8,128)(2,1)S(1)}, u32[]{:S(2)}, u32[]{:S(2)}) collective-permute-start(bf16[432,384]{1,0:T(8,128)(2,1)S(1)} %get-tuple-element.400), channel_id=1, source_target_pairs={{0,1},{1,2},{2,3},{3,0},{4,5},{5,6},{6,7},{7,4},{8,9},{9,10},{10,1... | collective-permute-start | bytes 995336 | tf_op jit(solution)/shard_map/ppermute | solution.py:36
  488.8 17.3 %collective-permute-start.41 = (bf16[432,384]{1,0:T(8,128)(2,1)S(1)}, bf16[432,384]{1,0:T(8,128)(2,1)S(1)}, u32[]{:S(2)}, u32[]{:S(2)}) collective-permute-start(bf16[432,384]{1,0:T(8,128)(2,1)S(1)} %get-tuple-element.401), channel_id=1, source_target_pairs={{0,3},{1,0},{2,1},{3,2},{4,7},{5,4},{6,5},{7,6},{8,11},{9,8},{10,9... | collective-permute-start | bytes 995336 | tf_op jit(solution)/shard_map/ppermute | solution.py:36
  492.1 15.9 %collective-permute-start.40 = (bf16[432,384]{1,0:T(8,128)(2,1)S(1)}, bf16[432,384]{1,0:T(8,128)(2,1)S(1)}, u32[]{:S(2)}, u32[]{:S(2)}) collective-permute-start(bf16[432,384]{1,0:T(8,128)(2,1)S(1)} %get-tuple-element.402), channel_id=1, source_target_pairs={{0,2},{1,3},{2,0},{3,1},{4,6},{5,7},{6,4},{7,5},{8,10},{9,11},{10,... | collective-permute-start | bytes 995336 | tf_op jit(solution)/shard_map/ppermute | solution.py:36
  509.4 14.2 %collective-permute-start.42 = (bf16[432,384]{1,0:T(8,128)(2,1)S(1)}, bf16[432,384]{1,0:T(8,128)(2,1)S(1)}, u32[]{:S(2)}, u32[]{:S(2)}) collective-permute-start(bf16[432,384]{1,0:T(8,128)(2,1)S(1)} %get-tuple-element.383), channel_id=1, source_target_pairs={{0,64},{64,0},{1,65},{65,1},{2,66},{66,2},{3,67},{67,3},{4,68},{68... | collective-permute-start | bytes 995336 | tf_op jit(solution)/shard_map/ppermute | solution.py:36
  524.4 14.4 %collective-permute-start.43 = (bf16[8,432,384]{2,1,0:T(8,128)(2,1)S(1)}, bf16[8,432,384]{2,1,0:T(8,128)(2,1)}, u32[]{:S(2)}, u32[]{:S(2)}) collective-permute-start(bf16[8,432,384]{2,1,0:T(8,128)(2,1)S(1)} %all-to-all-done.16.own), channel_id=1, source_target_pairs={{0,4},{4,0},{1,5},{5,1},{2,6},{6,2},{3,7},{7,3},{8,12},{12,8},{9,1... | collective-permute-start | bytes 7962632 | tf_op jit(solution)/shard_map/ppermute | solution.py:36
  527.2 42.5 %all-to-all-start.17 = ((bf16[8,432,384]{2,1,0:T(8,128)(2,1)}), bf16[8,432,384]{2,1,0:T(8,128)(2,1)}, u32[]{:S(2)}, u32[]{:S(2)}) async-start(bf16[8,432,384]{2,1,0:T(8,128)(2,1)} %broadcast_in_dim.38), calls=%async_computation.17 | async-start | bytes 5308416 | tf_op jit(solution)/shard_map/all_to_all | solution.py:343
  537.6 32.7 %copy-start.6 = (f32[64,768]{1,0:T(8,128)S(1)}, f32[64,768]{1,0:T(8,128)}, u32[]{:S(2)}) copy-start(f32[64,768]{1,0:T(8,128)} %copy-done.4) | copy-start | bytes 589828
  537.7 32.0 %collective-permute-start.44 = (f32[64,768]{1,0:T(8,128)S(1)}, f32[64,768]{1,0:T(8,128)S(1)}, u32[]{:S(2)}, u32[]{:S(2)}) collective-permute-start(f32[64,768]{1,0:T(8,128)S(1)} %broadcast_select_fusion.5), channel_id=1, source_target_pairs={{0,64},{64,0},{1,65},{65,1},{2,66},{66,2},{3,67},{67,3},{4,68},{68... | collective-permute-start | bytes 589832 | tf_op jit(solution)/shard_map/ppermute | solution.py:36
  569.7 5.2 collective-permute-start.45
  (60 other events, 399.2 us)

commit v3 on v2

--- a/solution.py
+++ b/solution.py
@@ -24,6 +24,7 @@
 SEQ = 1024
 HALF = SEQ // 2
 BLOCK = 256
+BLK = 32
 UNITS = 192
 SHARE = 416
 PACK = 432
@@ -113,33 +114,38 @@
         branch_out[k] = branch
 
 
-def share_weights(place, pieces, w_qkv, w_up, w_down, w_out):
+def share_weights(place, pieces, w_qkv, w_up, w_both):
     for k, piece in enumerate(pieces):
         at = lax.rem(place[0] + (4 - k), 4)
         w_qkv[pl.ds(pl.multiple_of(at * 192, 64), 192), :] = piece[0:192, 0:192]
         w_up[pl.ds(pl.multiple_of(at * 192, 64), 192), :] = piece[0:192, 192:384]
-        w_down[pl.ds(pl.multiple_of(at * 48, 16), 48), 0:384] = piece[192:240, :]
-        w_down[pl.ds(pl.multiple_of(at * 48, 16), 48), 384:768] = piece[304:352, :]
+        w_both[pl.ds(pl.multiple_of(at * 48, 16), 48), 0:384] = piece[192:240, :]
+        w_both[pl.ds(pl.multiple_of(at * 48, 16), 48), 384:768] = piece[304:352, :]
 
         @pl.when(at == place[1])
         def _():
-            w_out[:, 0:384] = piece[240:304, :]
-            w_out[:, 384:768] = piece[352:416, :]
-
-
-WEIGHT_SCRATCH = (
-    VMEM((D, UNITS), BF),
-    VMEM((D, UNITS), BF),
-    VMEM((UNITS, D), BF),
-    VMEM((HD, D), BF),
-)
-
-
-def scored(q, k, query_places, key_places):
+            w_both[192:256, 0:384] = piece[240:304, :]
+            w_both[192:256, 384:768] = piece[352:416, :]
+
+
+WEIGHT_SCRATCH = (VMEM((D, UNITS), BF), VMEM((D, UNITS), BF), VMEM((UNITS + HD, D), BF))
+
+
+def scored(tile, q, k):
     scores = dot(q * SCORE_SCALE, k, 1, 1)
-    scores = jnp.where(query_places >= key_places, scores, -1e30)
-    raised = jnp.exp(scores - jnp.max(scores, -1, keepdims=True))
+    row = lax.broadcasted_iota(jnp.int32, (BLOCK, BLOCK), 0)
+    column = lax.broadcasted_iota(jnp.int32, (BLOCK, BLOCK), 1)
+    last = jnp.where(row >= column, scores[:, tile * BLOCK :], -1e30)
+    if tile:
+        last = jnp.concatenate([scores[:, : tile * BLOCK], last], 1)
+    raised = jnp.exp(last - jnp.max(last, -1, keepdims=True))
     return raised * (1.0 / jnp.sum(raised, -1, keepdims=True))
+
+
+def spots(order, half, step):
+    for i in range(BLOCK // BLK):
+        at = order[half * (HALF // BLK) + step * (BLOCK // BLK) + i]
+        yield i * BLK, pl.ds(pl.multiple_of(at * BLK, BLK), BLK)
 
 
 def turn(v, tables, rows, sign):
@@ -150,11 +156,11 @@
 
 
 def forward_kernel(
-    place, own, other, vec, bias, s0, s1, s2, s3, cosine, ahead, behind, p_col, p_row,
+    place, order, own, other, vec, bias, s0, s1, s2, s3, cosine, ahead, behind,
     part_own, part_other, qkv, pre, act,
-    w_qkv, w_up, w_down, w_out,
+    w_qkv, w_up, w_both, att,
 ):
-    share_weights(place, (s0, s1, s2, s3), w_qkv, w_up, w_down, w_out)
+    share_weights(place, (s0, s1, s2, s3), w_qkv, w_up, w_both)
     tables = (cosine, ahead, behind)
     for half, source in enumerate((own, other)):
 
@@ -166,37 +172,38 @@
             one = (n * vec[0:1, :] + vec[1:2, :]).astype(BF)
             two = (n * vec[2:3, :] + vec[3:4, :]).astype(BF)
             merged = dot(one, w_qkv[...]) + bias[0:1, 0:192]
-            qkv[rows, 0:128] = turn(merged[:, 0:128], tables, rows, 1.0).astype(BF)
-            qkv[rows, 128:192] = merged[:, 128:192].astype(BF)
+            qk = turn(merged[:, 0:128], tables, rows, 1.0).astype(BF)
+            v = merged[:, 128:192].astype(BF)
+            for at, spot in spots(order, half, step):
+                qkv[spot, 0:128] = qk[at : at + BLK, :]
+                qkv[spot, 128:192] = v[at : at + BLK, :]
             up = dot(two, w_up[...]) + bias[1:2, 0:192]
             pre[rows, :] = up
             act[rows, 0:192] = (0.5 * up * (1.0 + lax.erf(up * 0.7071067811865476))).astype(BF)
 
-    k, v = qkv[:, 64:128], qkv[:, 128:192]
+    for tile in range(SEQ // BLOCK):
+        start, end = tile * BLOCK, (tile + 1) * BLOCK
+        probs = scored(tile, qkv[start:end, 0:64], qkv[0:end, 64:128]).astype(BF)
+        att[start:end, :] = dot(probs, qkv[0:end, 128:192]).astype(BF)
+
     for half, target in enumerate((part_own, part_other)):
 
         @pl.loop(0, HALF // BLOCK)
         def _(step):
-            here = pl.ds(step * BLOCK, BLOCK)
             rows = pl.ds(half * HALF + step * BLOCK, BLOCK)
-            probs = scored(qkv[rows, 0:64], k, p_col[rows, :], p_row[...]).astype(BF)
-            attended = dot(probs, v).astype(BF)
+            attended = jnp.concatenate([att[spot, :] for _, spot in spots(order, half, step)], 0)
             act[rows, 192:256] = attended
-            part = dot(attended, w_out[...]) + dot(act[rows, 0:192], w_down[...])
-            target[here, :] = part.astype(BF)
+            target[pl.ds(step * BLOCK, BLOCK), :] = dot(act[rows, :], w_both[...]).astype(BF)
 
 
 def backward_kernel(
-    place, b_own, b_other, n_own, n_other, vec, s0, s1, s2, s3, cosine, ahead, behind, p_col, p_row, qkv, pre,
+    place, order, b_own, b_other, n_own, n_other, vec, s0, s1, s2, s3, cosine, ahead, behind, qkv, pre,
     gy_own, gy_other, d_qkv, d_up, sums,
-    w_qkv, w_up, w_down, w_out, dq, dk, dv,
+    w_qkv, w_up, w_both, dq, dk, dv, grad,
 ):
-    share_weights(place, (s0, s1, s2, s3), w_qkv, w_up, w_down, w_out)
+    share_weights(place, (s0, s1, s2, s3), w_qkv, w_up, w_both)
     tables = (cosine, ahead, behind)
-    dk[...] = jnp.zeros_like(dk)
-    dv[...] = jnp.zeros_like(dv)
     sums[...] = jnp.zeros_like(sums)
-    k, v = qkv[:, 64:128], qkv[:, 128:192]
     for half, source in enumerate((b_own, b_other)):
 
         @pl.loop(0, HALF // BLOCK)
@@ -204,21 +211,32 @@
             rows = pl.ds(half * HALF + step * BLOCK, BLOCK)
             branch = source[pl.ds(step * BLOCK, BLOCK), :]
             sums[5:6, :] += jnp.sum(branch.astype(F32), 0, keepdims=True)
-            hidden = dot(branch, w_down[...], 1, 1)
+            both = dot(branch, w_both[...], 1, 1)
             up = pre[rows, :]
             slope = 0.5 * (1.0 + lax.erf(up * 0.7071067811865476)) + up * (
                 jnp.exp(-0.5 * up * up) * 0.3989422804014327
             )
-            d_up[rows, :] = (slope * hidden).astype(BF)
-            grad = dot(branch, w_out[...], 1, 1).astype(BF)
-            q = qkv[rows, 0:64]
-            probs = scored(q, k, p_col[rows, :], p_row[...])
-            prob_grad = dot(grad, v, 1, 1)
-            inner = jnp.sum(probs * prob_grad, -1, keepdims=True)
-            score_grad = (probs * (prob_grad - inner)).astype(BF)
-            dq[rows, :] = dot(score_grad, k)
-            dk[...] += dot(score_grad, q, 0, 0)
-            dv[...] += dot(probs.astype(BF), grad, 0, 0)
+            d_up[rows, :] = (slope * both[:, 0:192]).astype(BF)
+            head = both[:, 192:256].astype(BF)
+            for at, spot in spots(order, half, step):
+                grad[spot, :] = head[at : at + BLK, :]
+
+    for tile in reversed(range(SEQ // BLOCK)):
+        start, end = tile * BLOCK, (tile + 1) * BLOCK
+        q, k, v = qkv[start:end, 0:64], qkv[0:end, 64:128], qkv[0:end, 128:192]
+        out = grad[start:end, :]
+        probs = scored(tile, q, k)
+        prob_grad = dot(out, v, 1, 1)
+        inner = jnp.sum(probs * prob_grad, -1, keepdims=True)
+        score_grad = (probs * (prob_grad - inner)).astype(BF)
+        dq[start:end, :] = dot(score_grad, k)
+        k_part, v_part = dot(score_grad, q, 0, 0), dot(probs.astype(BF), out, 0, 0)
+        if end == SEQ:
+            dk[...] = k_part
+            dv[...] = v_part
+        else:
+            dk[0:end, :] += k_part
+            dv[0:end, :] += v_part
 
     for half, (source, target) in enumerate(((n_own, gy_own), (n_other, gy_other))):
 
@@ -226,9 +244,12 @@
         def _(step):
             here = pl.ds(step * BLOCK, BLOCK)
             rows = pl.ds(half * HALF + step * BLOCK, BLOCK)
-            both = jnp.concatenate([dq[rows, :], dk[rows, :]], 1) * SCORE_SCALE
-            d_qkv[rows, 0:128] = turn(both, tables, rows, -1.0).astype(BF)
-            d_qkv[rows, 128:192] = dv[rows, :].astype(BF)
+            places = [spot for _, spot in spots(order, half, step)]
+            both = jnp.concatenate(
+                [jnp.concatenate([ref[spot, :] for spot in places], 0) for ref in (dq, dk)], 1
+            )
+            d_qkv[rows, 0:128] = turn(both * SCORE_SCALE, tables, rows, -1.0).astype(BF)
+            d_qkv[rows, 128:192] = jnp.concatenate([dv[spot, :] for spot in places], 0).astype(BF)
             g_qkv, g_up = d_qkv[rows, :], d_up[rows, :]
             one = dot(g_qkv, w_qkv[...], 1, 1)
             two = dot(g_up, w_up[...], 1, 1)
@@ -317,7 +338,7 @@
         ],
         input_output_aliases={3 + i: i for i in range(len(earlier))},
         cost_estimate=cost(7),
-        compiler_params=pltpu.CompilerParams(vmem_limit_bytes=40 * MIB),
+        compiler_params=pltpu.CompilerParams(vmem_limit_bytes=56 * MIB),
     )(place, own, other, *earlier)
 
 
@@ -361,7 +382,11 @@
     down = cut(wd, (zero, unit * 48, zero), (2, 48, D))
     out = cut(wo, (zero, (unit % 3) * HD, zero), (2, HD, D)) * mask
     rows = jnp.concatenate([down, out], 1)
-    shares = jnp.concatenate([jnp.concatenate(cols, 2), rows[..., :384], rows[..., 384:]], 1)
+    vectors = jnp.concatenate([g1, h1, g2, h2, bq, bo, bu, bd], 1)
+    vectors = jnp.pad(vectors, ((0, 0), (0, 16 * 384 - vectors.shape[1]))).reshape(2, 16, 384)
+    shares = jnp.concatenate(
+        [jnp.concatenate(cols, 2), rows[..., :384], rows[..., 384:], vectors], 1
+    )
 
     def joined_sections(mine):
         theirs = shifted(mine, "s", 1)
@@ -370,41 +395,33 @@
     def pieces_round_z(block):
         return [block] + [shifted(block, "z", k) for k in range(1, 4)]
 
-    def round_z(block):
-        pieces = pieces_round_z(block)
-        order = [pieces[0]] * 4
-        for at in range(4):
-            order[at] = jnp.where(
-                z == at,
-                pieces[0],
-                jnp.where(
-                    z == (at + 1) % 4, pieces[1], jnp.where(z == (at + 2) % 4, pieces[2], pieces[3])
-                ),
-            )
-        return jnp.stack(order)
+    def vectors_of(pieces):
+        parts = [piece[at, SHARE:] for piece, at in pieces]
+        ordered = []
+        for shard in range(4):
+            pick = parts[3]
+            for k in range(3):
+                pick = jnp.where(z == (shard + k) % 4, parts[k], pick)
+            ordered.append(pick.reshape(-1))
+        whole_vectors = jnp.stack(ordered)
+        at, members = 0, []
+        for width in (192, 192, 192, 192, 576, 192, 768, 192):
+            members.append(whole_vectors[:, at : at + width].reshape(1, -1).astype(F32))
+            at += width
+        head = [lax.dynamic_slice_in_dim(members[4], t * D + unit * HD, HD, 1) for t in range(3)]
+        units = [lax.dynamic_slice_in_dim(members[6], t * D + unit * 48, 48, 1) for t in range(4)]
+        return (
+            jnp.concatenate(members[:4] + [jnp.zeros((4, D), F32)], 0),
+            jnp.concatenate(
+                [jnp.concatenate(head, 1), jnp.concatenate(units, 1), jnp.zeros((6, UNITS), F32)], 0
+            ),
+            members[5] + members[7],
+        )
 
     early = joined_sections(shares[0])
     early = after(n_sent, early)
     layer_share = [[(piece, 0) for piece in pieces_round_z(early[0][None])]]
     later = joined_sections(after(early, shares[1]))
-
-    vectors = after(early, jnp.concatenate([g1, h1, g2, h2, bq, bo, bu, bd], 1))
-    vectors = round_z(jnp.concatenate(joined_sections(vectors), 0))
-    layer_vec, layer_bias, layer_add = [], [], []
-    for l in range(LAYERS):
-        at, members = 0, []
-        for width in (192, 192, 192, 192, 576, 192, 768, 192):
-            members.append(vectors[:, l, at : at + width].reshape(1, -1).astype(F32))
-            at += width
-        layer_vec.append(jnp.concatenate(members[:4] + [jnp.zeros((4, D), F32)], 0))
-        head = [lax.dynamic_slice_in_dim(members[4], t * D + unit * HD, HD, 1) for t in range(3)]
-        units = [lax.dynamic_slice_in_dim(members[6], t * D + unit * 48, 48, 1) for t in range(4)]
-        layer_bias.append(
-            jnp.concatenate(
-                [jnp.concatenate(head, 1), jnp.concatenate(units, 1), jnp.zeros((6, UNITS), F32)], 0
-            )
-        )
-        layer_add.append(members[5] + members[7])
 
     blk = ROWS // 2
     offsets = jnp.arange(SEQ, dtype=jnp.int32)
@@ -421,11 +438,14 @@
     cosine = jnp.concatenate([cos, cos, still + 1.0] * 2, 1)
     ahead = jnp.concatenate([-sin, none, still] * 2, 1)
     behind = jnp.concatenate([none, sin, still] * 2, 1)
-    tables = (cosine, ahead, behind, places[:, None], places[None, :])
-    own, (tables, layer_vec, layer_bias, layer_add, layer_share[0]) = exchanged(
-        n_sent, (tables, layer_vec, layer_bias, layer_add, [piece for piece, _ in layer_share[0]])
+    order = row_blocks.reshape(8, 2, 2)
+    order = jnp.where(c == 0, order, order[:, ::-1]).transpose(1, 0, 2).reshape(SEQ // BLK)
+    tables = (cosine, ahead, behind)
+    own, (tables, layer_share[0]) = exchanged(
+        n_sent, (tables, [piece for piece, _ in layer_share[0]])
     )
     layer_share[0] = [(piece, 0) for piece in layer_share[0]]
+    layer_vectors = [vectors_of(layer_share[0])]
     normals = both_cores(own)
     place = jnp.stack([z.astype(jnp.int32), owner])
 
@@ -434,8 +454,8 @@
         own, other, qkv, pre, act = call(
             forward_kernel,
             [((HALF, D), BF), ((HALF, D), BF), ((SEQ, UNITS), BF), ((SEQ, UNITS), F32), ((SEQ, 256), BF)],
-            place, *normals, layer_vec[l], layer_bias[l], *layer_share[l], *tables,
-            scratch=WEIGHT_SCRATCH, smem=1, room=56, takes=11,
+            place, order, *normals, layer_vectors[l][0], layer_vectors[l][1], *layer_share[l], *tables,
+            scratch=WEIGHT_SCRATCH + (VMEM((SEQ, HD), BF),), smem=2, room=56, takes=11,
         )
         if l == 1:
             sent = after(normals, jnp.broadcast_to(dx[None], (8, ROWS, D)))
@@ -443,15 +463,20 @@
             branches = both_cores(branches)
         kept.append((x, normals, qkv, pre, act))
         if l + 1 < LAYERS:
-            got = exchanged(halves_joined(own, other))
+            joined = halves_joined(own, other)
+            if l == 0:
+                block = jnp.stack([later[0], early[1], later[1]])
+                pieces = pieces_round_z(after(layer_share[0], block))
+                joined, pieces[1], pieces[3] = lax.optimization_barrier((joined, pieces[1], pieces[3]))
+            got = exchanged(joined)
             x, n_sent = call(
                 functools.partial(finish_kernel, l == 1),
-                [((ROWS, D), F32), ((8, ROWS, D), BF)], got, x, layer_add[l],
+                [((ROWS, D), F32), ((8, ROWS, D), BF)], got, x, layer_vectors[l][2],
             )
             if l == 0:
-                block = after(normals, jnp.stack([later[0], early[1], later[1]]))
-                own, pieces = exchanged(n_sent, pieces_round_z(block))
+                own, pieces = exchanged(n_sent, pieces)
                 layer_share += [[(piece, i) for piece in pieces] for i in range(3)]
+                layer_vectors += [vectors_of(share) for share in layer_share[1:]]
                 normals = both_cores(own)
             else:
                 normals = both_cores(exchanged(n_sent))
@@ -476,21 +501,21 @@
         own, other, d_qkv, d_up, sums = call(
             backward_kernel,
             [((HALF, D), BF), ((HALF, D), BF), ((SEQ, UNITS), BF), ((SEQ, UNITS), BF), ((8, D), F32)],
-            place, *branches, *normals, layer_vec[l], *layer_share[l], *tables, qkv, pre,
-            scratch=WEIGHT_SCRATCH + (VMEM((SEQ, HD), F32),) * 3, smem=1, room=56, takes=13,
+            place, order, *branches, *normals, layer_vectors[l][0], *layer_share[l], *tables, qkv, pre,
+            scratch=WEIGHT_SCRATCH + (VMEM((SEQ, HD), F32),) * 3 + (VMEM((SEQ, HD), BF),), smem=2, room=56, takes=13,
         )
         if l + 1 == LAYERS:
             got, (own, other) = exchanged(last, (own, other))
             final = call(
                 functools.partial(finish_kernel, False),
-                [((ROWS, D), F32), ((8, ROWS, D), BF)], got, x, layer_add[l],
+                [((ROWS, D), F32), ((8, ROWS, D), BF)], got, x, layer_vectors[l][2],
             )[0]
         else:
             own, other, parts = lax.optimization_barrier((own, other, parts))
             shares[l + 1] = summed(parts)
         pack = call(
             product_kernel, [((4, PACK, 384), BF)],
-            *branches, *normals, layer_vec[l], act, d_qkv, d_up, sums,
+            *branches, *normals, layer_vectors[l][0], act, d_qkv, d_up, sums,
             scratch=(VMEM((D, UNITS), F32), VMEM((D, UNITS), F32), VMEM((256, D), F32)),
             room=56, takes=6,
         )[0]

time: 600 us -> 574 us (0.957)
  blocking collectives: 69.8 us -> 36.4 us
  waiting for transfers between devices: 182 us -> 197 us
  Pallas kernels: 145 us -> 135 us
  other arithmetic: 29.4 us -> 38.8 us
  local copies, waits for them, and re-layouts: 46.7 us -> 39.8 us
    all_to_all x4 -> x2, blocking collectives: 69.8 us -> 36.4 us  [exchanged(): got = lax.all_to_all(sent, CHIPS, 0, 0, tiled=True)]
    all_to_all x14 -> x16, waiting for transfers between devices: 46.2 us -> 79 us  [exchanged(): got = lax.all_to_all(sent, CHIPS, 0, 0, tiled=True)]
    ppermute x46 -> x42, waiting for transfers between devices: 136 us -> 118 us  [shifted(): lax.ppermute(block, axis, [(i, (i + distance) % size) for i in range(size)])]
    pallas_call x21, Pallas kernels: 132 us -> 121 us  [call(): pl.pallas_call(kernel, out_shape=[jax.ShapeDtypeStruct(shape, dtype) for...]
    unnamed x135 -> x104, local copies, waits for them, and re-layouts: 17.8 us -> 8.28 us
    ppermute x46 -> x42, starting transfers between devices: 37 us -> 33.1 us  [shifted(): lax.ppermute(block, axis, [(i, (i + distance) % size) for i in range(size)])]
    all_to_all x14 -> x16, starting transfers between devices: 77.9 us -> 81.7 us  [exchanged(): got = lax.all_to_all(sent, CHIPS, 0, 0, tiled=True)]
  transfers between devices with their start and end apart: 60 -> 58, of which waited for: 36 -> 41; matrix products, arithmetic and copies ran while one was open for 7% -> 8% of each run, Pallas kernels for 17% -> 19%
where the time goes in v3:
time: 574 us; the launch traced here: 564 us
  waiting for transfers between devices  197 us (34%)
  Pallas kernels  135 us (24%)
  starting transfers between devices  115 us (20%)
  local copies, waits for them, and re-layouts  39.8 us (7%)
  other arithmetic  38.8 us (7%)
  blocking collectives  36.4 us (6%)
    pallas_call x21, Pallas kernels, call(): pl.pallas_call(kernel, out_shape=[jax.ShapeDtypeStruct(shape, dtype) for...  121 us
    ppermute x42, waiting for transfers between devices, shifted(): lax.ppermute(block, axis, [(i, (i + distance) % size) for i in range(size)])  118 us
    all_to_all x16, starting transfers between devices, exchanged(): got = lax.all_to_all(sent, CHIPS, 0, 0, tiled=True)  81.7 us
    all_to_all x16, waiting for transfers between devices, exchanged(): got = lax.all_to_all(sent, CHIPS, 0, 0, tiled=True)  79 us
    all_to_all x2, blocking collectives, exchanged(): got = lax.all_to_all(sent, CHIPS, 0, 0, tiled=True)  36.4 us
    ppermute x42, starting transfers between devices, shifted(): lax.ppermute(block, axis, [(i, (i + distance) % size) for i in range(size)])  33.1 us
    add x8, other arithmetic, halves_joined(): return (own + shifted(other, 'c', 1)).reshape(8, ROWS, D)  16.5 us
    pallas_call x2, Pallas kernels, unpacked(): pl.pallas_call(unpack_kernel, grid=(1,), out_shape=[jax.ShapeDtypeStruct(...  14.1 us
  transfers between devices with their start and end apart: 58, of which 41 were waited for; matrix products, arithmetic and copies ran while one was open for 8% of the time, Pallas kernels for 19%

profile of v3, /device:TPU:0, one launch (start us, length us, event | category | flops | bytes accessed | tf_op | source)
XLA Modules:
  0.0 563.9 jit_solution(938520378164173052)
XLA Ops:
  11.5 7.1 %all-to-all-start = ((bf16[8,64,768]{2,1,0:T(8,128)(2,1)}), bf16[8,64,768]{2,1,0:T(8,128)(2,1)}, u32[]{:S(2)}, u32[]{:S(2)}) async-start(bf16[8,64,768]{2,1,0:T(8,128)(2,1)} %shard_map.237), calls=%async_computation | async-start | bytes 1572864 | tf_op jit(solution)/shard_map/all_to_all | solution.py:364
  19.5 4.0 collective-permute-start.4
  37.2 3.4 collective-permute-done.2.s1
  47.8 9.7 %shard_map.238 = (bf16[512,768]{1,0:T(8,128)(2,1)}, bf16[512,768]{1,0:T(8,128)(2,1)}, bf16[1024,192]{1,0:T(8,128)(2,1)}, f32[1024,192]{1,0:T(8,128)}, bf16[1024,256]{1,0:T(8,128)(2,1)}) custom-call(s32[2]{0:T(128)} %pad_add_fusion.place, s32[32]{0:T(128)} %reshape.1331.order, bf16[512,768]{1,0:T(8,128)(2,1)} %bitcast.8.own.n_own, ...), custom_call_target="tpu_custom_call" | custom-call | flops 11000000512 | bytes 38500000 | tf_op jit(solution)/shard_map/pallas_call | solution.py:65
  57.6 2.4 collective-permute-done.6
  65.5 6.9 %all-to-all-start.1 = ((bf16[8,64,768]{2,1,0:T(8,128)(2,1)}), bf16[8,64,768]{2,1,0:T(8,128)(2,1)S(1)}, u32[]{:S(2)}, u32[]{:S(2)}) async-start(bf16[8,64,768]{2,1,0:T(8,128)(2,1)} %bitcast.10), calls=%async_computation.1 | async-start | bytes 1572864 | tf_op jit(solution)/shard_map/all_to_all | solution.py:364
  73.5 10.6 %all-to-all-done.1.got = bf16[8,64,768]{2,1,0:T(8,128)(2,1)S(1)} async-done(((bf16[8,64,768]{2,1,0:T(8,128)(2,1)}), bf16[8,64,768]{2,1,0:T(8,128)(2,1)S(1)}, u32[]{:S(2)}, u32[]{:S(2)}) %all-to-all-start.1) | async-done | bytes 786464 | tf_op jit(solution)/shard_map/all_to_all | solution.py:364
  85.3 3.5 all-to-all-start.2
  88.8 6.7 %collective-permute-done.10.s2 = bf16[3,432,384]{2,1,0:T(8,128)(2,1)} collective-permute-done((bf16[3,432,384]{2,1,0:T(8,128)(2,1)S(1)}, bf16[3,432,384]{2,1,0:T(8,128)(2,1)}, u32[]{:S(2)}, u32[]{:S(2)}) %collective-permute-start.10) | collective-permute-done | bytes 995360 | tf_op jit(solution)/shard_map/ppermute | solution.py:37
  95.6 6.1 %all-to-all-done.2 = bf16[8,64,768]{2,1,0:T(8,128)(2,1)S(1)} async-done(((bf16[8,64,768]{2,1,0:T(8,128)(2,1)}), bf16[8,64,768]{2,1,0:T(8,128)(2,1)S(1)}, u32[]{:S(2)}, u32[]{:S(2)}) %all-to-all-start.2) | async-done | bytes 786464 | tf_op jit(solution)/shard_map/all_to_all | solution.py:364
  109.4 3.7 all-to-all-start.3
  113.2 9.5 %shard_map.240 = (bf16[512,768]{1,0:T(8,128)(2,1)}, bf16[512,768]{1,0:T(8,128)(2,1)}, bf16[1024,192]{1,0:T(8,128)(2,1)}, f32[1024,192]{1,0:T(8,128)}, bf16[1024,256]{1,0:T(8,128)(2,1)}) custom-call(s32[2]{0:T(128)} %pad_add_fusion.place, s32[32]{0:T(128)} %reshape.1331.order, bf16[512,768]{1,0:T(8,128)(2,1)} %bitcast.195, bf16[512,768]{1,0:T(8,128)(2,1)} %bitcast.294, ...), custom_call_target="tpu_custom_call" | custom-call | flops 11000000512 | bytes 38500000 | tf_op jit(solution)/shard_map/pallas_call | solution.py:65
  122.7 4.2 all-to-all-done.3
  126.9 2.5 collective-permute-done.12
  131.6 3.8 all-to-all-start.4
  135.6 13.5 %all-to-all-done.4.got = bf16[8,64,768]{2,1,0:T(8,128)(2,1)S(1)} async-done(((bf16[8,64,768]{2,1,0:T(8,128)(2,1)}), bf16[8,64,768]{2,1,0:T(8,128)(2,1)S(1)}, u32[]{:S(2)}, u32[]{:S(2)}) %all-to-all-start.4) | async-done | bytes 786464 | tf_op jit(solution)/shard_map/all_to_all | solution.py:364
  149.4 18.1 %all_to_all.90 = bf16[8,64,768]{2,1,0:T(8,128)(2,1)S(1)} all-to-all(bf16[8,64,768]{2,1,0:T(8,128)(2,1)S(1)} %get-tuple-element.178), channel_id=1, replica_groups=mesh['s'=2,'xh'=2,'y'=4,'c'=2,'z'=4] {'xh','y'}, dimensions={0} | all-to-all | bytes 1572864 | tf_op jit(solution)/shard_map/all_to_all | solution.py:364
  169.9 9.9 %shard_map.242 = (bf16[512,768]{1,0:T(8,128)(2,1)}, bf16[512,768]{1,0:T(8,128)(2,1)}, bf16[1024,192]{1,0:T(8,128)(2,1)}, f32[1024,192]{1,0:T(8,128)}, bf16[1024,256]{1,0:T(8,128)(2,1)}) custom-call(s32[2]{0:T(128)} %pad_add_fusion.place, s32[32]{0:T(128)} %reshape.1331.order, bf16[512,768]{1,0:T(8,128)(2,1)} %bitcast.198, ...), custom_call_target="tpu_custom_call" | custom-call | flops 11000000512 | bytes 38500000 | tf_op jit(solution)/shard_map/pallas_call | solution.py:65
  180.0 2.3 collective-permute-done.14
  184.5 3.5 all-to-all-start.6
  188.2 13.5 %all-to-all-done.6.got = bf16[8,64,768]{2,1,0:T(8,128)(2,1)S(1)} async-done(((bf16[8,64,768]{2,1,0:T(8,128)(2,1)}), bf16[8,64,768]{2,1,0:T(8,128)(2,1)S(1)}, u32[]{:S(2)}, u32[]{:S(2)}) %all-to-all-start.6) | async-done | bytes 786464 | tf_op jit(solution)/shard_map/all_to_all | solution.py:364
  202.0 18.3 %all_to_all.91 = bf16[8,64,768]{2,1,0:T(8,128)(2,1)S(1)} all-to-all(bf16[8,64,768]{2,1,0:T(8,128)(2,1)S(1)} %get-tuple-element.182), channel_id=1, replica_groups=mesh['s'=2,'xh'=2,'y'=4,'c'=2,'z'=4] {'xh','y'}, dimensions={0} | all-to-all | bytes 1572864 | tf_op jit(solution)/shard_map/all_to_all | solution.py:364
  222.7 9.5 %shard_map.244 = (bf16[512,768]{1,0:T(8,128)(2,1)}, bf16[512,768]{1,0:T(8,128)(2,1)}, bf16[1024,192]{1,0:T(8,128)(2,1)}, f32[1024,192]{1,0:T(8,128)}, bf16[1024,256]{1,0:T(8,128)(2,1)}) custom-call(s32[2]{0:T(128)} %pad_add_fusion.place, s32[32]{0:T(128)} %reshape.1331.order, bf16[512,768]{1,0:T(8,128)(2,1)} %bitcast.207, ...), custom_call_target="tpu_custom_call" | custom-call | flops 11000000512 | bytes 38500000 | tf_op jit(solution)/shard_map/pallas_call | solution.py:65
  237.0 3.5 all-to-all-start.8
  240.5 12.3 %shard_map.245 = (bf16[512,768]{1,0:T(8,128)(2,1)}, bf16[512,768]{1,0:T(8,128)(2,1)}, bf16[1024,192]{1,0:T(8,128)(2,1)}, bf16[1024,192]{1,0:T(8,128)(2,1)}, f32[8,768]{1,0:T(8,128)}) custom-call(s32[2]{0:T(128)} %pad_add_fusion.place, s32[32]{0:T(128)} %reshape.1331.order, bf16[512,768]{1,0:T(8,128)(2,1)} %bitcast.201, bf16[512,768]{1,0:T(8,128)(2,1)} %bitcast.25.b_other, ...), custom_call_target="tpu_custom_call" | custom-call | flops 12999999488 | bytes 45500000 | tf_op jit(solution)/shard_map/pallas_call | solution.py:65
  254.2 2.5 collective-permute-done.18
  258.9 5.9 %all-to-all-start.9 = ((bf16[8,64,768]{2,1,0:T(8,128)(2,1)}), bf16[8,64,768]{2,1,0:T(8,128)(2,1)S(1)}, u32[]{:S(2)}, u32[]{:S(2)}) async-start(bf16[8,64,768]{2,1,0:T(8,128)(2,1)} %bitcast.191), calls=%async_computation.9 | async-start | bytes 1572864 | tf_op jit(solution)/shard_map/all_to_all | solution.py:364
  264.8 6.1 %shard_map.246 = bf16[4,432,384]{2,1,0:T(8,128)(2,1)} custom-call(bf16[512,768]{1,0:T(8,128)(2,1)} %bitcast.202, bf16[512,768]{1,0:T(8,128)(2,1)} %bitcast.25.b_other, bf16[512,768]{1,0:T(8,128)(2,1)} %bitcast.209, bf16[512,768]{1,0:T(8,128)(2,1)} %bitcast.22.other.n_other, f32[8,768]{1,0:T(8,128)} %concatenate.88.vec, ...), custom_call_target="tpu_custom_call" | custom-call | flops 6000000000 | bytes 21000000 | tf_op jit(solution)/shard_map/pallas_call | solution.py:65
  270.8 7.6 %all-to-all-done.9.got = bf16[8,64,768]{2,1,0:T(8,128)(2,1)S(1)} async-done(((bf16[8,64,768]{2,1,0:T(8,128)(2,1)}), bf16[8,64,768]{2,1,0:T(8,128)(2,1)S(1)}, u32[]{:S(2)}, u32[]{:S(2)}) %all-to-all-start.9) | async-done | bytes 786464 | tf_op jit(solution)/shard_map/all_to_all | solution.py:364
  279.7 3.7 all-to-all-start.10
  283.4 2.2 dynamic-slice_bitcast_fusion.11
  287.7 8.9 %collective-permute-done.19 = bf16[432,384]{1,0:T(8,128)(2,1)S(1)} collective-permute-done((bf16[432,384]{1,0:T(8,128)(2,1)S(1)}, bf16[432,384]{1,0:T(8,128)(2,1)S(1)}, u32[]{:S(2)}, u32[]{:S(2)}) %collective-permute-start.19) | collective-permute-done | bytes 331808 | tf_op jit(solution)/shard_map/ppermute | solution.py:37
  300.2 12.3 %shard_map.248 = (bf16[512,768]{1,0:T(8,128)(2,1)}, bf16[512,768]{1,0:T(8,128)(2,1)}, bf16[1024,192]{1,0:T(8,128)(2,1)}, bf16[1024,192]{1,0:T(8,128)(2,1)}, f32[8,768]{1,0:T(8,128)}) custom-call(s32[2]{0:T(128)} %pad_add_fusion.place, s32[32]{0:T(128)} %reshape.1331.order, bf16[512,768]{1,0:T(8,128)(2,1)} %bitcast.203, bf16[512,768]{1,0:T(8,128)(2,1)} %bitcast.301, ...), custom_call_target="tpu_custom_call" | custom-call | flops 12999999488 | bytes 45500000 | tf_op jit(solution)/shard_map/pallas_call | solution.py:65
  312.7 2.4 collective-permute-done.23
  317.3 6.6 %all-to-all-start.11 = ((bf16[8,64,768]{2,1,0:T(8,128)(2,1)}), bf16[8,64,768]{2,1,0:T(8,128)(2,1)S(1)}, u32[]{:S(2)}, u32[]{:S(2)}) async-start(bf16[8,64,768]{2,1,0:T(8,128)(2,1)} %bitcast.192), calls=%async_computation.11 | async-start | bytes 1572864 | tf_op jit(solution)/shard_map/all_to_all | solution.py:364
  323.9 6.1 %shard_map.249 = bf16[4,432,384]{2,1,0:T(8,128)(2,1)} custom-call(bf16[512,768]{1,0:T(8,128)(2,1)} %bitcast.204, bf16[512,768]{1,0:T(8,128)(2,1)} %bitcast.302, bf16[512,768]{1,0:T(8,128)(2,1)} %bitcast.200, bf16[512,768]{1,0:T(8,128)(2,1)} %bitcast.19.other.n_other, f32[8,768]{1,0:T(8,128)} %concatenate.84.vec, bf16[1024,256]{1,0:T(8,128)(2,1)} %get-tuple-element.208.act, ...), custom_call_target="tpu_custom_call" | custom-call | flops 6000000000 | bytes 21000000 | tf_op jit(solution)/shard_map/pallas_call | solution.py:65
  330.0 7.6 %all-to-all-done.11.got = bf16[8,64,768]{2,1,0:T(8,128)(2,1)S(1)} async-done(((bf16[8,64,768]{2,1,0:T(8,128)(2,1)}), bf16[8,64,768]{2,1,0:T(8,128)(2,1)S(1)}, u32[]{:S(2)}, u32[]{:S(2)}) %all-to-all-start.11) | async-done | bytes 786464 | tf_op jit(solution)/shard_map/all_to_all | solution.py:364
  338.8 3.7 all-to-all-start.12
  342.6 2.3 dynamic-slice_bitcast_fusion.7
  346.9 8.9 %collective-permute-done.24 = bf16[432,384]{1,0:T(8,128)(2,1)S(1)} collective-permute-done((bf16[432,384]{1,0:T(8,128)(2,1)S(1)}, bf16[432,384]{1,0:T(8,128)(2,1)S(1)}, u32[]{:S(2)}, u32[]{:S(2)}) %collective-permute-start.24) | collective-permute-done | bytes 331808 | tf_op jit(solution)/shard_map/ppermute | solution.py:37
  356.2 2.3 collective-permute-start.27
  359.4 12.5 %shard_map.251 = (bf16[512,768]{1,0:T(8,128)(2,1)}, bf16[512,768]{1,0:T(8,128)(2,1)}, bf16[1024,192]{1,0:T(8,128)(2,1)}, bf16[1024,192]{1,0:T(8,128)(2,1)}, f32[8,768]{1,0:T(8,128)}) custom-call(s32[2]{0:T(128)} %pad_add_fusion.place, s32[32]{0:T(128)} %reshape.1331.order, bf16[512,768]{1,0:T(8,128)(2,1)} %bitcast.210, bf16[512,768]{1,0:T(8,128)(2,1)} %bitcast.299, ...), custom_call_target="tpu_custom_call" | custom-call | flops 12999999488 | bytes 45500000 | tf_op jit(solution)/shard_map/pallas_call | solution.py:65
  372.2 2.3 collective-permute-done.28
  376.7 6.7 %all-to-all-start.13 = ((bf16[8,64,768]{2,1,0:T(8,128)(2,1)}), bf16[8,64,768]{2,1,0:T(8,128)(2,1)S(1)}, u32[]{:S(2)}, u32[]{:S(2)}) async-start(bf16[8,64,768]{2,1,0:T(8,128)(2,1)} %bitcast.193), calls=%async_computation.13 | async-start | bytes 1572864 | tf_op jit(solution)/shard_map/all_to_all | solution.py:364
  383.4 6.1 %shard_map.252 = bf16[4,432,384]{2,1,0:T(8,128)(2,1)} custom-call(bf16[512,768]{1,0:T(8,128)(2,1)} %bitcast.211, bf16[512,768]{1,0:T(8,128)(2,1)} %bitcast.300, bf16[512,768]{1,0:T(8,128)(2,1)} %bitcast.197, bf16[512,768]{1,0:T(8,128)(2,1)} %bitcast.296, f32[8,768]{1,0:T(8,128)} %concatenate.80.vec, bf16[1024,256]{1,0:T(8,128)(2,1)} %get-tuple-element.224.act, ...), custom_call_target="tpu_custom_call" | custom-call | flops 6000000000 | bytes 21000000 | tf_op jit(solution)/shard_map/pallas_call | solution.py:65
  389.5 7.7 %all-to-all-done.13.got = bf16[8,64,768]{2,1,0:T(8,128)(2,1)S(1)} async-done(((bf16[8,64,768]{2,1,0:T(8,128)(2,1)}), bf16[8,64,768]{2,1,0:T(8,128)(2,1)S(1)}, u32[]{:S(2)}, u32[]{:S(2)}) %all-to-all-start.13) | async-done | bytes 786464 | tf_op jit(solution)/shard_map/all_to_all | solution.py:364
  398.3 3.7 all-to-all-start.14
  402.1 2.2 dynamic-slice_bitcast_fusion.3
  406.3 9.0 %collective-permute-done.29 = bf16[432,384]{1,0:T(8,128)(2,1)S(1)} collective-permute-done((bf16[432,384]{1,0:T(8,128)(2,1)S(1)}, bf16[432,384]{1,0:T(8,128)(2,1)S(1)}, u32[]{:S(2)}, u32[]{:S(2)}) %collective-permute-start.29) | collective-permute-done | bytes 331808 | tf_op jit(solution)/shard_map/ppermute | solution.py:37
  415.7 3.2 collective-permute-start.32
  419.8 12.4 %shard_map.254 = (bf16[512,768]{1,0:T(8,128)(2,1)}, bf16[512,768]{1,0:T(8,128)(2,1)}, bf16[1024,192]{1,0:T(8,128)(2,1)}, bf16[1024,192]{1,0:T(8,128)(2,1)}, f32[8,768]{1,0:T(8,128)}) custom-call(s32[2]{0:T(128)} %pad_add_fusion.place, s32[32]{0:T(128)} %reshape.1331.order, bf16[512,768]{1,0:T(8,128)(2,1)} %bitcast.205, bf16[512,768]{1,0:T(8,128)(2,1)} %bitcast.297, ...), custom_call_target="tpu_custom_call" | custom-call | flops 12999999488 | bytes 45500000 | tf_op jit(solution)/shard_map/pallas_call | solution.py:65
  435.8 6.8 %all-to-all-start.15 = ((bf16[8,64,768]{2,1,0:T(8,128)(2,1)}), bf16[8,64,768]{2,1,0:T(8,128)(2,1)S(1)}, u32[]{:S(2)}, u32[]{:S(2)}) async-start(bf16[8,64,768]{2,1,0:T(8,128)(2,1)} %bitcast.47), calls=%async_computation.15 | async-start | bytes 1572864 | tf_op jit(solution)/shard_map/all_to_all | solution.py:364
  442.7 6.1 %shard_map.255 = bf16[4,432,384]{2,1,0:T(8,128)(2,1)} custom-call(bf16[512,768]{1,0:T(8,128)(2,1)} %bitcast.206, bf16[512,768]{1,0:T(8,128)(2,1)} %bitcast.298, bf16[512,768]{1,0:T(8,128)(2,1)} %bitcast.8.own.n_own, bf16[512,768]{1,0:T(8,128)(2,1)} %bitcast.293, f32[8,768]{1,0:T(8,128)} %concatenate.76.vec, bf16[1024,256]{1,0:T(8,128)(2,1)} %get-tuple-element.240.act, ...), custom_call_target="tpu_custom_call" | custom-call | flops 6000000000 | bytes 21000000 | tf_op jit(solution)/shard_map/pallas_call | solution.py:65
  450.6 5.7 %all-to-all-done.15.got = bf16[8,64,768]{2,1,0:T(8,128)(2,1)S(1)} async-done(((bf16[8,64,768]{2,1,0:T(8,128)(2,1)}), bf16[8,64,768]{2,1,0:T(8,128)(2,1)S(1)}, u32[]{:S(2)}, u32[]{:S(2)}) %all-to-all-start.15) | async-done | bytes 786464 | tf_op jit(solution)/shard_map/all_to_all | solution.py:364
  458.0 4.4 all-to-all-start.16
  464.1 3.2 collective-permute-start.37
  468.6 6.4 %collective-permute-done.35 = bf16[432,384]{1,0:T(8,128)(2,1)S(1)} collective-permute-done((bf16[432,384]{1,0:T(8,128)(2,1)S(1)}, bf16[432,384]{1,0:T(8,128)(2,1)S(1)}, u32[]{:S(2)}, u32[]{:S(2)}) %collective-permute-start.35) | collective-permute-done | bytes 331808 | tf_op jit(solution)/shard_map/ppermute | solution.py:37
  475.0 5.7 %collective-permute-done.37 = bf16[432,384]{1,0:T(8,128)(2,1)S(1)} collective-permute-done((bf16[432,384]{1,0:T(8,128)(2,1)S(1)}, bf16[432,384]{1,0:T(8,128)(2,1)S(1)}, u32[]{:S(2)}, u32[]{:S(2)}) %collective-permute-start.37) | collective-permute-done | bytes 331808 | tf_op jit(solution)/shard_map/ppermute | solution.py:37
  485.8 13.0 %collective-permute-done.38 = bf16[432,384]{1,0:T(8,128)(2,1)S(1)} collective-permute-done((bf16[432,384]{1,0:T(8,128)(2,1)S(1)}, bf16[432,384]{1,0:T(8,128)(2,1)S(1)}, u32[]{:S(2)}, u32[]{:S(2)}) %collective-permute-start.38) | collective-permute-done | bytes 331808 | tf_op jit(solution)/shard_map/ppermute | solution.py:37
  500.8 7.7 %all-to-all-start.17 = ((bf16[8,432,384]{2,1,0:T(8,128)(2,1)}), bf16[8,432,384]{2,1,0:T(8,128)(2,1)}, u32[]{:S(2)}, u32[]{:S(2)}) async-start(bf16[8,432,384]{2,1,0:T(8,128)(2,1)} %broadcast_in_dim.38), calls=%async_computation.17 | async-start | bytes 5308416 | tf_op jit(solution)/shard_map/all_to_all | solution.py:364
  510.9 6.9 %shard_map.258 = (f32[2,192,2304]{2,1,0:T(8,128)}, f32[2,192,768]{2,1,0:T(8,128)}, f32[2,192,3072]{2,1,0:T(8,128)}, f32[2,768,768]{2,1,0:T(8,128)}, f32[2,16,16,384]{3,2,1,0:T(8,128)}) custom-call(s32[2]{0:T(128)} %pad_add_fusion.1.place, bf16[8,432,384]{2,1,0:T(8,128)(2,1)} %all-to-all-done.16.own, bf16[8,432,384]{2,1,0:T(8,128)(2,1)} %collective-permute-done.39.other), custom_call_target="tpu_custom_call" | custom-call | flops 7000000000 | bytes 24500000 | tf_op jit(solution)/shard_map/pallas_call | solution.py:331
  517.9 24.8 %collective-permute-done.40 = f32[64,768]{1,0:T(8,128)S(1)} collective-permute-done((f32[64,768]{1,0:T(8,128)S(1)}, f32[64,768]{1,0:T(8,128)S(1)}, u32[]{:S(2)}, u32[]{:S(2)}) %collective-permute-start.40) | collective-permute-done | bytes 196640 | tf_op jit(solution)/shard_map/ppermute | solution.py:37
  543.5 4.5 collective-permute-done.41.other
  547.9 7.1 %shard_map.259 = (f32[2,192,2304]{2,1,0:T(8,128)}, f32[2,192,768]{2,1,0:T(8,128)}, f32[2,192,3072]{2,1,0:T(8,128)}, f32[2,768,768]{2,1,0:T(8,128)}, f32[2,16,16,384]{3,2,1,0:T(8,128)}) custom-call(s32[2]{0:T(128)} %pad_add_fusion.1.place, ...), custom_call_target="tpu_custom_call", output_to_operand_aliasing={{0}: (3, {}), {1}: (4, {}), {2}: (5, {}), {3}: (6, {}), {4}... | custom-call | flops 7000000000 | bytes 24500000 | tf_op jit(solution)/shard_map/pallas_call | solution.py:331
  (316 shorter events, 116.1 us)
Async XLA Ops:
  1.8 8.5 %collective-permute-start = (bf16[64,768]{1,0:T(8,128)(2,1)S(1)}, bf16[64,768]{1,0:T(8,128)(2,1)S(1)}, u32[]{:S(2)}, u32[]{:S(2)}) collective-permute-start(bf16[64,768]{1,0:T(8,128)(2,1)S(1)} %select_bitcast_fusion.4), channel_id=1, source_target_pairs={{0,64},{64,0},{1,65},{65,1},{2,66},{66,2},{3,67},{67,3},{4,68},{68... | collective-permute-start | bytes 294920 | tf_op jit(solution)/shard_map/ppermute | solution.py:37
  9.2 9.4 %collective-permute-start.1 = (bf16[432,384]{1,0:T(8,128)(2,1)S(1)}, bf16[432,384]{1,0:T(8,128)(2,1)S(1)}, u32[]{:S(2)}, u32[]{:S(2)}) collective-permute-start(bf16[432,384]{1,0:T(8,128)(2,1)S(1)} %get-tuple-element.385), channel_id=1, source_target_pairs={{0,64},{64,0},{1,65},{65,1},{2,66},{66,2},{3,67},{67,3},{4,68},{68... | collective-permute-start | bytes 995336 | tf_op jit(solution)/shard_map/ppermute | solution.py:37
  11.5 29.2 %all-to-all-start = ((bf16[8,64,768]{2,1,0:T(8,128)(2,1)}), bf16[8,64,768]{2,1,0:T(8,128)(2,1)}, u32[]{:S(2)}, u32[]{:S(2)}) async-start(bf16[8,64,768]{2,1,0:T(8,128)(2,1)} %shard_map.237), calls=%async_computation | async-start | bytes 1572864 | tf_op jit(solution)/shard_map/all_to_all | solution.py:364
  19.5 17.7 %collective-permute-start.4 = (bf16[1,432,384]{2,1,0:T(8,128)(2,1)}, bf16[1,432,384]{2,1,0:T(8,128)(2,1)}, u32[]{:S(2)}, u32[]{:S(2)}) collective-permute-start(bf16[1,432,384]{2,1,0:T(8,128)(2,1)} %bitcast.7.s0), channel_id=1, source_target_pairs={{0,3},{1,0},{2,1},{3,2},{4,7},{5,4},{6,5},{7,6},{8,11},{9,8},{10,9... | collective-permute-start | bytes 995336 | tf_op jit(solution)/shard_map/ppermute | solution.py:37
  23.6 13.6 %collective-permute-start.3 = (bf16[1,432,384]{2,1,0:T(8,128)(2,1)}, bf16[1,432,384]{2,1,0:T(8,128)(2,1)}, u32[]{:S(2)}, u32[]{:S(2)}) collective-permute-start(bf16[1,432,384]{2,1,0:T(8,128)(2,1)} %bitcast.7.s0), channel_id=1, source_target_pairs={{0,2},{1,3},{2,0},{3,1},{4,6},{5,7},{6,4},{7,5},{8,10},{9,11},{10,... | collective-permute-start | bytes 995336 | tf_op jit(solution)/shard_map/ppermute | solution.py:37
  23.6 17.1 %collective-permute-start.2 = (bf16[1,432,384]{2,1,0:T(8,128)(2,1)}, bf16[1,432,384]{2,1,0:T(8,128)(2,1)}, u32[]{:S(2)}, u32[]{:S(2)}) collective-permute-start(bf16[1,432,384]{2,1,0:T(8,128)(2,1)} %bitcast.7.s0), channel_id=1, source_target_pairs={{0,1},{1,2},{2,3},{3,0},{4,5},{5,6},{6,7},{7,4},{8,9},{9,10},{10,1... | collective-permute-start | bytes 995336 | tf_op jit(solution)/shard_map/ppermute | solution.py:37
  25.2 9.7 %collective-permute-start.7 = (bf16[432,384]{1,0:T(8,128)(2,1)}, bf16[432,384]{1,0:T(8,128)(2,1)}, u32[]{:S(2)}, u32[]{:S(2)}) collective-permute-start(bf16[432,384]{1,0:T(8,128)(2,1)} %get-tuple-element.161), channel_id=1, source_target_pairs={{0,64},{64,0},{1,65},{65,1},{2,66},{66,2},{3,67},{67,3},{4,68},{68... | collective-permute-start | bytes 995336 | tf_op jit(solution)/shard_map/ppermute | solution.py:37
  36.2 68.4 %copy-start.4 = (bf16[3,432,384]{2,1,0:T(8,128)(2,1)}, bf16[3,432,384]{2,1,0:T(8,128)(2,1)S(1)}, u32[]{:S(2)}) copy-start(bf16[3,432,384]{2,1,0:T(8,128)(2,1)S(1)} %pad_maximum_fusion.s0) | copy-start | bytes 2985988
  40.6 23.7 %collective-permute-start.9 = (bf16[3,432,384]{2,1,0:T(8,128)(2,1)S(1)}, bf16[3,432,384]{2,1,0:T(8,128)(2,1)}, u32[]{:S(2)}, u32[]{:S(2)}) collective-permute-start(bf16[3,432,384]{2,1,0:T(8,128)(2,1)S(1)} %pad_maximum_fusion.s0), channel_id=1, source_target_pairs={{0,3},{1,0},{2,1},{3,2},{4,7},{5,4},{6,5},{7,6},{8,11},{9,8},{10,9... | collective-permute-start | bytes 2985992 | tf_op jit(solution)/shard_map/ppermute | solution.py:37
  41.5 24.0 %collective-permute-start.8 = (bf16[3,432,384]{2,1,0:T(8,128)(2,1)S(1)}, bf16[3,432,384]{2,1,0:T(8,128)(2,1)}, u32[]{:S(2)}, u32[]{:S(2)}) collective-permute-start(bf16[3,432,384]{2,1,0:T(8,128)(2,1)S(1)} %pad_maximum_fusion.s0), channel_id=1, source_target_pairs={{0,1},{1,2},{2,3},{3,0},{4,5},{5,6},{6,7},{7,4},{8,9},{9,10},{10,1... | collective-permute-start | bytes 2985992 | tf_op jit(solution)/shard_map/ppermute | solution.py:37
  44.3 2.6 collective-permute-start.5
  57.5 2.5 collective-permute-start.6
  65.5 18.6 %all-to-all-start.1 = ((bf16[8,64,768]{2,1,0:T(8,128)(2,1)}), bf16[8,64,768]{2,1,0:T(8,128)(2,1)S(1)}, u32[]{:S(2)}, u32[]{:S(2)}) async-start(bf16[8,64,768]{2,1,0:T(8,128)(2,1)} %bitcast.10), calls=%async_computation.1 | async-start | bytes 1572864 | tf_op jit(solution)/shard_map/all_to_all | solution.py:364
  72.5 23.1 %collective-permute-start.10 = (bf16[3,432,384]{2,1,0:T(8,128)(2,1)S(1)}, bf16[3,432,384]{2,1,0:T(8,128)(2,1)}, u32[]{:S(2)}, u32[]{:S(2)}) collective-permute-start(bf16[3,432,384]{2,1,0:T(8,128)(2,1)S(1)} %pad_maximum_fusion.s0), channel_id=1, source_target_pairs={{0,2},{1,3},{2,0},{3,1},{4,6},{5,7},{6,4},{7,5},{8,10},{9,11},{10,... | collective-permute-start | bytes 2985992 | tf_op jit(solution)/shard_map/ppermute | solution.py:37
  85.3 16.4 %all-to-all-start.2 = ((bf16[8,64,768]{2,1,0:T(8,128)(2,1)}), bf16[8,64,768]{2,1,0:T(8,128)(2,1)S(1)}, u32[]{:S(2)}, u32[]{:S(2)}) async-start(bf16[8,64,768]{2,1,0:T(8,128)(2,1)} %get-tuple-element.164), calls=%async_computation.2 | async-start | bytes 1572864 | tf_op jit(solution)/shard_map/all_to_all | solution.py:364
  105.5 114.8 %copy-start.14 = (bf16[1,1,16,384]{3,1,2,0:T(2,128)(2,1)}, bf16[1,1,16,384]{3,1,2,0:T(2,128)(2,1)S(1)}, u32[]{:S(2)}) copy-start(bf16[1,1,16,384]{3,1,2,0:T(2,128)(2,1)S(1)} %copy.78) | copy-start | bytes 36868
  106.1 2.3 collective-permute-start.11
  109.4 17.5 %all-to-all-start.3 = ((bf16[8,64,768]{2,1,0:T(8,128)(2,1)}), bf16[8,64,768]{2,1,0:T(8,128)(2,1)S(1)}, u32[]{:S(2)}, u32[]{:S(2)}) async-start(bf16[8,64,768]{2,1,0:T(8,128)(2,1)} %broadcast_in_dim.36), calls=%async_computation.3 | async-start | bytes 1572864 | tf_op jit(solution)/shard_map/all_to_all | solution.py:364
  126.9 105.5 %copy-start.7 = (bf16[8,64,768]{2,1,0:T(8,128)(2,1)}, bf16[8,64,768]{2,1,0:T(8,128)(2,1)S(1)}, u32[]{:S(2)}) copy-start(bf16[8,64,768]{2,1,0:T(8,128)(2,1)S(1)} %all-to-all-done.3) | copy-start | bytes 2359300
  126.9 2.5 collective-permute-start.12
  131.6 17.5 %all-to-all-start.4 = ((bf16[8,64,768]{2,1,0:T(8,128)(2,1)}), bf16[8,64,768]{2,1,0:T(8,128)(2,1)S(1)}, u32[]{:S(2)}, u32[]{:S(2)}) async-start(bf16[8,64,768]{2,1,0:T(8,128)(2,1)} %bitcast.17), calls=%async_computation.4 | async-start | bytes 1572864 | tf_op jit(solution)/shard_map/all_to_all | solution.py:364
  167.5 2.4 collective-permute-start.13
  179.8 2.5 collective-permute-start.14
  184.5 17.2 %all-to-all-start.6 = ((bf16[8,64,768]{2,1,0:T(8,128)(2,1)}), bf16[8,64,768]{2,1,0:T(8,128)(2,1)S(1)}, u32[]{:S(2)}, u32[]{:S(2)}) async-start(bf16[8,64,768]{2,1,0:T(8,128)(2,1)} %bitcast.20), calls=%async_computation.6 | async-start | bytes 1572864 | tf_op jit(solution)/shard_map/all_to_all | solution.py:364
  220.3 2.4 collective-permute-start.15
  232.3 2.5 collective-permute-start.16
  232.4 8.1 %collective-permute-start.17 = (bf16[8,64,768]{2,1,0:T(8,128)(2,1)S(1)}, bf16[8,64,768]{2,1,0:T(8,128)(2,1)}, u32[]{:S(2)}, u32[]{:S(2)}) collective-permute-start(bf16[8,64,768]{2,1,0:T(8,128)(2,1)S(1)} %all-to-all-done.3), channel_id=1, source_target_pairs={{0,4},{4,0},{1,5},{5,1},{2,6},{6,2},{3,7},{7,3},{8,12},{12,8},{9,1... | collective-permute-start | bytes 2359304 | tf_op jit(solution)/shard_map/ppermute | solution.py:37
  237.0 17.2 %all-to-all-start.8 = ((bf16[8,64,768]{2,1,0:T(8,128)(2,1)}), bf16[8,64,768]{2,1,0:T(8,128)(2,1)S(1)}, u32[]{:S(2)}, u32[]{:S(2)}) async-start(bf16[8,64,768]{2,1,0:T(8,128)(2,1)} %bitcast.23), calls=%async_computation.8 | async-start | bytes 1572864 | tf_op jit(solution)/shard_map/all_to_all | solution.py:364
  254.2 2.5 collective-permute-start.18
  258.9 19.6 %all-to-all-start.9 = ((bf16[8,64,768]{2,1,0:T(8,128)(2,1)}), bf16[8,64,768]{2,1,0:T(8,128)(2,1)S(1)}, u32[]{:S(2)}, u32[]{:S(2)}) async-start(bf16[8,64,768]{2,1,0:T(8,128)(2,1)} %bitcast.191), calls=%async_computation.9 | async-start | bytes 1572864 | tf_op jit(solution)/shard_map/all_to_all | solution.py:364
  279.7 17.3 %all-to-all-start.10 = ((bf16[8,64,768]{2,1,0:T(8,128)(2,1)}), bf16[8,64,768]{2,1,0:T(8,128)(2,1)S(1)}, u32[]{:S(2)}, u32[]{:S(2)}) async-start(bf16[8,64,768]{2,1,0:T(8,128)(2,1)} %get-tuple-element.198), calls=%async_computation.10 | async-start | bytes 1572864 | tf_op jit(solution)/shard_map/all_to_all | solution.py:364
  285.6 10.9 %collective-permute-start.19 = (bf16[432,384]{1,0:T(8,128)(2,1)S(1)}, bf16[432,384]{1,0:T(8,128)(2,1)S(1)}, u32[]{:S(2)}, u32[]{:S(2)}) collective-permute-start(bf16[432,384]{1,0:T(8,128)(2,1)S(1)} %get-tuple-element.376), channel_id=1, source_target_pairs={{0,2},{1,3},{2,0},{3,1},{4,6},{5,7},{6,4},{7,5},{8,10},{9,11},{10,... | collective-permute-start | bytes 995336 | tf_op jit(solution)/shard_map/ppermute | solution.py:37
  297.0 2.3 collective-permute-start.20
  297.0 15.5 %collective-permute-start.22 = (bf16[432,384]{1,0:T(8,128)(2,1)}, bf16[432,384]{1,0:T(8,128)(2,1)S(1)}, u32[]{:S(2)}, u32[]{:S(2)}) collective-permute-start(bf16[432,384]{1,0:T(8,128)(2,1)} %get-tuple-element.373), channel_id=1, source_target_pairs={{0,3},{1,0},{2,1},{3,2},{4,7},{5,4},{6,5},{7,6},{8,11},{9,8},{10,9... | collective-permute-start | bytes 995336 | tf_op jit(solution)/shard_map/ppermute | solution.py:37
  298.3 14.3 %collective-permute-start.21 = (bf16[432,384]{1,0:T(8,128)(2,1)}, bf16[432,384]{1,0:T(8,128)(2,1)S(1)}, u32[]{:S(2)}, u32[]{:S(2)}) collective-permute-start(bf16[432,384]{1,0:T(8,128)(2,1)} %get-tuple-element.374), channel_id=1, source_target_pairs={{0,1},{1,2},{2,3},{3,0},{4,5},{5,6},{6,7},{7,4},{8,9},{9,10},{10,1... | collective-permute-start | bytes 995336 | tf_op jit(solution)/shard_map/ppermute | solution.py:37
  312.5 2.6 collective-permute-start.23
  317.3 20.3 %all-to-all-start.11 = ((bf16[8,64,768]{2,1,0:T(8,128)(2,1)}), bf16[8,64,768]{2,1,0:T(8,128)(2,1)S(1)}, u32[]{:S(2)}, u32[]{:S(2)}) async-start(bf16[8,64,768]{2,1,0:T(8,128)(2,1)} %bitcast.192), calls=%async_computation.11 | async-start | bytes 1572864 | tf_op jit(solution)/shard_map/all_to_all | solution.py:364
  338.8 17.3 %all-to-all-start.12 = ((bf16[8,64,768]{2,1,0:T(8,128)(2,1)}), bf16[8,64,768]{2,1,0:T(8,128)(2,1)S(1)}, u32[]{:S(2)}, u32[]{:S(2)}) async-start(bf16[8,64,768]{2,1,0:T(8,128)(2,1)} %get-tuple-element.214), calls=%async_computation.12 | async-start | bytes 1572864 | tf_op jit(solution)/shard_map/all_to_all | solution.py:364
  344.8 10.9 %collective-permute-start.24 = (bf16[432,384]{1,0:T(8,128)(2,1)S(1)}, bf16[432,384]{1,0:T(8,128)(2,1)S(1)}, u32[]{:S(2)}, u32[]{:S(2)}) collective-permute-start(bf16[432,384]{1,0:T(8,128)(2,1)S(1)} %get-tuple-element.372), channel_id=1, source_target_pairs={{0,2},{1,3},{2,0},{3,1},{4,6},{5,7},{6,4},{7,5},{8,10},{9,11},{10,... | collective-permute-start | bytes 995336 | tf_op jit(solution)/shard_map/ppermute | solution.py:37
  356.1 2.3 collective-permute-start.25
  356.2 15.7 %collective-permute-start.27 = (bf16[432,384]{1,0:T(8,128)(2,1)}, bf16[432,384]{1,0:T(8,128)(2,1)S(1)}, u32[]{:S(2)}, u32[]{:S(2)}) collective-permute-start(bf16[432,384]{1,0:T(8,128)(2,1)} %get-tuple-element.369), channel_id=1, source_target_pairs={{0,3},{1,0},{2,1},{3,2},{4,7},{5,4},{6,5},{7,6},{8,11},{9,8},{10,9... | collective-permute-start | bytes 995336 | tf_op jit(solution)/shard_map/ppermute | solution.py:37
  358.5 13.4 %collective-permute-start.26 = (bf16[432,384]{1,0:T(8,128)(2,1)}, bf16[432,384]{1,0:T(8,128)(2,1)S(1)}, u32[]{:S(2)}, u32[]{:S(2)}) collective-permute-start(bf16[432,384]{1,0:T(8,128)(2,1)} %get-tuple-element.370), channel_id=1, source_target_pairs={{0,1},{1,2},{2,3},{3,0},{4,5},{5,6},{6,7},{7,4},{8,9},{9,10},{10,1... | collective-permute-start | bytes 995336 | tf_op jit(solution)/shard_map/ppermute | solution.py:37
  371.9 2.6 collective-permute-start.28
  376.7 20.4 %all-to-all-start.13 = ((bf16[8,64,768]{2,1,0:T(8,128)(2,1)}), bf16[8,64,768]{2,1,0:T(8,128)(2,1)S(1)}, u32[]{:S(2)}, u32[]{:S(2)}) async-start(bf16[8,64,768]{2,1,0:T(8,128)(2,1)} %bitcast.193), calls=%async_computation.13 | async-start | bytes 1572864 | tf_op jit(solution)/shard_map/all_to_all | solution.py:364
  398.3 17.3 %all-to-all-start.14 = ((bf16[8,64,768]{2,1,0:T(8,128)(2,1)}), bf16[8,64,768]{2,1,0:T(8,128)(2,1)S(1)}, u32[]{:S(2)}, u32[]{:S(2)}) async-start(bf16[8,64,768]{2,1,0:T(8,128)(2,1)} %get-tuple-element.230), calls=%async_computation.14 | async-start | bytes 1572864 | tf_op jit(solution)/shard_map/all_to_all | solution.py:364
  404.3 10.9 %collective-permute-start.29 = (bf16[432,384]{1,0:T(8,128)(2,1)S(1)}, bf16[432,384]{1,0:T(8,128)(2,1)S(1)}, u32[]{:S(2)}, u32[]{:S(2)}) collective-permute-start(bf16[432,384]{1,0:T(8,128)(2,1)S(1)} %get-tuple-element.368), channel_id=1, source_target_pairs={{0,2},{1,3},{2,0},{3,1},{4,6},{5,7},{6,4},{7,5},{8,10},{9,11},{10,... | collective-permute-start | bytes 995336 | tf_op jit(solution)/shard_map/ppermute | solution.py:37
  415.6 3.2 collective-permute-start.30
  415.7 16.5 %collective-permute-start.32 = (bf16[432,384]{1,0:T(8,128)(2,1)}, bf16[432,384]{1,0:T(8,128)(2,1)S(1)}, u32[]{:S(2)}, u32[]{:S(2)}) collective-permute-start(bf16[432,384]{1,0:T(8,128)(2,1)} %get-tuple-element.365), channel_id=1, source_target_pairs={{0,3},{1,0},{2,1},{3,2},{4,7},{5,4},{6,5},{7,6},{8,11},{9,8},{10,9... | collective-permute-start | bytes 995336 | tf_op jit(solution)/shard_map/ppermute | solution.py:37
  418.9 13.3 %collective-permute-start.31 = (bf16[432,384]{1,0:T(8,128)(2,1)}, bf16[432,384]{1,0:T(8,128)(2,1)S(1)}, u32[]{:S(2)}, u32[]{:S(2)}) collective-permute-start(bf16[432,384]{1,0:T(8,128)(2,1)} %get-tuple-element.366), channel_id=1, source_target_pairs={{0,1},{1,2},{2,3},{3,0},{4,5},{5,6},{6,7},{7,4},{8,9},{9,10},{10,1... | collective-permute-start | bytes 995336 | tf_op jit(solution)/shard_map/ppermute | solution.py:37
  432.2 2.6 collective-permute-start.33
  433.6 15.1 %collective-permute-start.34 = (bf16[432,384]{1,0:T(8,128)(2,1)}, bf16[432,384]{1,0:T(8,128)(2,1)S(1)}, u32[]{:S(2)}, u32[]{:S(2)}) collective-permute-start(bf16[432,384]{1,0:T(8,128)(2,1)} %get-tuple-element.338), channel_id=1, source_target_pairs={{0,64},{64,0},{1,65},{65,1},{2,66},{66,2},{3,67},{67,3},{4,68},{68... | collective-permute-start | bytes 995336 | tf_op jit(solution)/shard_map/ppermute | solution.py:37
  435.8 20.5 %all-to-all-start.15 = ((bf16[8,64,768]{2,1,0:T(8,128)(2,1)}), bf16[8,64,768]{2,1,0:T(8,128)(2,1)S(1)}, u32[]{:S(2)}, u32[]{:S(2)}) async-start(bf16[8,64,768]{2,1,0:T(8,128)(2,1)} %bitcast.47), calls=%async_computation.15 | async-start | bytes 1572864 | tf_op jit(solution)/shard_map/all_to_all | solution.py:364
  458.0 40.9 %all-to-all-start.16 = ((bf16[8,432,384]{2,1,0:T(8,128)(2,1)}), bf16[8,432,384]{2,1,0:T(8,128)(2,1)}, u32[]{:S(2)}, u32[]{:S(2)}) async-start(bf16[8,432,384]{2,1,0:T(8,128)(2,1)} %broadcast_in_dim.37), calls=%async_computation.16 | async-start | bytes 5308416 | tf_op jit(solution)/shard_map/all_to_all | solution.py:364
  462.4 20.0 %copy-start.2 = (bf16[432,384]{1,0:T(8,128)(2,1)S(1)}, bf16[432,384]{1,0:T(8,128)(2,1)}, u32[]{:S(2)}) copy-start(bf16[432,384]{1,0:T(8,128)(2,1)} %get-tuple-element.255) | copy-start | bytes 995332
  462.4 20.0 %copy-start.19 = (bf16[432,384]{1,0:T(8,128)(2,1)S(1)}, bf16[432,384]{1,0:T(8,128)(2,1)}, u32[]{:S(2)}) copy-start(bf16[432,384]{1,0:T(8,128)(2,1)} %copy-done.18) | copy-start | bytes 995332
  462.4 20.0 %copy-start.23 = (bf16[432,384]{1,0:T(8,128)(2,1)S(1)}, bf16[432,384]{1,0:T(8,128)(2,1)}, u32[]{:S(2)}) copy-start(bf16[432,384]{1,0:T(8,128)(2,1)} %copy-done.22) | copy-start | bytes 995332
  463.8 11.1 %collective-permute-start.35 = (bf16[432,384]{1,0:T(8,128)(2,1)S(1)}, bf16[432,384]{1,0:T(8,128)(2,1)S(1)}, u32[]{:S(2)}, u32[]{:S(2)}) collective-permute-start(bf16[432,384]{1,0:T(8,128)(2,1)S(1)} %get-tuple-element.362), channel_id=1, source_target_pairs={{0,1},{1,2},{2,3},{3,0},{4,5},{5,6},{6,7},{7,4},{8,9},{9,10},{10,1... | collective-permute-start | bytes 995336 | tf_op jit(solution)/shard_map/ppermute | solution.py:37
  464.1 16.6 %collective-permute-start.37 = (bf16[432,384]{1,0:T(8,128)(2,1)S(1)}, bf16[432,384]{1,0:T(8,128)(2,1)S(1)}, u32[]{:S(2)}, u32[]{:S(2)}) collective-permute-start(bf16[432,384]{1,0:T(8,128)(2,1)S(1)} %get-tuple-element.363), channel_id=1, source_target_pairs={{0,3},{1,0},{2,1},{3,2},{4,7},{5,4},{6,5},{7,6},{8,11},{9,8},{10,9... | collective-permute-start | bytes 995336 | tf_op jit(solution)/shard_map/ppermute | solution.py:37
  467.2 15.2 %collective-permute-start.36 = (bf16[432,384]{1,0:T(8,128)(2,1)S(1)}, bf16[432,384]{1,0:T(8,128)(2,1)S(1)}, u32[]{:S(2)}, u32[]{:S(2)}) collective-permute-start(bf16[432,384]{1,0:T(8,128)(2,1)S(1)} %get-tuple-element.364), channel_id=1, source_target_pairs={{0,2},{1,3},{2,0},{3,1},{4,6},{5,7},{6,4},{7,5},{8,10},{9,11},{10,... | collective-permute-start | bytes 995336 | tf_op jit(solution)/shard_map/ppermute | solution.py:37
  483.9 14.9 %collective-permute-start.38 = (bf16[432,384]{1,0:T(8,128)(2,1)S(1)}, bf16[432,384]{1,0:T(8,128)(2,1)S(1)}, u32[]{:S(2)}, u32[]{:S(2)}) collective-permute-start(bf16[432,384]{1,0:T(8,128)(2,1)S(1)} %get-tuple-element.335), channel_id=1, source_target_pairs={{0,64},{64,0},{1,65},{65,1},{2,66},{66,2},{3,67},{67,3},{4,68},{68... | collective-permute-start | bytes 995336 | tf_op jit(solution)/shard_map/ppermute | solution.py:37
  498.9 12.0 %collective-permute-start.39 = (bf16[8,432,384]{2,1,0:T(8,128)(2,1)}, bf16[8,432,384]{2,1,0:T(8,128)(2,1)}, u32[]{:S(2)}, u32[]{:S(2)}) collective-permute-start(bf16[8,432,384]{2,1,0:T(8,128)(2,1)} %all-to-all-done.16.own), channel_id=1, source_target_pairs={{0,4},{4,0},{1,5},{5,1},{2,6},{6,2},{3,7},{7,3},{8,12},{12,8},{9,1... | collective-permute-start | bytes 7962632 | tf_op jit(solution)/shard_map/ppermute | solution.py:37
  500.8 41.8 %all-to-all-start.17 = ((bf16[8,432,384]{2,1,0:T(8,128)(2,1)}), bf16[8,432,384]{2,1,0:T(8,128)(2,1)}, u32[]{:S(2)}, u32[]{:S(2)}) async-start(bf16[8,432,384]{2,1,0:T(8,128)(2,1)} %broadcast_in_dim.38), calls=%async_computation.17 | async-start | bytes 5308416 | tf_op jit(solution)/shard_map/all_to_all | solution.py:364
  510.5 32.2 %collective-permute-start.40 = (f32[64,768]{1,0:T(8,128)S(1)}, f32[64,768]{1,0:T(8,128)S(1)}, u32[]{:S(2)}, u32[]{:S(2)}) collective-permute-start(f32[64,768]{1,0:T(8,128)S(1)} %broadcast_select_fusion.5), channel_id=1, source_target_pairs={{0,64},{64,0},{1,65},{65,1},{2,66},{66,2},{3,67},{67,3},{4,68},{68... | collective-permute-start | bytes 589832 | tf_op jit(solution)/shard_map/ppermute | solution.py:37
  542.6 5.3 collective-permute-start.41
  (32 other events, 207.9 us)

commit v4 on v3

--- a/solution.py
+++ b/solution.py
@@ -58,7 +58,10 @@
     for i in range(smem, len(args)):
         if isinstance(args[i], tuple):
             block, at = args[i]
-            specs.append(pl.BlockSpec((None,) + block.shape[1:], lambda _, at=at: (at, 0, 0)))
+            if block.shape[0] == 8:
+                specs.append(pl.BlockSpec((8, ROWS, D), lambda _, at=at: (0, at, 0)))
+            else:
+                specs.append(pl.BlockSpec((None,) + block.shape[1:], lambda _, at=at: (at, 0, 0)))
         else:
             specs.append(whole(args[i].shape))
     args = [a[0] if isinstance(a, tuple) else a for a in args]
@@ -80,10 +83,16 @@
     return offset * scale, scale
 
 
-def start_kernel(x, n_out):
+def start_kernel(x, cotangent, out):
     n = centred(x[...])[0].astype(BF)
     for k in range(8):
-        n_out[k] = n
+        out[k, 0:ROWS] = n
+        out[k, ROWS:] = cotangent[...]
+
+
+def rows_of(source, step):
+    count = BLOCK // ROWS
+    return source[pl.ds(step * count, count)].reshape(BLOCK, D)
 
 
 def finish_kernel(rounded, got, x, bias, x_out, n_out):
@@ -166,9 +175,8 @@
 
         @pl.loop(0, HALF // BLOCK)
         def _(step):
-            here = pl.ds(step * BLOCK, BLOCK)
             rows = pl.ds(half * HALF + step * BLOCK, BLOCK)
-            n = source[here, :].astype(F32)
+            n = rows_of(source, step).astype(F32)
             one = (n * vec[0:1, :] + vec[1:2, :]).astype(BF)
             two = (n * vec[2:3, :] + vec[3:4, :]).astype(BF)
             merged = dot(one, w_qkv[...]) + bias[0:1, 0:192]
@@ -209,7 +217,7 @@
         @pl.loop(0, HALF // BLOCK)
         def _(step):
             rows = pl.ds(half * HALF + step * BLOCK, BLOCK)
-            branch = source[pl.ds(step * BLOCK, BLOCK), :]
+            branch = rows_of(source, step)
             sums[5:6, :] += jnp.sum(branch.astype(F32), 0, keepdims=True)
             both = dot(branch, w_both[...], 1, 1)
             up = pre[rows, :]
@@ -254,7 +262,7 @@
             one = dot(g_qkv, w_qkv[...], 1, 1)
             two = dot(g_up, w_up[...], 1, 1)
             target[here, :] = (one * vec[0:1, :] + two * vec[2:3, :]).astype(BF)
-            n = source[here, :].astype(F32)
+            n = rows_of(source, step).astype(F32)
             for at, part in enumerate((one * n, one, two * n, two)):
                 sums[at : at + 1, :] += jnp.sum(part, 0, keepdims=True)
             sums[4:5, 0:192] += jnp.sum(g_qkv.astype(F32), 0, keepdims=True)
@@ -269,14 +277,13 @@
 
         @pl.loop(0, HALF // BLOCK)
         def _(step):
-            here = pl.ds(step * BLOCK, BLOCK)
             rows = pl.ds(half * HALF + step * BLOCK, BLOCK)
-            n = normal[here, :].astype(F32)
+            n = rows_of(normal, step).astype(F32)
             one = (n * vec[0:1, :] + vec[1:2, :]).astype(BF)
             two = (n * vec[2:3, :] + vec[3:4, :]).astype(BF)
             in_qkv[...] += dot(one, d_qkv[rows, :], 0, 0)
             in_up[...] += dot(two, d_up[rows, :], 0, 0)
-            in_act[...] += dot(act[rows, :], branch[here, :], 0, 0)
+            in_act[...] += dot(act[rows, :], rows_of(branch, step), 0, 0)
 
     blank = jnp.zeros((12, 384), F32)
     out = in_act[192:256, :].astype(BF)
@@ -365,12 +372,12 @@
         return got if beside is None else lax.optimization_barrier((got, beside))
 
     def both_cores(own):
-        return own.reshape(HALF, D), shifted(own, "c", 1).reshape(HALF, D)
+        return own, shifted(own, "c", 1)
 
     def halves_joined(own, other):
         return (own + shifted(other, "c", 1)).reshape(8, ROWS, D)
 
-    n_sent = call(start_kernel, [((8, ROWS, D), BF)], x)[0]
+    n_sent = call(start_kernel, [((8, 2 * ROWS, D), BF)], x, dx)[0]
     mask = has_head.astype(BF)
 
     def cut(w, at, sizes):
@@ -446,7 +453,9 @@
     )
     layer_share[0] = [(piece, 0) for piece in layer_share[0]]
     layer_vectors = [vectors_of(layer_share[0])]
-    normals = both_cores(own)
+    started = both_cores(own)
+    normals = [(rows, 0) for rows in started]
+    branches = [(rows, 1) for rows in started]
     place = jnp.stack([z.astype(jnp.int32), owner])
 
     kept = []
@@ -457,10 +466,6 @@
             place, order, *normals, layer_vectors[l][0], layer_vectors[l][1], *layer_share[l], *tables,
             scratch=WEIGHT_SCRATCH + (VMEM((SEQ, HD), BF),), smem=2, room=56, takes=11,
         )
-        if l == 1:
-            sent = after(normals, jnp.broadcast_to(dx[None], (8, ROWS, D)))
-            branches, (own, other) = exchanged(sent, (own, other))
-            branches = both_cores(branches)
         kept.append((x, normals, qkv, pre, act))
         if l + 1 < LAYERS:
             joined = halves_joined(own, other)
@@ -510,16 +515,17 @@
                 functools.partial(finish_kernel, False),
                 [((ROWS, D), F32), ((8, ROWS, D), BF)], got, x, layer_vectors[l][2],
             )[0]
-        else:
-            own, other, parts = lax.optimization_barrier((own, other, parts))
-            shares[l + 1] = summed(parts)
         pack = call(
             product_kernel, [((4, PACK, 384), BF)],
             *branches, *normals, layer_vectors[l][0], act, d_qkv, d_up, sums,
             scratch=(VMEM((D, UNITS), F32), VMEM((D, UNITS), F32), VMEM((256, D), F32)),
             room=56, takes=6,
         )[0]
-        got, pack = exchanged(halves_joined(own, other), pack)
+        joined = halves_joined(own, other)
+        if l + 1 < LAYERS:
+            joined, parts = lax.optimization_barrier((joined, parts))
+            shares[l + 1] = summed(parts)
+        got, pack = exchanged(joined, pack)
         dx, branch_sent = call(
             functools.partial(finish_back_kernel, l == 2),
             [((ROWS, D), F32), ((8, ROWS, D), BF)], got, x, dx,

time: 574 us -> 599 us (1.044)
  waiting for transfers between devices: 197 us -> 224 us
    ppermute x42 -> x41, waiting for transfers between devices: 118 us -> 159 us  [shifted(): lax.ppermute(block, axis, [(i, (i + distance) % size) for i in range(size)])]
    all_to_all x16 -> x15, waiting for transfers between devices: 79 us -> 65.5 us  [exchanged(): got = lax.all_to_all(sent, CHIPS, 0, 0, tiled=True)]
    ppermute x42 -> x41, starting transfers between devices: 33.1 us -> 28.8 us  [shifted(): lax.ppermute(block, axis, [(i, (i + distance) % size) for i in range(size)])]
    all_to_all x16 -> x15, starting transfers between devices: 81.7 us -> 81 us  [exchanged(): got = lax.all_to_all(sent, CHIPS, 0, 0, tiled=True)]
  transfers between devices with their start and end apart: 58 -> 56, of which waited for: 41 -> 44; matrix products, arithmetic and copies ran while one was open for 8% -> 8% of each run, Pallas kernels for 19% -> 10%
where the time goes in v4:
time: 599 us; the launch traced here: 588 us
  waiting for transfers between devices  224 us (37%)
  Pallas kernels  136 us (23%)
  starting transfers between devices  110 us (18%)
  local copies, waits for them, and re-layouts  40.6 us (7%)
  other arithmetic  39.7 us (7%)
  blocking collectives  36.7 us (6%)
    ppermute x41, waiting for transfers between devices, shifted(): lax.ppermute(block, axis, [(i, (i + distance) % size) for i in range(size)])  159 us
    pallas_call x21, Pallas kernels, call(): pl.pallas_call(kernel, out_shape=[jax.ShapeDtypeStruct(shape, dtype) for...  122 us
    all_to_all x15, starting transfers between devices, exchanged(): got = lax.all_to_all(sent, CHIPS, 0, 0, tiled=True)  81 us
    all_to_all x15, waiting for transfers between devices, exchanged(): got = lax.all_to_all(sent, CHIPS, 0, 0, tiled=True)  65.5 us
    all_to_all x2, blocking collectives, exchanged(): got = lax.all_to_all(sent, CHIPS, 0, 0, tiled=True)  36.7 us
    ppermute x41, starting transfers between devices, shifted(): lax.ppermute(block, axis, [(i, (i + distance) % size) for i in range(size)])  28.8 us
    add x8, other arithmetic, halves_joined(): return (own + shifted(other, 'c', 1)).reshape(8, ROWS, D)  17.6 us
    pallas_call x2, Pallas kernels, unpacked(): pl.pallas_call(unpack_kernel, grid=(1,), out_shape=[jax.ShapeDtypeStruct(...  14.1 us
  transfers between devices with their start and end apart: 56, of which 44 were waited for; matrix products, arithmetic and copies ran while one was open for 8% of the time, Pallas kernels for 10%

profile of v4, /device:TPU:0, one launch (start us, length us, event | category | flops | bytes accessed | tf_op | source)
XLA Modules:
  0.0 588.4 jit_solution(13792028867657308661)
XLA Ops:
  11.1 7.1 %all-to-all-start = ((bf16[8,128,768]{2,1,0:T(8,128)(2,1)}), bf16[8,128,768]{2,1,0:T(8,128)(2,1)}, u32[]{:S(2)}, u32[]{:S(2)}) async-start(bf16[8,128,768]{2,1,0:T(8,128)(2,1)} %shard_map.237), calls=%async_computation | async-start | bytes 3145728 | tf_op jit(solution)/shard_map/all_to_all | solution.py:371
  19.8 4.0 collective-permute-start.4
  34.0 3.4 collective-permute-done.4.s3
  37.5 3.4 collective-permute-done.2.s1
  44.3 4.1 collective-permute-start.9
  52.1 9.7 %shard_map.238 = (bf16[512,768]{1,0:T(8,128)(2,1)}, bf16[512,768]{1,0:T(8,128)(2,1)}, bf16[1024,192]{1,0:T(8,128)(2,1)}, f32[1024,192]{1,0:T(8,128)}, bf16[1024,256]{1,0:T(8,128)(2,1)}) custom-call(s32[2]{0:T(128)} %pad_add_fusion.place, s32[32]{0:T(128)} %reshape.1282.order, bf16[8,128,768]{2,1,0:T(8,128)(2,1)} %all-to-all-done.own.b_own.n_own, ...), custom_call_target="tpu_custom_call" | custom-call | flops 11000000512 | bytes 38500000 | tf_op jit(solution)/shard_map/pallas_call | solution.py:68
  61.9 2.5 collective-permute-done.6
  68.2 3.5 collective-permute-done.8.s1
  71.7 7.5 %all-to-all-start.1 = ((bf16[8,64,768]{2,1,0:T(8,128)(2,1)}), bf16[8,64,768]{2,1,0:T(8,128)(2,1)S(1)}, u32[]{:S(2)}, u32[]{:S(2)}) async-start(bf16[8,64,768]{2,1,0:T(8,128)(2,1)} %bitcast.8), calls=%async_computation.1 | async-start | bytes 1572864 | tf_op jit(solution)/shard_map/all_to_all | solution.py:371
  79.4 10.7 %all-to-all-done.1.got = bf16[8,64,768]{2,1,0:T(8,128)(2,1)S(1)} async-done(((bf16[8,64,768]{2,1,0:T(8,128)(2,1)}), bf16[8,64,768]{2,1,0:T(8,128)(2,1)S(1)}, u32[]{:S(2)}, u32[]{:S(2)}) %all-to-all-start.1) | async-done | bytes 786464 | tf_op jit(solution)/shard_map/all_to_all | solution.py:371
  91.2 3.5 all-to-all-start.2
  94.7 6.6 %collective-permute-done.10.s2 = bf16[3,432,384]{2,1,0:T(8,128)(2,1)} collective-permute-done((bf16[3,432,384]{2,1,0:T(8,128)(2,1)S(1)}, bf16[3,432,384]{2,1,0:T(8,128)(2,1)}, u32[]{:S(2)}, u32[]{:S(2)}) %collective-permute-start.10) | collective-permute-done | bytes 995360 | tf_op jit(solution)/shard_map/ppermute | solution.py:37
  101.3 4.2 all-to-all-done.2.own.n_own
  113.2 9.5 %shard_map.240 = (bf16[512,768]{1,0:T(8,128)(2,1)}, bf16[512,768]{1,0:T(8,128)(2,1)}, bf16[1024,192]{1,0:T(8,128)(2,1)}, f32[1024,192]{1,0:T(8,128)}, bf16[1024,256]{1,0:T(8,128)(2,1)}) custom-call(s32[2]{0:T(128)} %pad_add_fusion.place, s32[32]{0:T(128)} %reshape.1282.order, bf16[8,64,768]{2,1,0:T(8,128)(2,1)} %copy-done.5, bf16[8,64,768]{2,1,0:T(8,128)(2,1)} %copy-done.31, ...), custom_call_target="tpu_custom_call" | custom-call | flops 11000000512 | bytes 38500000 | tf_op jit(solution)/shard_map/pallas_call | solution.py:68
  127.4 3.5 all-to-all-start.3
  131.1 13.5 %all-to-all-done.3.got = bf16[8,64,768]{2,1,0:T(8,128)(2,1)S(1)} async-done(((bf16[8,64,768]{2,1,0:T(8,128)(2,1)}), bf16[8,64,768]{2,1,0:T(8,128)(2,1)S(1)}, u32[]{:S(2)}, u32[]{:S(2)}) %all-to-all-start.3) | async-done | bytes 786464 | tf_op jit(solution)/shard_map/all_to_all | solution.py:371
  144.9 18.4 %all_to_all.85.own.n_own = bf16[8,64,768]{2,1,0:T(8,128)(2,1)S(1)} all-to-all(bf16[8,64,768]{2,1,0:T(8,128)(2,1)S(1)} %get-tuple-element.168), channel_id=1, replica_groups=mesh['s'=2,'xh'=2,'y'=4,'c'=2,'z'=4] {'xh','y'}, dimensions={0} | all-to-all | bytes 1572864 | tf_op jit(solution)/shard_map/all_to_all | solution.py:371
  166.5 9.9 %shard_map.242 = (bf16[512,768]{1,0:T(8,128)(2,1)}, bf16[512,768]{1,0:T(8,128)(2,1)}, bf16[1024,192]{1,0:T(8,128)(2,1)}, f32[1024,192]{1,0:T(8,128)}, bf16[1024,256]{1,0:T(8,128)(2,1)}) custom-call(s32[2]{0:T(128)} %pad_add_fusion.place, s32[32]{0:T(128)} %reshape.1282.order, bf16[8,64,768]{2,1,0:T(8,128)(2,1)} %copy-done.6, bf16[8,64,768]{2,1,0:T(8,128)(2,1)} %copy-done.32, ...), custom_call_target="tpu_custom_call" | custom-call | flops 11000000512 | bytes 38500000 | tf_op jit(solution)/shard_map/pallas_call | solution.py:68
  176.6 2.4 collective-permute-done.14
  181.1 3.5 all-to-all-start.5
  184.8 13.5 %all-to-all-done.5.got = bf16[8,64,768]{2,1,0:T(8,128)(2,1)S(1)} async-done(((bf16[8,64,768]{2,1,0:T(8,128)(2,1)}), bf16[8,64,768]{2,1,0:T(8,128)(2,1)S(1)}, u32[]{:S(2)}, u32[]{:S(2)}) %all-to-all-start.5) | async-done | bytes 786464 | tf_op jit(solution)/shard_map/all_to_all | solution.py:371
  198.6 18.3 %all_to_all.86.own.n_own = bf16[8,64,768]{2,1,0:T(8,128)(2,1)S(1)} all-to-all(bf16[8,64,768]{2,1,0:T(8,128)(2,1)S(1)} %get-tuple-element.172), channel_id=1, replica_groups=mesh['s'=2,'xh'=2,'y'=4,'c'=2,'z'=4] {'xh','y'}, dimensions={0} | all-to-all | bytes 1572864 | tf_op jit(solution)/shard_map/all_to_all | solution.py:371
  220.1 9.5 %shard_map.244 = (bf16[512,768]{1,0:T(8,128)(2,1)}, bf16[512,768]{1,0:T(8,128)(2,1)}, bf16[1024,192]{1,0:T(8,128)(2,1)}, f32[1024,192]{1,0:T(8,128)}, bf16[1024,256]{1,0:T(8,128)(2,1)}) custom-call(s32[2]{0:T(128)} %pad_add_fusion.place, s32[32]{0:T(128)} %reshape.1282.order, bf16[8,64,768]{2,1,0:T(8,128)(2,1)} %copy-done.9, bf16[8,64,768]{2,1,0:T(8,128)(2,1)} %copy-done.33, ...), custom_call_target="tpu_custom_call" | custom-call | flops 11000000512 | bytes 38500000 | tf_op jit(solution)/shard_map/pallas_call | solution.py:68
  229.7 2.4 collective-permute-done.16
  234.3 3.5 all-to-all-start.7
  237.9 12.3 %shard_map.245 = (bf16[512,768]{1,0:T(8,128)(2,1)}, bf16[512,768]{1,0:T(8,128)(2,1)}, bf16[1024,192]{1,0:T(8,128)(2,1)}, bf16[1024,192]{1,0:T(8,128)(2,1)}, f32[8,768]{1,0:T(8,128)}) custom-call(s32[2]{0:T(128)} %pad_add_fusion.place, s32[32]{0:T(128)} %reshape.1282.order, bf16[8,128,768]{2,1,0:T(8,128)(2,1)} %all-to-all-done.own.b_own.n_own, ...), custom_call_target="tpu_custom_call" | custom-call | flops 12999999488 | bytes 45500000 | tf_op jit(solution)/shard_map/pallas_call | solution.py:68
  251.5 2.5 collective-permute-done.17
  256.2 5.9 all-to-all-start.8
  262.1 6.1 %shard_map.246 = bf16[4,432,384]{2,1,0:T(8,128)(2,1)} custom-call(bf16[8,128,768]{2,1,0:T(8,128)(2,1)} %all-to-all-done.own.b_own.n_own, bf16[8,128,768]{2,1,0:T(8,128)(2,1)} %collective-permute-done.5.other.b_other.n_other, bf16[8,64,768]{2,1,0:T(8,128)(2,1)} %copy-done.9, bf16[8,64,768]{2,1,0:T(8,128)(2,1)} %copy-done.33, f32[8,768]{1,0:T(8,128)} %concatenate.88.vec, ...), custom_call_target="tpu_custom_call" | custom-call | flops 6000000000 | bytes 21000000 | tf_op jit(solution)/shard_map/pallas_call | solution.py:68
  268.2 7.6 %all-to-all-done.8.got = bf16[8,64,768]{2,1,0:T(8,128)(2,1)S(1)} async-done(((bf16[8,64,768]{2,1,0:T(8,128)(2,1)}), bf16[8,64,768]{2,1,0:T(8,128)(2,1)S(1)}, u32[]{:S(2)}, u32[]{:S(2)}) %all-to-all-start.8) | async-done | bytes 786464 | tf_op jit(solution)/shard_map/all_to_all | solution.py:371
  277.1 3.7 all-to-all-start.9
  285.2 8.8 %collective-permute-done.18 = bf16[432,384]{1,0:T(8,128)(2,1)S(1)} collective-permute-done((bf16[432,384]{1,0:T(8,128)(2,1)S(1)}, bf16[432,384]{1,0:T(8,128)(2,1)S(1)}, u32[]{:S(2)}, u32[]{:S(2)}) %collective-permute-start.18) | collective-permute-done | bytes 331808 | tf_op jit(solution)/shard_map/ppermute | solution.py:37
  294.4 2.3 collective-permute-done.19.b_other
  297.6 12.4 %shard_map.248 = (bf16[512,768]{1,0:T(8,128)(2,1)}, bf16[512,768]{1,0:T(8,128)(2,1)}, bf16[1024,192]{1,0:T(8,128)(2,1)}, bf16[1024,192]{1,0:T(8,128)(2,1)}, f32[8,768]{1,0:T(8,128)}) custom-call(s32[2]{0:T(128)} %pad_add_fusion.place, s32[32]{0:T(128)} %reshape.1282.order, bf16[8,64,768]{2,1,0:T(8,128)(2,1)} %copy-done.7, bf16[8,64,768]{2,1,0:T(8,128)(2,1)} %copy-done.36, ...), custom_call_target="tpu_custom_call" | custom-call | flops 12999999488 | bytes 45500000 | tf_op jit(solution)/shard_map/pallas_call | solution.py:68
  310.1 3.5 collective-permute-start.22
  315.9 5.4 collective-permute-done.22
  321.2 3.5 collective-permute-done.21
  324.7 6.6 %all-to-all-start.10 = ((bf16[8,64,768]{2,1,0:T(8,128)(2,1)}), bf16[8,64,768]{2,1,0:T(8,128)(2,1)S(1)}, u32[]{:S(2)}, u32[]{:S(2)}) async-start(bf16[8,64,768]{2,1,0:T(8,128)(2,1)} %bitcast.175), calls=%async_computation.10 | async-start | bytes 1572864 | tf_op jit(solution)/shard_map/all_to_all | solution.py:371
  331.4 6.1 %shard_map.249 = bf16[4,432,384]{2,1,0:T(8,128)(2,1)} custom-call(bf16[8,64,768]{2,1,0:T(8,128)(2,1)} %copy-done.7, bf16[8,64,768]{2,1,0:T(8,128)(2,1)} %copy-done.36, bf16[8,64,768]{2,1,0:T(8,128)(2,1)} %copy-done.6, bf16[8,64,768]{2,1,0:T(8,128)(2,1)} %copy-done.32, f32[8,768]{1,0:T(8,128)} %concatenate.84.vec, bf16[1024,256]{1,0:T(8,128)(2,1)} %get-tuple-element.196.act, ...), custom_call_target="tpu_custom_call" | custom-call | flops 6000000000 | bytes 21000000 | tf_op jit(solution)/shard_map/pallas_call | solution.py:68
  337.5 6.8 %all-to-all-done.10.got = bf16[8,64,768]{2,1,0:T(8,128)(2,1)S(1)} async-done(((bf16[8,64,768]{2,1,0:T(8,128)(2,1)}), bf16[8,64,768]{2,1,0:T(8,128)(2,1)S(1)}, u32[]{:S(2)}, u32[]{:S(2)}) %all-to-all-start.10) | async-done | bytes 786464 | tf_op jit(solution)/shard_map/all_to_all | solution.py:371
  345.5 3.7 all-to-all-start.11
  351.4 10.9 %collective-permute-done.23 = bf16[432,384]{1,0:T(8,128)(2,1)S(1)} collective-permute-done((bf16[432,384]{1,0:T(8,128)(2,1)S(1)}, bf16[432,384]{1,0:T(8,128)(2,1)S(1)}, u32[]{:S(2)}, u32[]{:S(2)}) %collective-permute-start.23) | collective-permute-done | bytes 331808 | tf_op jit(solution)/shard_map/ppermute | solution.py:37
  362.7 2.3 collective-permute-done.24.b_other
  365.9 12.6 %shard_map.251 = (bf16[512,768]{1,0:T(8,128)(2,1)}, bf16[512,768]{1,0:T(8,128)(2,1)}, bf16[1024,192]{1,0:T(8,128)(2,1)}, bf16[1024,192]{1,0:T(8,128)(2,1)}, f32[8,768]{1,0:T(8,128)}) custom-call(s32[2]{0:T(128)} %pad_add_fusion.place, s32[32]{0:T(128)} %reshape.1282.order, bf16[8,64,768]{2,1,0:T(8,128)(2,1)} %copy-done.10, bf16[8,64,768]{2,1,0:T(8,128)(2,1)} %copy-done.35, ...), custom_call_target="tpu_custom_call" | custom-call | flops 12999999488 | bytes 45500000 | tf_op jit(solution)/shard_map/pallas_call | solution.py:68
  383.2 5.5 collective-permute-done.27
  390.3 6.6 %all-to-all-start.12 = ((bf16[8,64,768]{2,1,0:T(8,128)(2,1)}), bf16[8,64,768]{2,1,0:T(8,128)(2,1)S(1)}, u32[]{:S(2)}, u32[]{:S(2)}) async-start(bf16[8,64,768]{2,1,0:T(8,128)(2,1)} %bitcast.176), calls=%async_computation.12 | async-start | bytes 1572864 | tf_op jit(solution)/shard_map/all_to_all | solution.py:371
  396.9 6.1 %shard_map.252 = bf16[4,432,384]{2,1,0:T(8,128)(2,1)} custom-call(bf16[8,64,768]{2,1,0:T(8,128)(2,1)} %copy-done.10, bf16[8,64,768]{2,1,0:T(8,128)(2,1)} %copy-done.35, bf16[8,64,768]{2,1,0:T(8,128)(2,1)} %copy-done.5, bf16[8,64,768]{2,1,0:T(8,128)(2,1)} %copy-done.31, f32[8,768]{1,0:T(8,128)} %concatenate.80.vec, bf16[1024,256]{1,0:T(8,128)(2,1)} %get-tuple-element.211.act, ...), custom_call_target="tpu_custom_call" | custom-call | flops 6000000000 | bytes 21000000 | tf_op jit(solution)/shard_map/pallas_call | solution.py:68
  403.0 6.8 %all-to-all-done.12.got = bf16[8,64,768]{2,1,0:T(8,128)(2,1)S(1)} async-done(((bf16[8,64,768]{2,1,0:T(8,128)(2,1)}), bf16[8,64,768]{2,1,0:T(8,128)(2,1)S(1)}, u32[]{:S(2)}, u32[]{:S(2)}) %all-to-all-start.12) | async-done | bytes 786464 | tf_op jit(solution)/shard_map/all_to_all | solution.py:371
  411.0 3.7 all-to-all-start.13
  417.9 10.0 %collective-permute-done.28 = bf16[432,384]{1,0:T(8,128)(2,1)S(1)} collective-permute-done((bf16[432,384]{1,0:T(8,128)(2,1)S(1)}, bf16[432,384]{1,0:T(8,128)(2,1)S(1)}, u32[]{:S(2)}, u32[]{:S(2)}) %collective-permute-start.28) | collective-permute-done | bytes 331808 | tf_op jit(solution)/shard_map/ppermute | solution.py:37
  431.4 12.3 %shard_map.254 = (bf16[512,768]{1,0:T(8,128)(2,1)}, bf16[512,768]{1,0:T(8,128)(2,1)}, bf16[1024,192]{1,0:T(8,128)(2,1)}, bf16[1024,192]{1,0:T(8,128)(2,1)}, f32[8,768]{1,0:T(8,128)}) custom-call(s32[2]{0:T(128)} %pad_add_fusion.place, s32[32]{0:T(128)} %reshape.1282.order, bf16[8,64,768]{2,1,0:T(8,128)(2,1)} %copy-done.8, bf16[8,64,768]{2,1,0:T(8,128)(2,1)} %copy-done.34, ...), custom_call_target="tpu_custom_call" | custom-call | flops 12999999488 | bytes 45500000 | tf_op jit(solution)/shard_map/pallas_call | solution.py:68
  448.5 5.5 collective-permute-done.32
  456.2 6.6 %all-to-all-start.14 = ((bf16[8,64,768]{2,1,0:T(8,128)(2,1)}), bf16[8,64,768]{2,1,0:T(8,128)(2,1)S(1)}, u32[]{:S(2)}, u32[]{:S(2)}) async-start(bf16[8,64,768]{2,1,0:T(8,128)(2,1)} %bitcast.28), calls=%async_computation.14 | async-start | bytes 1572864 | tf_op jit(solution)/shard_map/all_to_all | solution.py:371
  465.2 6.1 %shard_map.255 = bf16[4,432,384]{2,1,0:T(8,128)(2,1)} custom-call(bf16[8,64,768]{2,1,0:T(8,128)(2,1)} %copy-done.8, bf16[8,64,768]{2,1,0:T(8,128)(2,1)} %copy-done.34, bf16[8,128,768]{2,1,0:T(8,128)(2,1)} %all-to-all-done.own.b_own.n_own, bf16[8,128,768]{2,1,0:T(8,128)(2,1)} %collective-permute-done.5.other.b_other.n_other, f32[8,768]{1,0:T(8,128)} %concatenate.76.vec, ...), custom_call_target="tpu_custom_call" | custom-call | flops 6000000000 | bytes 21000000 | tf_op jit(solution)/shard_map/pallas_call | solution.py:68
  471.3 7.5 %collective-permute-done.33 = bf16[432,384]{1,0:T(8,128)(2,1)S(1)} collective-permute-done((bf16[432,384]{1,0:T(8,128)(2,1)S(1)}, bf16[432,384]{1,0:T(8,128)(2,1)S(1)}, u32[]{:S(2)}, u32[]{:S(2)}) %collective-permute-start.33) | collective-permute-done | bytes 331808 | tf_op jit(solution)/shard_map/ppermute | solution.py:37
  480.7 7.6 %all-to-all-start.15 = ((bf16[8,432,384]{2,1,0:T(8,128)(2,1)}), bf16[8,432,384]{2,1,0:T(8,128)(2,1)}, u32[]{:S(2)}, u32[]{:S(2)}) async-start(bf16[8,432,384]{2,1,0:T(8,128)(2,1)} %broadcast_in_dim.30), calls=%async_computation.15 | async-start | bytes 5308416 | tf_op jit(solution)/shard_map/all_to_all | solution.py:371
  490.1 2.9 collective-permute-start.36
  493.0 12.6 %collective-permute-done.34 = bf16[432,384]{1,0:T(8,128)(2,1)S(1)} collective-permute-done((bf16[432,384]{1,0:T(8,128)(2,1)S(1)}, bf16[432,384]{1,0:T(8,128)(2,1)S(1)}, u32[]{:S(2)}, u32[]{:S(2)}) %collective-permute-start.34) | collective-permute-done | bytes 331808 | tf_op jit(solution)/shard_map/ppermute | solution.py:37
  508.7 14.3 %collective-permute-done.37 = bf16[432,384]{1,0:T(8,128)(2,1)S(1)} collective-permute-done((bf16[432,384]{1,0:T(8,128)(2,1)S(1)}, bf16[432,384]{1,0:T(8,128)(2,1)S(1)}, u32[]{:S(2)}, u32[]{:S(2)}) %collective-permute-start.37) | collective-permute-done | bytes 331808 | tf_op jit(solution)/shard_map/ppermute | solution.py:37
  525.1 7.7 %all-to-all-start.16 = ((bf16[8,432,384]{2,1,0:T(8,128)(2,1)}), bf16[8,432,384]{2,1,0:T(8,128)(2,1)}, u32[]{:S(2)}, u32[]{:S(2)}) async-start(bf16[8,432,384]{2,1,0:T(8,128)(2,1)} %broadcast_in_dim.31), calls=%async_computation.16 | async-start | bytes 5308416 | tf_op jit(solution)/shard_map/all_to_all | solution.py:371
  535.3 6.9 %shard_map.258 = (f32[2,192,2304]{2,1,0:T(8,128)}, f32[2,192,768]{2,1,0:T(8,128)}, f32[2,192,3072]{2,1,0:T(8,128)}, f32[2,768,768]{2,1,0:T(8,128)}, f32[2,16,16,384]{3,2,1,0:T(8,128)}) custom-call(s32[2]{0:T(128)} %pad_add_fusion.1.place, bf16[8,432,384]{2,1,0:T(8,128)(2,1)} %all-to-all-done.15.own, bf16[8,432,384]{2,1,0:T(8,128)(2,1)} %collective-permute-done.38.other), custom_call_target="tpu_custom_call" | custom-call | flops 7000000000 | bytes 24500000 | tf_op jit(solution)/shard_map/pallas_call | solution.py:338
  542.2 25.0 %collective-permute-done.39 = f32[64,768]{1,0:T(8,128)S(1)} collective-permute-done((f32[64,768]{1,0:T(8,128)S(1)}, f32[64,768]{1,0:T(8,128)S(1)}, u32[]{:S(2)}, u32[]{:S(2)}) %collective-permute-start.39) | collective-permute-done | bytes 196640 | tf_op jit(solution)/shard_map/ppermute | solution.py:37
  568.0 4.5 collective-permute-done.40.other
  572.5 7.1 %shard_map.259 = (f32[2,192,2304]{2,1,0:T(8,128)}, f32[2,192,768]{2,1,0:T(8,128)}, f32[2,192,3072]{2,1,0:T(8,128)}, f32[2,768,768]{2,1,0:T(8,128)}, f32[2,16,16,384]{3,2,1,0:T(8,128)}) custom-call(s32[2]{0:T(128)} %pad_add_fusion.1.place, ...), custom_call_target="tpu_custom_call", output_to_operand_aliasing={{0}: (3, {}), {1}: (4, {}), {2}: (5, {}), {3}: (6, {}), {4}... | custom-call | flops 7000000000 | bytes 24500000 | tf_op jit(solution)/shard_map/pallas_call | solution.py:338
  (309 shorter events, 120.1 us)
Async XLA Ops:
  1.8 7.9 %collective-permute-start = (bf16[64,768]{1,0:T(8,128)(2,1)S(1)}, bf16[64,768]{1,0:T(8,128)(2,1)S(1)}, u32[]{:S(2)}, u32[]{:S(2)}) collective-permute-start(bf16[64,768]{1,0:T(8,128)(2,1)S(1)} %select_bitcast_fusion.4), channel_id=1, source_target_pairs={{0,64},{64,0},{1,65},{65,1},{2,66},{66,2},{3,67},{67,3},{4,68},{68... | collective-permute-start | bytes 294920 | tf_op jit(solution)/shard_map/ppermute | solution.py:37
  9.2 9.7 %collective-permute-start.1 = (bf16[432,384]{1,0:T(8,128)(2,1)S(1)}, bf16[432,384]{1,0:T(8,128)(2,1)S(1)}, u32[]{:S(2)}, u32[]{:S(2)}) collective-permute-start(bf16[432,384]{1,0:T(8,128)(2,1)S(1)} %get-tuple-element.371), channel_id=1, source_target_pairs={{0,64},{64,0},{1,65},{65,1},{2,66},{66,2},{3,67},{67,3},{4,68},{68... | collective-permute-start | bytes 995336 | tf_op jit(solution)/shard_map/ppermute | solution.py:37
  11.1 29.8 %all-to-all-start = ((bf16[8,128,768]{2,1,0:T(8,128)(2,1)}), bf16[8,128,768]{2,1,0:T(8,128)(2,1)}, u32[]{:S(2)}, u32[]{:S(2)}) async-start(bf16[8,128,768]{2,1,0:T(8,128)(2,1)} %shard_map.237), calls=%async_computation | async-start | bytes 3145728 | tf_op jit(solution)/shard_map/all_to_all | solution.py:371
  19.8 17.7 %collective-permute-start.4 = (bf16[1,432,384]{2,1,0:T(8,128)(2,1)}, bf16[1,432,384]{2,1,0:T(8,128)(2,1)}, u32[]{:S(2)}, u32[]{:S(2)}) collective-permute-start(bf16[1,432,384]{2,1,0:T(8,128)(2,1)} %bitcast.7.s0), channel_id=1, source_target_pairs={{0,3},{1,0},{2,1},{3,2},{4,7},{5,4},{6,5},{7,6},{8,11},{9,8},{10,9... | collective-permute-start | bytes 995336 | tf_op jit(solution)/shard_map/ppermute | solution.py:37
  23.8 13.6 %collective-permute-start.3 = (bf16[1,432,384]{2,1,0:T(8,128)(2,1)}, bf16[1,432,384]{2,1,0:T(8,128)(2,1)}, u32[]{:S(2)}, u32[]{:S(2)}) collective-permute-start(bf16[1,432,384]{2,1,0:T(8,128)(2,1)} %bitcast.7.s0), channel_id=1, source_target_pairs={{0,2},{1,3},{2,0},{3,1},{4,6},{5,7},{6,4},{7,5},{8,10},{9,11},{10,... | collective-permute-start | bytes 995336 | tf_op jit(solution)/shard_map/ppermute | solution.py:37
  23.8 17.1 %collective-permute-start.2 = (bf16[1,432,384]{2,1,0:T(8,128)(2,1)}, bf16[1,432,384]{2,1,0:T(8,128)(2,1)}, u32[]{:S(2)}, u32[]{:S(2)}) collective-permute-start(bf16[1,432,384]{2,1,0:T(8,128)(2,1)} %bitcast.7.s0), channel_id=1, source_target_pairs={{0,1},{1,2},{2,3},{3,0},{4,5},{5,6},{6,7},{7,4},{8,9},{9,10},{10,1... | collective-permute-start | bytes 995336 | tf_op jit(solution)/shard_map/ppermute | solution.py:37
  25.4 17.6 %collective-permute-start.7 = (bf16[432,384]{1,0:T(8,128)(2,1)}, bf16[432,384]{1,0:T(8,128)(2,1)}, u32[]{:S(2)}, u32[]{:S(2)}) collective-permute-start(bf16[432,384]{1,0:T(8,128)(2,1)} %get-tuple-element.154), channel_id=1, source_target_pairs={{0,64},{64,0},{1,65},{65,1},{2,66},{66,2},{3,67},{67,3},{4,68},{68... | collective-permute-start | bytes 995336 | tf_op jit(solution)/shard_map/ppermute | solution.py:37
  40.9 11.2 %collective-permute-start.5 = (bf16[8,128,768]{2,1,0:T(8,128)(2,1)}, bf16[8,128,768]{2,1,0:T(8,128)(2,1)}, u32[]{:S(2)}, u32[]{:S(2)}) collective-permute-start(bf16[8,128,768]{2,1,0:T(8,128)(2,1)} %all-to-all-done.own.b_own.n_own), channel_id=1, source_target_pairs={{0,4},{4,0},{1,5},{5,1},{2,6},{6,2},{3,7},{7,3},{8,12},{12,8},{9,1... | collective-permute-start | bytes 4718600 | tf_op jit(solution)/shard_map/ppermute | solution.py:37
  44.3 64.2 %copy-start.4 = (bf16[3,432,384]{2,1,0:T(8,128)(2,1)}, bf16[3,432,384]{2,1,0:T(8,128)(2,1)S(1)}, u32[]{:S(2)}) copy-start(bf16[3,432,384]{2,1,0:T(8,128)(2,1)S(1)} %pad_maximum_fusion.s0) | copy-start | bytes 2985988
  44.3 23.9 %collective-permute-start.9 = (bf16[3,432,384]{2,1,0:T(8,128)(2,1)S(1)}, bf16[3,432,384]{2,1,0:T(8,128)(2,1)}, u32[]{:S(2)}, u32[]{:S(2)}) collective-permute-start(bf16[3,432,384]{2,1,0:T(8,128)(2,1)S(1)} %pad_maximum_fusion.s0), channel_id=1, source_target_pairs={{0,3},{1,0},{2,1},{3,2},{4,7},{5,4},{6,5},{7,6},{8,11},{9,8},{10,9... | collective-permute-start | bytes 2985992 | tf_op jit(solution)/shard_map/ppermute | solution.py:37
  48.4 23.3 %collective-permute-start.8 = (bf16[3,432,384]{2,1,0:T(8,128)(2,1)S(1)}, bf16[3,432,384]{2,1,0:T(8,128)(2,1)}, u32[]{:S(2)}, u32[]{:S(2)}) collective-permute-start(bf16[3,432,384]{2,1,0:T(8,128)(2,1)S(1)} %pad_maximum_fusion.s0), channel_id=1, source_target_pairs={{0,1},{1,2},{2,3},{3,0},{4,5},{5,6},{6,7},{7,4},{8,9},{9,10},{10,1... | collective-permute-start | bytes 2985992 | tf_op jit(solution)/shard_map/ppermute | solution.py:37
  61.9 2.5 collective-permute-start.6
  71.7 18.3 %all-to-all-start.1 = ((bf16[8,64,768]{2,1,0:T(8,128)(2,1)}), bf16[8,64,768]{2,1,0:T(8,128)(2,1)S(1)}, u32[]{:S(2)}, u32[]{:S(2)}) async-start(bf16[8,64,768]{2,1,0:T(8,128)(2,1)} %bitcast.8), calls=%async_computation.1 | async-start | bytes 1572864 | tf_op jit(solution)/shard_map/all_to_all | solution.py:371
  79.2 22.1 %collective-permute-start.10 = (bf16[3,432,384]{2,1,0:T(8,128)(2,1)S(1)}, bf16[3,432,384]{2,1,0:T(8,128)(2,1)}, u32[]{:S(2)}, u32[]{:S(2)}) collective-permute-start(bf16[3,432,384]{2,1,0:T(8,128)(2,1)S(1)} %pad_maximum_fusion.s0), channel_id=1, source_target_pairs={{0,2},{1,3},{2,0},{3,1},{4,6},{5,7},{6,4},{7,5},{8,10},{9,11},{10,... | collective-permute-start | bytes 2985992 | tf_op jit(solution)/shard_map/ppermute | solution.py:37
  91.2 14.3 %all-to-all-start.2 = ((bf16[8,64,768]{2,1,0:T(8,128)(2,1)}), bf16[8,64,768]{2,1,0:T(8,128)(2,1)S(1)}, u32[]{:S(2)}, u32[]{:S(2)}) async-start(bf16[8,64,768]{2,1,0:T(8,128)(2,1)} %get-tuple-element.157), calls=%async_computation.2 | async-start | bytes 1572864 | tf_op jit(solution)/shard_map/all_to_all | solution.py:371
  109.4 107.5 %copy-start.12 = (bf16[1,1,16,384]{3,1,2,0:T(2,128)(2,1)}, bf16[1,1,16,384]{3,1,2,0:T(2,128)(2,1)S(1)}, u32[]{:S(2)}) copy-start(bf16[1,1,16,384]{3,1,2,0:T(2,128)(2,1)S(1)} %copy.78) | copy-start | bytes 36868
  110.0 2.3 collective-permute-start.11
  122.7 2.5 collective-permute-start.12
  127.4 17.2 %all-to-all-start.3 = ((bf16[8,64,768]{2,1,0:T(8,128)(2,1)}), bf16[8,64,768]{2,1,0:T(8,128)(2,1)S(1)}, u32[]{:S(2)}, u32[]{:S(2)}) async-start(bf16[8,64,768]{2,1,0:T(8,128)(2,1)} %bitcast.13), calls=%async_computation.3 | async-start | bytes 1572864 | tf_op jit(solution)/shard_map/all_to_all | solution.py:371
  163.3 2.3 collective-permute-start.13
  176.4 2.5 collective-permute-start.14
  181.1 17.2 %all-to-all-start.5 = ((bf16[8,64,768]{2,1,0:T(8,128)(2,1)}), bf16[8,64,768]{2,1,0:T(8,128)(2,1)S(1)}, u32[]{:S(2)}, u32[]{:S(2)}) async-start(bf16[8,64,768]{2,1,0:T(8,128)(2,1)} %bitcast.14), calls=%async_computation.5 | async-start | bytes 1572864 | tf_op jit(solution)/shard_map/all_to_all | solution.py:371
  216.9 2.3 collective-permute-start.15
  229.6 2.5 collective-permute-start.16
  234.3 17.2 %all-to-all-start.7 = ((bf16[8,64,768]{2,1,0:T(8,128)(2,1)}), bf16[8,64,768]{2,1,0:T(8,128)(2,1)S(1)}, u32[]{:S(2)}, u32[]{:S(2)}) async-start(bf16[8,64,768]{2,1,0:T(8,128)(2,1)} %bitcast.15), calls=%async_computation.7 | async-start | bytes 1572864 | tf_op jit(solution)/shard_map/all_to_all | solution.py:371
  251.5 2.5 collective-permute-start.17
  256.2 19.6 %all-to-all-start.8 = ((bf16[8,64,768]{2,1,0:T(8,128)(2,1)}), bf16[8,64,768]{2,1,0:T(8,128)(2,1)S(1)}, u32[]{:S(2)}, u32[]{:S(2)}) async-start(bf16[8,64,768]{2,1,0:T(8,128)(2,1)} %bitcast.177), calls=%async_computation.8 | async-start | bytes 1572864 | tf_op jit(solution)/shard_map/all_to_all | solution.py:371
  277.1 17.3 %all-to-all-start.9 = ((bf16[8,64,768]{2,1,0:T(8,128)(2,1)}), bf16[8,64,768]{2,1,0:T(8,128)(2,1)S(1)}, u32[]{:S(2)}, u32[]{:S(2)}) async-start(bf16[8,64,768]{2,1,0:T(8,128)(2,1)} %get-tuple-element.187), calls=%async_computation.9 | async-start | bytes 1572864 | tf_op jit(solution)/shard_map/all_to_all | solution.py:371
  283.1 10.9 %collective-permute-start.18 = (bf16[432,384]{1,0:T(8,128)(2,1)S(1)}, bf16[432,384]{1,0:T(8,128)(2,1)S(1)}, u32[]{:S(2)}, u32[]{:S(2)}) collective-permute-start(bf16[432,384]{1,0:T(8,128)(2,1)S(1)} %get-tuple-element.362), channel_id=1, source_target_pairs={{0,2},{1,3},{2,0},{3,1},{4,6},{5,7},{6,4},{7,5},{8,10},{9,11},{10,... | collective-permute-start | bytes 995336 | tf_op jit(solution)/shard_map/ppermute | solution.py:37
  294.4 2.3 collective-permute-start.19
  297.6 16.1 %copy-start.25 = (bf16[432,384]{1,0:T(8,128)(2,1)S(1)}, bf16[432,384]{1,0:T(8,128)(2,1)}, u32[]{:S(2)}) copy-start(bf16[432,384]{1,0:T(8,128)(2,1)} %get-tuple-element.360) | copy-start | bytes 995332
  309.9 3.7 collective-permute-start.20
  310.1 11.1 %collective-permute-start.22 = (bf16[432,384]{1,0:T(8,128)(2,1)S(1)}, bf16[432,384]{1,0:T(8,128)(2,1)S(1)}, u32[]{:S(2)}, u32[]{:S(2)}) collective-permute-start(bf16[432,384]{1,0:T(8,128)(2,1)S(1)} %copy-done.26), channel_id=1, source_target_pairs={{0,3},{1,0},{2,1},{3,2},{4,7},{5,4},{6,5},{7,6},{8,11},{9,8},{10,9... | collective-permute-start | bytes 995336 | tf_op jit(solution)/shard_map/ppermute | solution.py:37
  313.6 11.1 %collective-permute-start.21 = (bf16[432,384]{1,0:T(8,128)(2,1)S(1)}, bf16[432,384]{1,0:T(8,128)(2,1)}, u32[]{:S(2)}, u32[]{:S(2)}) collective-permute-start(bf16[432,384]{1,0:T(8,128)(2,1)S(1)} %copy-done.25), channel_id=1, source_target_pairs={{0,1},{1,2},{2,3},{3,0},{4,5},{5,6},{6,7},{7,4},{8,9},{9,10},{10,1... | collective-permute-start | bytes 995336 | tf_op jit(solution)/shard_map/ppermute | solution.py:37
  321.2 16.2 %copy-start.17 = (bf16[432,384]{1,0:T(8,128)(2,1)}, bf16[432,384]{1,0:T(8,128)(2,1)S(1)}, u32[]{:S(2)}) copy-start(bf16[432,384]{1,0:T(8,128)(2,1)S(1)} %collective-permute-done.22) | copy-start | bytes 995332
  324.7 19.5 %all-to-all-start.10 = ((bf16[8,64,768]{2,1,0:T(8,128)(2,1)}), bf16[8,64,768]{2,1,0:T(8,128)(2,1)S(1)}, u32[]{:S(2)}, u32[]{:S(2)}) async-start(bf16[8,64,768]{2,1,0:T(8,128)(2,1)} %bitcast.175), calls=%async_computation.10 | async-start | bytes 1572864 | tf_op jit(solution)/shard_map/all_to_all | solution.py:371
  345.5 17.2 %all-to-all-start.11 = ((bf16[8,64,768]{2,1,0:T(8,128)(2,1)}), bf16[8,64,768]{2,1,0:T(8,128)(2,1)S(1)}, u32[]{:S(2)}, u32[]{:S(2)}) async-start(bf16[8,64,768]{2,1,0:T(8,128)(2,1)} %get-tuple-element.202), calls=%async_computation.11 | async-start | bytes 1572864 | tf_op jit(solution)/shard_map/all_to_all | solution.py:371
  351.4 10.9 %collective-permute-start.23 = (bf16[432,384]{1,0:T(8,128)(2,1)S(1)}, bf16[432,384]{1,0:T(8,128)(2,1)S(1)}, u32[]{:S(2)}, u32[]{:S(2)}) collective-permute-start(bf16[432,384]{1,0:T(8,128)(2,1)S(1)} %get-tuple-element.358), channel_id=1, source_target_pairs={{0,2},{1,3},{2,0},{3,1},{4,6},{5,7},{6,4},{7,5},{8,10},{9,11},{10,... | collective-permute-start | bytes 995336 | tf_op jit(solution)/shard_map/ppermute | solution.py:37
  362.3 16.1 %copy-start.15 = (bf16[432,384]{1,0:T(8,128)(2,1)}, bf16[432,384]{1,0:T(8,128)(2,1)S(1)}, u32[]{:S(2)}) copy-start(bf16[432,384]{1,0:T(8,128)(2,1)S(1)} %collective-permute-done.23) | copy-start | bytes 995332
  362.7 2.3 collective-permute-start.24
  378.5 2.6 collective-permute-start.25
  378.7 10.1 %collective-permute-start.27 = (bf16[432,384]{1,0:T(8,128)(2,1)S(1)}, bf16[432,384]{1,0:T(8,128)(2,1)S(1)}, u32[]{:S(2)}, u32[]{:S(2)}) collective-permute-start(bf16[432,384]{1,0:T(8,128)(2,1)S(1)} %copy-done.24), channel_id=1, source_target_pairs={{0,3},{1,0},{2,1},{3,2},{4,7},{5,4},{6,5},{7,6},{8,11},{9,8},{10,9... | collective-permute-start | bytes 995336 | tf_op jit(solution)/shard_map/ppermute | solution.py:37
  379.2 11.1 %collective-permute-start.26 = (bf16[432,384]{1,0:T(8,128)(2,1)S(1)}, bf16[432,384]{1,0:T(8,128)(2,1)}, u32[]{:S(2)}, u32[]{:S(2)}) collective-permute-start(bf16[432,384]{1,0:T(8,128)(2,1)S(1)} %copy-done.23), channel_id=1, source_target_pairs={{0,1},{1,2},{2,3},{3,0},{4,5},{5,6},{6,7},{7,4},{8,9},{9,10},{10,1... | collective-permute-start | bytes 995336 | tf_op jit(solution)/shard_map/ppermute | solution.py:37
  390.3 19.5 %all-to-all-start.12 = ((bf16[8,64,768]{2,1,0:T(8,128)(2,1)}), bf16[8,64,768]{2,1,0:T(8,128)(2,1)S(1)}, u32[]{:S(2)}, u32[]{:S(2)}) async-start(bf16[8,64,768]{2,1,0:T(8,128)(2,1)} %bitcast.176), calls=%async_computation.12 | async-start | bytes 1572864 | tf_op jit(solution)/shard_map/all_to_all | solution.py:371
  411.0 17.2 %all-to-all-start.13 = ((bf16[8,64,768]{2,1,0:T(8,128)(2,1)}), bf16[8,64,768]{2,1,0:T(8,128)(2,1)S(1)}, u32[]{:S(2)}, u32[]{:S(2)}) async-start(bf16[8,64,768]{2,1,0:T(8,128)(2,1)} %get-tuple-element.217), calls=%async_computation.13 | async-start | bytes 1572864 | tf_op jit(solution)/shard_map/all_to_all | solution.py:371
  416.9 10.9 %collective-permute-start.28 = (bf16[432,384]{1,0:T(8,128)(2,1)S(1)}, bf16[432,384]{1,0:T(8,128)(2,1)S(1)}, u32[]{:S(2)}, u32[]{:S(2)}) collective-permute-start(bf16[432,384]{1,0:T(8,128)(2,1)S(1)} %get-tuple-element.354), channel_id=1, source_target_pairs={{0,2},{1,3},{2,0},{3,1},{4,6},{5,7},{6,4},{7,5},{8,10},{9,11},{10,... | collective-permute-start | bytes 995336 | tf_op jit(solution)/shard_map/ppermute | solution.py:37
  428.3 2.3 collective-permute-start.29
  443.8 2.6 collective-permute-start.30
  444.0 10.1 %collective-permute-start.32 = (bf16[432,384]{1,0:T(8,128)(2,1)S(1)}, bf16[432,384]{1,0:T(8,128)(2,1)S(1)}, u32[]{:S(2)}, u32[]{:S(2)}) collective-permute-start(bf16[432,384]{1,0:T(8,128)(2,1)S(1)} %copy-done.22), channel_id=1, source_target_pairs={{0,3},{1,0},{2,1},{3,2},{4,7},{5,4},{6,5},{7,6},{8,11},{9,8},{10,9... | collective-permute-start | bytes 995336 | tf_op jit(solution)/shard_map/ppermute | solution.py:37
  444.5 11.0 %collective-permute-start.31 = (bf16[432,384]{1,0:T(8,128)(2,1)S(1)}, bf16[432,384]{1,0:T(8,128)(2,1)S(1)}, u32[]{:S(2)}, u32[]{:S(2)}) collective-permute-start(bf16[432,384]{1,0:T(8,128)(2,1)S(1)} %copy-done.21), channel_id=1, source_target_pairs={{0,1},{1,2},{2,3},{3,0},{4,5},{5,6},{6,7},{7,4},{8,9},{9,10},{10,1... | collective-permute-start | bytes 995336 | tf_op jit(solution)/shard_map/ppermute | solution.py:37
  456.2 22.7 %all-to-all-start.14 = ((bf16[8,64,768]{2,1,0:T(8,128)(2,1)}), bf16[8,64,768]{2,1,0:T(8,128)(2,1)S(1)}, u32[]{:S(2)}, u32[]{:S(2)}) async-start(bf16[8,64,768]{2,1,0:T(8,128)(2,1)} %bitcast.28), calls=%async_computation.14 | async-start | bytes 1572864 | tf_op jit(solution)/shard_map/all_to_all | solution.py:371
  464.7 14.1 %collective-permute-start.33 = (bf16[432,384]{1,0:T(8,128)(2,1)S(1)}, bf16[432,384]{1,0:T(8,128)(2,1)S(1)}, u32[]{:S(2)}, u32[]{:S(2)}) collective-permute-start(bf16[432,384]{1,0:T(8,128)(2,1)S(1)} %get-tuple-element.324), channel_id=1, source_target_pairs={{0,64},{64,0},{1,65},{65,1},{2,66},{66,2},{3,67},{67,3},{4,68},{68... | collective-permute-start | bytes 995336 | tf_op jit(solution)/shard_map/ppermute | solution.py:37
  480.7 42.5 %all-to-all-start.15 = ((bf16[8,432,384]{2,1,0:T(8,128)(2,1)}), bf16[8,432,384]{2,1,0:T(8,128)(2,1)}, u32[]{:S(2)}, u32[]{:S(2)}) async-start(bf16[8,432,384]{2,1,0:T(8,128)(2,1)} %broadcast_in_dim.30), calls=%async_computation.15 | async-start | bytes 5308416 | tf_op jit(solution)/shard_map/all_to_all | solution.py:371
  488.3 17.3 %copy-start.2 = (bf16[432,384]{1,0:T(8,128)(2,1)S(1)}, bf16[432,384]{1,0:T(8,128)(2,1)}, u32[]{:S(2)}) copy-start(bf16[432,384]{1,0:T(8,128)(2,1)} %get-tuple-element.241) | copy-start | bytes 995332
  488.3 17.3 %copy-start.16 = (bf16[432,384]{1,0:T(8,128)(2,1)S(1)}, bf16[432,384]{1,0:T(8,128)(2,1)}, u32[]{:S(2)}) copy-start(bf16[432,384]{1,0:T(8,128)(2,1)} %copy-done.15) | copy-start | bytes 995332
  488.3 17.3 %copy-start.19 = (bf16[432,384]{1,0:T(8,128)(2,1)S(1)}, bf16[432,384]{1,0:T(8,128)(2,1)}, u32[]{:S(2)}) copy-start(bf16[432,384]{1,0:T(8,128)(2,1)} %copy-done.18) | copy-start | bytes 995332
  489.7 15.9 %collective-permute-start.34 = (bf16[432,384]{1,0:T(8,128)(2,1)S(1)}, bf16[432,384]{1,0:T(8,128)(2,1)S(1)}, u32[]{:S(2)}, u32[]{:S(2)}) collective-permute-start(bf16[432,384]{1,0:T(8,128)(2,1)S(1)} %get-tuple-element.348), channel_id=1, source_target_pairs={{0,1},{1,2},{2,3},{3,0},{4,5},{5,6},{6,7},{7,4},{8,9},{9,10},{10,1... | collective-permute-start | bytes 995336 | tf_op jit(solution)/shard_map/ppermute | solution.py:37
  490.1 15.5 %collective-permute-start.36 = (bf16[432,384]{1,0:T(8,128)(2,1)S(1)}, bf16[432,384]{1,0:T(8,128)(2,1)S(1)}, u32[]{:S(2)}, u32[]{:S(2)}) collective-permute-start(bf16[432,384]{1,0:T(8,128)(2,1)S(1)} %get-tuple-element.349), channel_id=1, source_target_pairs={{0,3},{1,0},{2,1},{3,2},{4,7},{5,4},{6,5},{7,6},{8,11},{9,8},{10,9... | collective-permute-start | bytes 995336 | tf_op jit(solution)/shard_map/ppermute | solution.py:37
  493.0 12.6 %collective-permute-start.35 = (bf16[432,384]{1,0:T(8,128)(2,1)S(1)}, bf16[432,384]{1,0:T(8,128)(2,1)S(1)}, u32[]{:S(2)}, u32[]{:S(2)}) collective-permute-start(bf16[432,384]{1,0:T(8,128)(2,1)S(1)} %get-tuple-element.350), channel_id=1, source_target_pairs={{0,2},{1,3},{2,0},{3,1},{4,6},{5,7},{6,4},{7,5},{8,10},{9,11},{10,... | collective-permute-start | bytes 995336 | tf_op jit(solution)/shard_map/ppermute | solution.py:37
  507.1 16.0 %collective-permute-start.37 = (bf16[432,384]{1,0:T(8,128)(2,1)S(1)}, bf16[432,384]{1,0:T(8,128)(2,1)S(1)}, u32[]{:S(2)}, u32[]{:S(2)}) collective-permute-start(bf16[432,384]{1,0:T(8,128)(2,1)S(1)} %get-tuple-element.321), channel_id=1, source_target_pairs={{0,64},{64,0},{1,65},{65,1},{2,66},{66,2},{3,67},{67,3},{4,68},{68... | collective-permute-start | bytes 995336 | tf_op jit(solution)/shard_map/ppermute | solution.py:37
  523.2 12.1 %collective-permute-start.38 = (bf16[8,432,384]{2,1,0:T(8,128)(2,1)}, bf16[8,432,384]{2,1,0:T(8,128)(2,1)}, u32[]{:S(2)}, u32[]{:S(2)}) collective-permute-start(bf16[8,432,384]{2,1,0:T(8,128)(2,1)} %all-to-all-done.15.own), channel_id=1, source_target_pairs={{0,4},{4,0},{1,5},{5,1},{2,6},{6,2},{3,7},{7,3},{8,12},{12,8},{9,1... | collective-permute-start | bytes 7962632 | tf_op jit(solution)/shard_map/ppermute | solution.py:37
  525.1 42.1 %all-to-all-start.16 = ((bf16[8,432,384]{2,1,0:T(8,128)(2,1)}), bf16[8,432,384]{2,1,0:T(8,128)(2,1)}, u32[]{:S(2)}, u32[]{:S(2)}) async-start(bf16[8,432,384]{2,1,0:T(8,128)(2,1)} %broadcast_in_dim.31), calls=%async_computation.16 | async-start | bytes 5308416 | tf_op jit(solution)/shard_map/all_to_all | solution.py:371
  534.7 32.5 %collective-permute-start.39 = (f32[64,768]{1,0:T(8,128)S(1)}, f32[64,768]{1,0:T(8,128)S(1)}, u32[]{:S(2)}, u32[]{:S(2)}) collective-permute-start(f32[64,768]{1,0:T(8,128)S(1)} %broadcast_select_fusion.5), channel_id=1, source_target_pairs={{0,64},{64,0},{1,65},{65,1},{2,66},{66,2},{3,67},{67,3},{4,68},{68... | collective-permute-start | bytes 589832 | tf_op jit(solution)/shard_map/ppermute | solution.py:37
  567.2 5.3 collective-permute-start.40
  (29 other events, 196.6 us)
